TPU v7x, 128 devices: a whole 4x4x4 slice. The times are simulated.
128 devices in a mesh: lat: 4 (over x_hi, core), lon: 32 (over x_lo, y, z).
Axes of the slice: x: 4 (x_hi: 2, x_lo: 2; x = x_hi * 2 + x_lo), y: 4, z: 4, core: 2. Of those that a mesh axis runs over, the one named last changes fastest.
Arguments:
- grid: bfloat16 [2, 20, 768, 1536], P(None, None, 'lat', 'lon'), may hold values from -6 to 6
- patch_weight: bfloat16 [5120, 768], replicated, may hold values from -0.078125 to 0.078125
- norm_gain_one: float32 [768], replicated, may hold values from 0.1 to 1.9
- spectral_one: float32 [2, 8, 96, 96], replicated, may hold values from -0.4375 to 0.4375
- spectral_bias: float32 [2, 768], replicated, may hold values from -1.5 to 1.5
- spectral_two: float32 [2, 8, 96, 96], replicated, may hold values from -0.4375 to 0.4375
- norm_gain_two: float32 [768], replicated, may hold values from 0.1 to 1.9
- fc_up: bfloat16 [768, 3072], replicated, may hold values from -0.21875 to 0.21875
- fc_down: bfloat16 [3072, 768], replicated, may hold values from -0.109375 to 0.109375
Outputs:
- block_out: bfloat16 [2, 96, 192, 768], P(None, 'lat', 'lon')
All inputs are finite; a program needn't handle non-finite values.
Results may differ from a plain program's by a relative error of at most 0.014.
Values may be sent and summed in bfloat16 or wider, within the bound.
A program may use at most 128 MiB of HBM per device.

v0:
```python
import math

import jax
import jax.numpy as jnp
from jax import lax
from jax.sharding import PartitionSpec as P

PATCH = 8
KMD = 2


def extended(block, sides, width):
    for axis, dim in sides:
        count = lax.axis_size(axis)
        forward = [(i, i + 1) for i in range(count - 1)]
        forward.append((count - 1, 0))
        backward = [(target, source) for source, target in forward]
        low = lax.ppermute(
            lax.slice_in_dim(block, block.shape[dim] - width, None, axis=dim), axis, forward
        )
        high = lax.ppermute(lax.slice_in_dim(block, 0, width, axis=dim), axis, backward)
        block = jnp.concatenate([low, block, high], axis=dim)
    return block


def embed(padded, weight, rows, cols):
    samples, depth, tall, broad = padded.shape
    half = PATCH // 2
    width = weight.shape[1]
    blocked = padded.reshape(samples, depth, rows + 1, 2, half, cols + 1, 2, half)
    table = weight.reshape(4, 4, depth, half, half, width)
    total = jnp.zeros((samples, rows, cols, width), jnp.float32)
    for row_par in range(2):
        for col_par in range(2):
            view = blocked[:, :, :, row_par, :, :, col_par, :]
            chosen = jnp.stack(
                [
                    table[2 * row_pair + row_par, 2 * col_pair + col_par]
                    for row_pair in range(2)
                    for col_pair in range(2)
                ],
                axis=-2,
            )
            product = jnp.einsum(
                "svirjq,vrqkc->sijkc", view, chosen, preferred_element_type=jnp.float32
            )
            for row_pair in range(2):
                for col_pair in range(2):
                    total = (
                        total
                        + product[
                            :,
                            row_pair : row_pair + rows,
                            col_pair : col_pair + cols,
                            2 * row_pair + col_pair,
                        ]
                    )
    return total.astype(jnp.bfloat16)


def layer_norm(values, gain):
    flat = values.astype(jnp.float32)
    centre = jnp.mean(flat, axis=-1, keepdims=True)
    spread = jnp.mean(jnp.square(flat - centre), axis=-1, keepdims=True)
    return ((flat - centre) * lax.rsqrt(spread + 1e-05) * gain).astype(jnp.bfloat16)


def token_mlp(middle, gain, fc_up, fc_down):
    normed = layer_norm(middle, gain)
    shape = normed.shape
    flat = normed.reshape(-1, shape[-1])
    hidden = jax.nn.gelu(
        jnp.dot(flat, fc_up, preferred_element_type=jnp.float32), approximate=False
    ).astype(jnp.bfloat16)
    update = jnp.dot(hidden, fc_down, preferred_element_type=jnp.float32).reshape(shape)
    return (middle.astype(jnp.float32) + update).astype(jnp.bfloat16)


def twiddle(length, first, second):
    product = first[:, None] * second[None, :] % length
    angle = product.astype(jnp.float32) * (2.0 * math.pi / length)
    return (jnp.cos(angle), jnp.sin(angle))


def high_dot(left, right):
    return jnp.dot(left, right, precision=lax.Precision.HIGHEST)


def dense_block(weights):
    blocks, width, _ = weights.shape
    unit = jnp.eye(blocks, dtype=jnp.float32)
    spread_out = jnp.einsum("bio,bd->bido", weights, unit, precision=lax.Precision.HIGHEST)
    return spread_out.reshape(blocks * width, blocks * width)


def filter_modes(spectrum, first_w, bias, second_w):
    shape = spectrum.shape
    depth = shape[-1]
    real_in = spectrum[:, 0].reshape(-1, depth)
    imag_in = spectrum[:, 1].reshape(-1, depth)
    first_re = dense_block(first_w[0])
    first_im = dense_block(first_w[1])
    second_re = dense_block(second_w[0])
    second_im = dense_block(second_w[1])
    mid_re = jax.nn.relu(high_dot(real_in, first_re) - high_dot(imag_in, first_im) + bias[0])
    mid_im = jax.nn.relu(high_dot(real_in, first_im) + high_dot(imag_in, first_re) + bias[1])
    out_re = high_dot(mid_re, second_re) - high_dot(mid_im, second_im)
    out_im = high_dot(mid_re, second_im) + high_dot(mid_im, second_re)
    out_re = out_re - jnp.clip(out_re, -0.01, 0.01)
    out_im = out_im - jnp.clip(out_im, -0.01, 0.01)
    inner = (shape[0],) + shape[2:]
    return jnp.stack([out_re.reshape(inner), out_im.reshape(inner)], axis=1)


def lon_turn(values, width, modes):
    flat = values.astype(jnp.float32).reshape(width, -1)
    cos_lon, sin_lon = twiddle(
        width, jnp.arange(modes, dtype=jnp.int32), jnp.arange(width, dtype=jnp.int32)
    )
    scale = 1.0 / math.sqrt(width)
    return (high_dot(cos_lon, flat) * scale, -high_dot(sin_lon, flat) * scale)


def lon_back(values, width):
    modes = values.shape[1]
    cos_lon, sin_lon = twiddle(
        width, jnp.arange(width, dtype=jnp.int32), jnp.arange(modes, dtype=jnp.int32)
    )
    weights = jnp.where(jnp.arange(modes) == 0, 1.0, 2.0).astype(jnp.float32) / math.sqrt(width)
    return high_dot(cos_lon * weights[None, :], values[0]) - high_dot(
        sin_lon * weights[None, :], values[1]
    )


def local(
    grid,
    patch_weight,
    norm_gain_one,
    spectral_one,
    spectral_bias,
    spectral_two,
    norm_gain_two,
    fc_up,
    fc_down,
):
    samples = grid.shape[0]
    rows = grid.shape[2] // PATCH
    cols = grid.shape[3] // PATCH
    half = PATCH // 2
    lat_count = lax.axis_size("lat")
    lon_count = lax.axis_size("lon")
    lat_pos = lax.axis_index("lat")
    tall = rows * lat_count
    broad = cols * lon_count
    modes = KMD * lon_count
    padded = extended(grid, (("lat", 2), ("lon", 3)), half)
    row_ids = jnp.arange(grid.shape[2] + 2 * half)
    outside = (lat_pos == 0) & (row_ids < half) | (lat_pos == lat_count - 1) & (
        row_ids >= grid.shape[2] + half
    )
    padded = jnp.where(outside[None, None, :, None], jnp.zeros((), padded.dtype), padded)
    tokens = embed(padded, patch_weight, rows, cols)
    normed_one = layer_norm(tokens, norm_gain_one)
    depth = normed_one.shape[3]
    root_tall = 1.0 / math.sqrt(tall)
    band_rows = lat_pos * rows + jnp.arange(rows, dtype=jnp.int32)
    share = depth // lon_count
    arranged = normed_one.reshape(samples, rows, cols, lon_count, share).transpose(3, 2, 0, 1, 4)
    arranged = arranged.reshape(lon_count, 1, cols, samples, rows, share)
    piece = lax.all_to_all(arranged, "lon", split_axis=0, concat_axis=1, tiled=True)
    items = piece.shape[3]
    part_re, part_im = lon_turn(piece, broad, modes)
    col_re = part_re.reshape(modes, items, rows, share)
    col_im = part_im.reshape(modes, items, rows, share)
    band_re = col_re.transpose(2, 0, 1, 3).reshape(rows, -1)
    band_im = col_im.transpose(2, 0, 1, 3).reshape(rows, -1)
    wanted = jnp.arange(lax.axis_size("lat") * rows, dtype=jnp.int32)
    cos_lat, sin_lat = twiddle(tall, wanted, band_rows)
    term_re = high_dot(cos_lat, band_re) + high_dot(sin_lat, band_im)
    term_im = high_dot(cos_lat, band_im) - high_dot(sin_lat, band_re)
    partial_modes = lax.psum_scatter(
        (jnp.stack([term_re, term_im], axis=1) * root_tall).astype(jnp.bfloat16),
        "lat",
        scatter_dimension=0,
        tiled=True,
    ).astype(jnp.float32)
    partial_modes = partial_modes.reshape(rows, 2, lon_count, KMD, samples, 1, share)
    spectrum = lax.all_to_all(
        partial_modes.astype(jnp.bfloat16), "lon", split_axis=2, concat_axis=5, tiled=True
    ).astype(partial_modes.dtype)
    spectrum = spectrum.reshape(rows, 2, KMD, samples, depth)
    filtered = filter_modes(spectrum, spectral_one, spectral_bias, spectral_two)
    outgoing = filtered.reshape(rows, 2, 1, KMD, samples, lon_count, share)
    spectra = lax.all_to_all(
        outgoing.astype(jnp.bfloat16), "lon", split_axis=5, concat_axis=2, tiled=True
    ).astype(outgoing.dtype)
    spectra = spectra.reshape(rows, 2, -1)
    spec_re = spectra[:, 0]
    spec_im = spectra[:, 1]
    wanted = jnp.arange(lax.axis_size("lat") * rows, dtype=jnp.int32)
    cos_lat, sin_lat = twiddle(tall, wanted, band_rows)
    term_re = high_dot(cos_lat, spec_re) - high_dot(sin_lat, spec_im)
    term_im = high_dot(cos_lat, spec_im) + high_dot(sin_lat, spec_re)
    band_modes = lax.psum_scatter(
        (jnp.stack([term_re, term_im], axis=1) * root_tall).astype(jnp.bfloat16),
        "lat",
        scatter_dimension=0,
        tiled=True,
    ).astype(jnp.float32)
    both = band_modes.reshape(rows, 2, modes, -1).transpose(1, 2, 0, 3).reshape(2, modes, -1)
    surface = lon_back(both, broad).reshape(lon_count, cols, rows, samples, 1, share)
    field = lax.all_to_all(
        surface.astype(jnp.bfloat16), "lon", split_axis=0, concat_axis=4, tiled=True
    ).astype(surface.dtype)
    field = field.reshape(cols, rows, samples, depth)
    field = field.transpose(2, 1, 0, 3)
    middle = (field + normed_one.astype(jnp.float32) + tokens.astype(jnp.float32)).astype(
        jnp.bfloat16
    )
    return token_mlp(middle, norm_gain_two, fc_up, fc_down)


def solution(mesh):
    in_specs = (P(None, None, "lat", "lon"), P(), P(), P(), P(), P(), P(), P(), P())
    out_specs = P(None, "lat", "lon", None)
    return jax.shard_map(local, mesh=mesh, in_specs=in_specs, out_specs=out_specs, check_vma=False)
```

profile of v0, /device:TPU:0, one launch (start us, length us, event | category | flops | bytes accessed | tf_op | source)
XLA Modules:
  0.0 398.9 jit_solution(7435859717744228174)
XLA Ops:
  6.5 2.3 fusion.240
  8.8 3.2 collective-permute-start.1
  12.1 14.0 %reshape.213 = bf16[4,4,20,4,4,768]{5,4,3,2,1,0:T(4,128)(2,1)} reshape(bf16[5120,768]{1,0:T(8,128)(2,1)} %param.10) | data formatting | bytes 15728640 | tf_op jit(solution)/shard_map/reshape | solution.py:31
  26.1 6.6 %fusion.239 = (bf16[1,1,20,4,4,768]{5,4,3,2,1,0:T(4,128)(2,1)S(1)}, bf16[1,1,20,4,4,768]{5,4,3,2,1,0:T(4,128)(2,1)S(1)}, bf16[1,1,20,4,4,768]{5,4,3,2,1,0:T(4,12...) fusion(bf16[4,4,20,4,4,768]{5,4,3,2,1,0:T(4,128)(2,1)} %reshape.213), kind=kLoop, calls=%fused_computation.317 | loop fusion | bytes 15728640 | tf_op jit(solution)/shard_map/slice | solution.py:38
  45.8 5.6 %collective-permute-start.3 = (bf16[2,20,200,4]{2,3,1,0:T(4,128)(2,1)S(1)}, bf16[2,20,200,4]{2,3,1,0:T(4,128)(2,1)S(1)}, u32[]{:S(2)}, u32[]{:S(2)}) collective-permute-start(bf16[2,20,200,4]{2,3,1,0:T(4,128)(2,1)S(1)} %get-tuple-element.28), channel_id=1, source_target_pairs={{1,0},{2,1},{3,2},{4,3},{5,4},{6,5},{7,6},{8,7},{9,8},{10,9},{11,1... | collective-permute-start | bytes 192008 | tf_op jit(solution)/shard_map/ppermute | solution.py:21
  55.2 6.3 %copy.120 = bf16[2,20,200,56]{1,3,2,0:T(8,128)(2,1)} copy(bf16[2,20,200,56]{2,3,1,0:T(8,128)(2,1)S(1)} %pad_maximum_fusion.1) | data formatting | bytes 1792000 | tf_op jit(solution)/shard_map/concatenate | solution.py:22
  61.5 3.7 copy_select_fusion
  65.3 8.9 %fusion.50 = f32[2,25,7,4,768]{4,2,3,1,0:T(8,128)S(1)} fusion(bf16[20,4,4,1,768]{4,0,1,2,3:T(8,128)(2,1)S(1)} %copy-done.8, bf16[20,4,4,1,768]{4,0,1,2,3:T(8,128)(2,1)S(1)} %copy-done.9, bf16[20,4,4,1,768]{4,0,1,2,3:T(8,128)(2,1)S(1)} %copy-done.10, bf16[20,4,4,1,768]{4,0,1,2,3:T(8,128)(2,1)S(1)} %copy-done.11, ...), kind=kOutput, calls=%fused_computation.79 | convolution fusion | flops 695992320 | bytes 8298496 | tf_op jit(solution)/shard_map/svirjq,vrqkc->sijkc/dot_general | solution.py:44
  74.3 9.1 %fusion.49 = f32[2,25,7,4,768]{4,2,3,1,0:T(8,128)S(1)} fusion(bf16[20,4,4,1,768]{4,0,1,2,3:T(8,128)(2,1)S(1)} %copy-done.12, bf16[20,4,4,1,768]{4,0,1,2,3:T(8,128)(2,1)S(1)} %copy-done.13, bf16[20,4,4,1,768]{4,0,1,2,3:T(8,128)(2,1)S(1)} %copy-done.14, bf16[20,4,4,1,768]{4,0,1,2,3:T(8,128)(2,1)S(1)} %copy-done.15, ...), kind=kOutput, calls=%fused_computation.78 | convolution fusion | flops 695992320 | bytes 8298496 | tf_op jit(solution)/shard_map/svirjq,vrqkc->sijkc/dot_general | solution.py:44
  83.5 9.3 %fusion.48 = f32[2,25,7,4,768]{4,2,3,1,0:T(8,128)S(1)} fusion(bf16[20,4,4,1,768]{4,0,1,2,3:T(8,128)(2,1)S(1)} %copy-done.16, bf16[20,4,4,1,768]{4,0,1,2,3:T(8,128)(2,1)S(1)} %copy-done.17, bf16[20,4,4,1,768]{4,0,1,2,3:T(8,128)(2,1)S(1)} %copy-done.18, bf16[20,4,4,1,768]{4,0,1,2,3:T(8,128)(2,1)S(1)} %copy-done.19, ...), kind=kOutput, calls=%fused_computation.77 | convolution fusion | flops 695992320 | bytes 8298496 | tf_op jit(solution)/shard_map/svirjq,vrqkc->sijkc/dot_general | solution.py:44
  92.9 9.1 %fusion.47 = f32[2,25,7,4,768]{4,2,3,1,0:T(8,128)S(1)} fusion(bf16[20,4,4,1,768]{4,0,1,2,3:T(8,128)(2,1)S(1)} %copy-done.22, bf16[20,4,4,1,768]{4,0,1,2,3:T(8,128)(2,1)S(1)} %copy-done.23, bf16[20,4,4,1,768]{4,0,1,2,3:T(8,128)(2,1)S(1)} %copy-done.20, bf16[20,4,4,1,768]{4,0,1,2,3:T(8,128)(2,1)S(1)} %copy-done.21, ...), kind=kOutput, calls=%fused_computation.76 | convolution fusion | flops 695992320 | bytes 8298496 | tf_op jit(solution)/shard_map/svirjq,vrqkc->sijkc/dot_general | solution.py:44
  105.1 3.8 reshape.253
  110.9 3.8 reshape.276
  114.7 8.0 %all-to-all-start = ((bf16[32,2,3456]{2,1,0:T(2,128)(2,1)}), bf16[32,2,3456]{2,1,0:T(2,128)(2,1)S(1)}, u32[]{:S(2)}, u32[]{:S(2)}) async-start(bf16[32,2,3456]{2,1,0:T(2,128)(2,1)} %reshape.276), calls=%async_computation | async-start | bytes 884736 | tf_op jit(solution)/shard_map/all_to_all | solution.py:170
  122.8 9.7 %all-to-all-done = bf16[32,2,3456]{2,1,0:T(2,128)(2,1)S(1)} async-done(((bf16[32,2,3456]{2,1,0:T(2,128)(2,1)}), bf16[32,2,3456]{2,1,0:T(2,128)(2,1)S(1)}, u32[]{:S(2)}, u32[]{:S(2)}) %all-to-all-start) | async-done | bytes 442400 | tf_op jit(solution)/shard_map/all_to_all | solution.py:170
  132.5 3.3 reshape.277
  137.6 3.8 reshape.215
  143.7 2.4 reshape.217
  147.6 2.4 reshape.219
  158.2 28.9 %reduce-scatter.7.cloned.1.call-done = bf16[24,6144]{1,0:T(8,128)(2,1)} async-done(((bf16[96,6144]{1,0:T(8,128)(2,1)}), bf16[24,6144]{1,0:T(8,128)(2,1)}) %reduce-scatter.7.cloned.1.call-update) | async-done | bytes 294928
  187.0 5.8 %reshape.272 = bf16[24,2,32,2,2,1,24]{6,4,3,2,1,0,5:T(2,128)(2,1)S(1)} reshape(bf16[24,6144]{1,0:T(8,128)(2,1)} %reduce-scatter.7.cloned.1.call-done) | data formatting | bytes 589824 | tf_op jit(solution)/shard_map/convert_element_type | solution.py:189
  194.5 2.9 reshape.278
  197.3 7.4 %all-to-all-start.1 = ((bf16[32,2,2304]{2,1,0:T(2,128)(2,1)}), bf16[32,2,2304]{2,1,0:T(2,128)(2,1)}, u32[]{:S(2)}, u32[]{:S(2)}) async-start(bf16[32,2,2304]{2,1,0:T(2,128)(2,1)} %reshape.278), calls=%async_computation.1 | async-start | bytes 589824 | tf_op jit(solution)/shard_map/all_to_all | solution.py:188
  204.8 5.1 %multiply_bitcast_fusion.1 = (f32[8,96,8,96]{3,2,1,0:T(8,128)}, f32[8,96,8,96]{3,2,1,0:T(8,128)S(1)}, f32[8,96,8,96]{3,2,1,0:T(8,128)}, f32[8,96,8,96]{3,2,1,0:T(8,128)}) fusion(f32[8,96,96]{2,1,0:T(8,128)S(1)} %get-tuple-element.33, f32[8,8]{1,0:T(8,128)S(1)} %fusion.165, f32[8,96,96]{2,1,0:T(8,128)} %get-tuple-element.60, ...), kind=kLoop, calls=%fused_computation.31 | loop fusion | flops 2359296 | bytes 10617088 | tf_op jit(solution)/shard_map/bio,bd->bido/transpose | solution.py:92
  209.9 4.4 %reshape.221 = f32[768,768]{1,0:T(8,128)} reshape(f32[8,96,8,96]{3,2,1,0:T(8,128)} %get-tuple-element.42) | data formatting | bytes 4718592 | tf_op jit(solution)/shard_map/reshape | solution.py:93
  216.4 3.1 reshape.223
  219.5 4.5 %reshape.224 = f32[768,768]{1,0:T(8,128)} reshape(f32[8,96,8,96]{3,2,1,0:T(8,128)} %get-tuple-element.41) | data formatting | bytes 4718592 | tf_op jit(solution)/shard_map/reshape | solution.py:93
  223.9 6.8 %reshape.279 = bf16[32,1,2,24,2,2,24]{6,5,4,3,2,1,0:T(2,128)(2,1)} reshape(bf16[32,2,2304]{2,1,0:T(2,128)(2,1)} %all-to-all-done.1) | data formatting | bytes 589824
  230.8 2.7 bitcast_bitcast_fusion.2
  233.5 2.2 copy.148
  235.7 3.6 reshape.220
  239.7 2.8 fusion.245
  245.9 2.2 fusion.248
  249.0 2.2 fusion.73
  253.3 3.1 fusion.72
  262.9 17.3 %all_to_all.48 = bf16[32,2,2304]{2,1,0:T(2,128)(2,1)S(1)} all-to-all(bf16[32,2,2304]{2,1,0:T(2,128)(2,1)S(1)} %reshape.280), channel_id=1, replica_groups=mesh['lat'=4,'lon'=32] {'lon'}, dimensions={0} | all-to-all | bytes 589824 | tf_op jit(solution)/shard_map/all_to_all | solution.py:194
  280.2 2.2 reshape.281
  285.4 3.0 reshape.225
  293.0 29.6 %reduce-scatter.9.cloned.1.call-done = bf16[24,6144]{1,0:T(8,128)(2,1)} async-done(((bf16[96,6144]{1,0:T(8,128)(2,1)}), bf16[24,6144]{1,0:T(8,128)(2,1)}) %reduce-scatter.9.cloned.1.call-update) | async-done | bytes 294928
  327.6 3.2 convert_element_type.127
  330.8 3.0 bitcast_bitcast_fusion
  333.8 8.1 %reshape.282 = bf16[32,2,3456]{2,1,0:T(2,128)(2,1)S(1)} reshape(bf16[32,1,6,24,2,24]{5,4,3,2,1,0:T(2,128)(2,1)} %bitcast_bitcast_fusion) | data formatting | bytes 884736
  341.9 18.2 %all_to_all.49 = bf16[32,2,3456]{2,1,0:T(2,128)(2,1)S(1)} all-to-all(bf16[32,2,3456]{2,1,0:T(2,128)(2,1)S(1)} %reshape.282), channel_id=1, replica_groups=mesh['lat'=4,'lon'=32] {'lon'}, dimensions={0} | all-to-all | bytes 884736 | tf_op jit(solution)/shard_map/all_to_all | solution.py:212
  360.1 3.3 reshape.283
  363.4 2.6 convert_bitcast_fusion
  366.0 4.9 %copy.171 = f32[1,6,24,2,32,1,24]{6,4,1,2,3,5,0:T(8,128)} copy(f32[1,6,24,2,32,1,24]{6,3,2,1,4,5,0:T(2,128)S(1)} %convert_bitcast_fusion) | data formatting | bytes 1769472 | tf_op jit(solution)/shard_map/transpose | solution.py:216
  371.0 4.8 %reshape.267 = f32[6,24,2,768]{3,0,1,2:T(8,128)S(1)} reshape(f32[1,6,24,2,32,1,24]{6,4,1,2,3,5,0:T(8,128)} %copy.171) | data formatting | bytes 1769472 | tf_op jit(solution)/shard_map/transpose | solution.py:216
  377.1 13.7 %fusion.51 = f32[288,768]{1,0:T(8,128)S(1)} fusion(bf16[3072,768]{1,0:T(8,128)(2,1)} %param.17, bf16[288,768]{1,0:T(8,128)(2,1)S(1)} %reshape.227, bf16[768,3072]{1,0:T(8,128)(2,1)} %param.16), kind=kOutput, calls=%fused_computation.80 | convolution fusion | flops 2775416832 | bytes 10764288 | tf_op jit(solution)/shard_map/dot_general | solution.py:75
  (155 shorter events, 67.6 us)
Async XLA Ops:
  8.8 34.6 %collective-permute-start = (bf16[2,20,4,48]{2,3,1,0:T(8,128)(2,1)}, bf16[2,20,4,48]{2,3,1,0:T(8,128)(2,1)S(1)}, u32[]{:S(2)}, u32[]{:S(2)}) collective-permute-start(bf16[2,20,4,48]{2,3,1,0:T(8,128)(2,1)} %get-tuple-element.29), channel_id=1, source_target_pairs={{0,32},{32,64},{64,96},{96,0},{1,33},{33,65},{65,97},{97,1},{2,34}... | collective-permute-start | bytes 46088 | tf_op jit(solution)/shard_map/ppermute | solution.py:18
  8.8 34.6 %collective-permute-start.1 = (bf16[2,20,4,48]{2,3,1,0:T(8,128)(2,1)}, bf16[2,20,4,48]{2,3,1,0:T(8,128)(2,1)S(1)}, u32[]{:S(2)}, u32[]{:S(2)}) collective-permute-start(bf16[2,20,4,48]{2,3,1,0:T(8,128)(2,1)} %get-tuple-element.30), channel_id=1, source_target_pairs={{32,0},{64,32},{96,64},{0,96},{33,1},{65,33},{97,65},{1,97},{34,2}... | collective-permute-start | bytes 46088 | tf_op jit(solution)/shard_map/ppermute | solution.py:21
  40.8 2.7 copy-start.5
  42.1 9.4 %copy-start.28 = (f32[768]{0:T(1024)S(1)}, f32[768]{0:T(1024)}, u32[]{:S(2)}) copy-start(f32[768]{0:T(1024)} %param.11) | copy-start | bytes 9220
  43.7 10.0 %collective-permute-start.2 = (bf16[2,20,200,4]{2,3,1,0:T(4,128)(2,1)S(1)}, bf16[2,20,200,4]{2,3,1,0:T(4,128)(2,1)S(1)}, u32[]{:S(2)}, u32[]{:S(2)}) collective-permute-start(bf16[2,20,200,4]{2,3,1,0:T(4,128)(2,1)S(1)} %get-tuple-element.27), channel_id=1, source_target_pairs={{0,1},{1,2},{2,3},{3,4},{4,5},{5,6},{6,7},{7,8},{8,9},{9,10},{10,1... | collective-permute-start | bytes 192008 | tf_op jit(solution)/shard_map/ppermute | solution.py:18
  45.8 7.9 %collective-permute-start.3 = (bf16[2,20,200,4]{2,3,1,0:T(4,128)(2,1)S(1)}, bf16[2,20,200,4]{2,3,1,0:T(4,128)(2,1)S(1)}, u32[]{:S(2)}, u32[]{:S(2)}) collective-permute-start(bf16[2,20,200,4]{2,3,1,0:T(4,128)(2,1)S(1)} %get-tuple-element.28), channel_id=1, source_target_pairs={{1,0},{2,1},{3,2},{4,3},{5,4},{6,5},{7,6},{8,7},{9,8},{10,9},{11,1... | collective-permute-start | bytes 192008 | tf_op jit(solution)/shard_map/ppermute | solution.py:21
  61.5 3.8 copy-start.8
  61.5 3.8 copy-start.9
  61.5 3.8 copy-start.10
  61.5 3.8 copy-start.11
  65.3 9.0 %copy-start.12 = (bf16[20,4,4,1,768]{4,0,1,2,3:T(8,128)(2,1)S(1)}, bf16[20,4,4,1,768]{4,0,1,2,3:T(8,128)(2,1)}, u32[]{:S(2)}) copy-start(bf16[20,4,4,1,768]{4,0,1,2,3:T(8,128)(2,1)} %get-tuple-element.51) | copy-start | bytes 1474564
  65.3 9.0 %copy-start.13 = (bf16[20,4,4,1,768]{4,0,1,2,3:T(8,128)(2,1)S(1)}, bf16[20,4,4,1,768]{4,0,1,2,3:T(8,128)(2,1)}, u32[]{:S(2)}) copy-start(bf16[20,4,4,1,768]{4,0,1,2,3:T(8,128)(2,1)} %get-tuple-element.52) | copy-start | bytes 1474564
  65.3 9.0 %copy-start.14 = (bf16[20,4,4,1,768]{4,0,1,2,3:T(8,128)(2,1)S(1)}, bf16[20,4,4,1,768]{4,0,1,2,3:T(8,128)(2,1)}, u32[]{:S(2)}) copy-start(bf16[20,4,4,1,768]{4,0,1,2,3:T(8,128)(2,1)} %get-tuple-element.53) | copy-start | bytes 1474564
  65.3 9.0 %copy-start.15 = (bf16[20,4,4,1,768]{4,0,1,2,3:T(8,128)(2,1)S(1)}, bf16[20,4,4,1,768]{4,0,1,2,3:T(8,128)(2,1)}, u32[]{:S(2)}) copy-start(bf16[20,4,4,1,768]{4,0,1,2,3:T(8,128)(2,1)} %get-tuple-element.54) | copy-start | bytes 1474564
  74.3 9.2 %copy-start.16 = (bf16[20,4,4,1,768]{4,0,1,2,3:T(8,128)(2,1)S(1)}, bf16[20,4,4,1,768]{4,0,1,2,3:T(8,128)(2,1)}, u32[]{:S(2)}) copy-start(bf16[20,4,4,1,768]{4,0,1,2,3:T(8,128)(2,1)} %get-tuple-element.47) | copy-start | bytes 1474564
  74.3 9.2 %copy-start.17 = (bf16[20,4,4,1,768]{4,0,1,2,3:T(8,128)(2,1)S(1)}, bf16[20,4,4,1,768]{4,0,1,2,3:T(8,128)(2,1)}, u32[]{:S(2)}) copy-start(bf16[20,4,4,1,768]{4,0,1,2,3:T(8,128)(2,1)} %get-tuple-element.48) | copy-start | bytes 1474564
  74.3 9.2 %copy-start.18 = (bf16[20,4,4,1,768]{4,0,1,2,3:T(8,128)(2,1)S(1)}, bf16[20,4,4,1,768]{4,0,1,2,3:T(8,128)(2,1)}, u32[]{:S(2)}) copy-start(bf16[20,4,4,1,768]{4,0,1,2,3:T(8,128)(2,1)} %get-tuple-element.49) | copy-start | bytes 1474564
  74.3 9.2 %copy-start.19 = (bf16[20,4,4,1,768]{4,0,1,2,3:T(8,128)(2,1)S(1)}, bf16[20,4,4,1,768]{4,0,1,2,3:T(8,128)(2,1)}, u32[]{:S(2)}) copy-start(bf16[20,4,4,1,768]{4,0,1,2,3:T(8,128)(2,1)} %get-tuple-element.50) | copy-start | bytes 1474564
  83.5 9.4 %copy-start.20 = (bf16[20,4,4,1,768]{4,0,1,2,3:T(8,128)(2,1)S(1)}, bf16[20,4,4,1,768]{4,0,1,2,3:T(8,128)(2,1)}, u32[]{:S(2)}) copy-start(bf16[20,4,4,1,768]{4,0,1,2,3:T(8,128)(2,1)} %get-tuple-element.45) | copy-start | bytes 1474564
  83.5 9.4 %copy-start.21 = (bf16[20,4,4,1,768]{4,0,1,2,3:T(8,128)(2,1)S(1)}, bf16[20,4,4,1,768]{4,0,1,2,3:T(8,128)(2,1)}, u32[]{:S(2)}) copy-start(bf16[20,4,4,1,768]{4,0,1,2,3:T(8,128)(2,1)} %get-tuple-element.46) | copy-start | bytes 1474564
  83.5 9.4 %copy-start.22 = (bf16[20,4,4,1,768]{4,0,1,2,3:T(8,128)(2,1)S(1)}, bf16[20,4,4,1,768]{4,0,1,2,3:T(8,128)(2,1)}, u32[]{:S(2)}) copy-start(bf16[20,4,4,1,768]{4,0,1,2,3:T(8,128)(2,1)} %get-tuple-element.43) | copy-start | bytes 1474564
  83.5 9.4 %copy-start.23 = (bf16[20,4,4,1,768]{4,0,1,2,3:T(8,128)(2,1)S(1)}, bf16[20,4,4,1,768]{4,0,1,2,3:T(8,128)(2,1)}, u32[]{:S(2)}) copy-start(bf16[20,4,4,1,768]{4,0,1,2,3:T(8,128)(2,1)} %get-tuple-element.44) | copy-start | bytes 1474564
  103.6 0.8 copy-start.3
  104.5 0.6 copy-start.24
  108.9 1.0 copy-start.26
  114.7 17.8 %all-to-all-start = ((bf16[32,2,3456]{2,1,0:T(2,128)(2,1)}), bf16[32,2,3456]{2,1,0:T(2,128)(2,1)S(1)}, u32[]{:S(2)}, u32[]{:S(2)}) async-start(bf16[32,2,3456]{2,1,0:T(2,128)(2,1)} %reshape.276), calls=%async_computation | async-start | bytes 884736 | tf_op jit(solution)/shard_map/all_to_all | solution.py:170
  122.7 64.3 %reduce-scatter.7.cloned.1.call-start = ((), (), s32[]{:S(2)}) async-start(), calls=%async_computation.6 | async-start | bytes 1474560
  155.3 1.4 copy-start.6
  155.3 1.8 copy-start.7
  197.3 26.6 %all-to-all-start.1 = ((bf16[32,2,2304]{2,1,0:T(2,128)(2,1)}), bf16[32,2,2304]{2,1,0:T(2,128)(2,1)}, u32[]{:S(2)}, u32[]{:S(2)}) async-start(bf16[32,2,2304]{2,1,0:T(2,128)(2,1)} %reshape.278), calls=%async_computation.1 | async-start | bytes 589824 | tf_op jit(solution)/shard_map/all_to_all | solution.py:188
  204.7 118.0 %reduce-scatter.9.cloned.1.call-start = ((), (), s32[]{:S(2)}) async-start(), calls=%async_computation.7 | async-start | bytes 1474560
  219.4 4.5 %copy-start.29 = (f32[2,768]{1,0:T(2,128)S(1)}, f32[2,768]{1,0:T(2,128)}, u32[]{:S(2)}) copy-start(f32[2,768]{1,0:T(2,128)} %param.13) | copy-start | bytes 18436
  239.7 2.8 copy-start.2
  243.4 2.5 copy-start.1
  244.4 3.7 copy-start
  370.9 4.8 %copy-start.4 = (bf16[2,24,6,1,768]{4,2,3,1,0:T(8,128)(2,1)S(1)}, bf16[2,24,6,1,768]{4,2,3,1,0:T(8,128)(2,1)}, u32[]{:S(2)}) copy-start(bf16[2,24,6,1,768]{4,2,3,1,0:T(8,128)(2,1)} %copy-done.3) | copy-start | bytes 1327108
  370.9 4.8 %copy-start.25 = (f32[2,24,6]{2,1,0:T(8,128)S(1)}, f32[2,24,6]{2,1,0:T(8,128)}, u32[]{:S(2)}) copy-start(f32[2,24,6]{2,1,0:T(8,128)} %copy-done.24) | copy-start | bytes 3460
  370.9 4.8 %copy-start.27 = (f32[2,24,6]{2,1,0:T(8,128)S(1)}, f32[2,24,6]{2,1,0:T(8,128)}, u32[]{:S(2)}) copy-start(f32[2,24,6]{2,1,0:T(8,128)} %copy-done.26) | copy-start | bytes 3460
  375.8 0.9 copy-start.30
Sparse Core Ops, SparseCore 0:
  156.6 30.3 reduce-scatter.6
  293.2 29.4 reduce-scatter.8
where the time goes:
time: 407 us; the launch traced here: 399 us
  local copies, waits for them, and re-layouts  158 us (39%)
  matrix products  76.2 us (19%)
  waiting for transfers between devices  70.4 us (17%)
  blocking collectives  35.5 us (9%)
  starting transfers between devices  26.3 us (6%)
  other arithmetic  18.2 us (4%)
  between operations  14.6 us (4%)
    unnamed x4, waiting for transfers between devices  58.5 us
    unnamed x74, local copies, waits for them, and re-layouts  40.5 us
    dot_general x4, matrix products, embed(): jnp.einsum('svirjq,vrqkc->sijkc', view, chosen, preferred_element_type=jn...  36.5 us
    dot_general x20, matrix products, high_dot(): return jnp.dot(left, right, precision=lax.Precision.HIGHEST)  26.1 us
    all_to_all x1, blocking collectives, local(): lax.all_to_all(surface.astype(jnp.bfloat16), 'lon', split_axis=0, concat_...  18.2 us
    all_to_all x1, blocking collectives, local(): lax.all_to_all(outgoing.astype(jnp.bfloat16), 'lon', split_axis=5, concat...  17.3 us
    reshape x1, local copies, waits for them, and re-layouts, embed(): table = weight.reshape(4, 4, depth, half, half, width)  14 us
    reshape x4, local copies, waits for them, and re-layouts, dense_block(): return spread_out.reshape(blocks * width, blocks * width)  14 us
  transfers between devices with their start and end apart: 8, of which 4 were waited for; matrix products, arithmetic and copies ran while one was open for 13% of the time, Pallas kernels for 0%

commit v1 on v0

v1 whole, which is shorter than its diff:
```python
import math

import jax
import jax.numpy as jnp
import numpy as np
from jax import lax
from jax.experimental import pallas as pl
from jax.experimental.pallas import tpu as pltpu
from jax.sharding import PartitionSpec as P

MESH = pl.DeviceIdType.MESH
F32 = jnp.float32
BF16 = jnp.bfloat16

NLAT, NLON = 4, 32
NV, C, HID, NB, BS = 20, 768, 3072, 8, 96
H, W, KW = 96, 192, 64
ROWS, COLS = 24, 6
ROW12 = 12
MSG = ROW12 * BS


def pick_table():
    sel = np.zeros((64, 48), np.float32)
    for q8 in range(8):
        for jj in range(7):
            lon = 8 * jj + q8 - 4
            if 0 <= lon < 48:
                sel[q8 * 8 + jj, lon] = 1.0
    return sel


def feature_table(shift):
    table = np.zeros((4, 160, 768), np.float32)
    for q in range(4):
        for v in range(NV):
            for r8 in range(8):
                table[q, v * 8 + r8, (r8 // 4) * 384 + shift + v * 16 + (r8 % 4) * 4 + q] = 1.0
    return table


def lon_tables():
    k = np.arange(KW)
    w = np.arange(W)
    angle = 2.0 * math.pi * ((k[:, None] * w[None, :]) % W) / W
    scale = 1.0 / math.sqrt(W)
    both = np.stack([np.cos(angle), -np.sin(angle)]) * scale
    fwd = both.reshape(2, 8, 8, NLON, COLS).transpose(1, 0, 2, 3, 4).reshape(128, NLON, COLS)
    fwd = np.pad(fwd, ((0, 0), (0, 0), (0, 2))).reshape(128, 256)
    weight = np.where(k == 0, 1.0, 2.0)
    back = both * weight[None, :, None]
    back = back.reshape(2, 8, 8, NLON, COLS).transpose(3, 4, 1, 0, 2).reshape(NLON, COLS, 128)
    back = np.pad(back, ((0, 0), (0, 2), (0, 0))).reshape(256, 128)
    return fwd, back


def lat_tables():
    h = np.arange(H)
    angle = 2.0 * math.pi * ((h[:, None] * h[None, :]) % H) / H
    cos, sin = np.cos(angle) / math.sqrt(H), np.sin(angle) / math.sqrt(H)
    fwd = np.block([[cos, sin], [-sin, cos]])
    back = np.block([[cos, -sin], [sin, cos]])
    return fwd, back


def norm(values, gain):
    centre = jnp.mean(values, axis=-1, keepdims=True)
    off = values - centre
    spread = jnp.mean(jnp.square(off), axis=-1, keepdims=True)
    return off * lax.rsqrt(spread + 1e-05) * gain


def dot(left, right):
    return jnp.dot(left, right, preferred_element_type=F32)


def kernel(
    grid_h, pw_h, one_h, two_h, up_h, down_h, elo_h, ehi_h,
    g1_ref, bias_ref, g2_ref, sel_ref, fw_ref, bw_ref, fh_ref, bh_ref,
    out_ref,
    grid_v, pw_v, one_v, two_v, up_v, down_v, elo_v, ehi_v,
    t_v, lo_v, hi_v, s_v, lhs_v, acc_v, tn_v, mid_v, nrm_v,
    ew_s, ew_r, ns_s, ns_r,
    p1_s, p1_r, p2_s, p2_r, p3_s, p3_r, p4_s, p4_r,
    z_v, v_v, w1_v, w2_v,
    lsem, halo_ss, halo_rs, s1, r1, s2, r2, s3, r3, s4, r4,
):
    a = lax.axis_index("lat")
    b = lax.axis_index("lon")
    q = b // 16
    p = b % 16
    n = b % 8
    g = 2 * a + q

    def load(index, src, dst):
        copy = pltpu.make_async_copy(src, dst, lsem.at[index])
        copy.start()
        return copy

    c_grid = load(0, grid_h, grid_v)
    c_elo = load(1, elo_h, elo_v)
    c_ehi = load(2, ehi_h, ehi_v)
    c_pw = load(3, pw_h, pw_v)
    c_one = load(4, one_h.at[:, n], one_v)
    c_two = load(5, two_h.at[:, n], two_v)
    c_up = load(6, up_h, up_v)
    c_down = load(7, down_h, down_v)

    barrier = pltpu.get_barrier_semaphore()

    def greet_lon(d, _):
        pl.semaphore_signal(
            barrier, inc=1, device_id=(a, lax.rem(b + d, NLON)), device_id_type=MESH
        )
        return 0

    lax.fori_loop(1, NLON, greet_lon, 0)

    def greet_lat(d, _):
        mate = lax.rem(a + 1 + d // 2, NLAT)
        pl.semaphore_signal(
            barrier, inc=1, device_id=(mate, (d % 2) * 16 + p), device_id_type=MESH
        )
        return 0

    lax.fori_loop(0, 6, greet_lat, 0)

    c_grid.wait()

    def turn(it, _):
        smp = it // 12
        rp = it % 12
        block = grid_v[smp, :, pl.ds(pl.multiple_of(16 * rp, 16), 16), :]
        block = block.astype(F32).reshape(NV, 2, 8, 48)
        turned = []
        for half in range(2):
            x = block[:, half].reshape(NV * 8, 48).astype(BF16)
            turned.append(
                lax.dot_general(
                    sel_ref[...], x, (((1,), (1,)), ((), ())), preferred_element_type=F32
                )
            )
        for q8 in range(8):
            pair = jnp.concatenate([t[8 * q8 : 8 * q8 + 8] for t in turned], axis=0)
            t_v[q8, pl.ds(pl.multiple_of(16 * it, 16), 16), :] = pair.astype(BF16)
        return 0

    lax.fori_loop(0, 24, turn, 0)

    c_elo.wait()
    c_ehi.wait()
    for part, (table, total) in enumerate(((elo_v, lo_v), (ehi_v, hi_v))):
        value = dot(t_v[4 * part], table[0])
        for i in range(1, 4):
            value = value + dot(t_v[4 * part + i], table[i])
        for tile in range(6):
            total[tile] = value[:, 128 * tile : 128 * tile + 128]

    pl.semaphore_wait(barrier, NLON - 1 + 6)

    def remote(src, dst, ssem, rsem, dev):
        return pltpu.make_async_remote_copy(
            src_ref=src, dst_ref=dst, send_sem=ssem, recv_sem=rsem,
            device_id=dev, device_id_type=MESH,
        )

    for tile in range(6):
        cols = slice(128 * tile, 128 * tile + 128)
        ew_s[0, :, cols] = lo_v[tile, pl.ds(6, 48, stride=8), :].astype(BF16)
        ew_s[1, :, cols] = hi_v[tile, pl.ds(0, 48, stride=8), :].astype(BF16)
    east = remote(ew_s.at[0], ew_r.at[0], halo_ss.at[0], halo_rs.at[0], (a, lax.rem(b + 1, NLON)))
    west = remote(
        ew_s.at[1], ew_r.at[1], halo_ss.at[1], halo_rs.at[1], (a, lax.rem(b + NLON - 1, NLON))
    )
    east.start()
    west.start()
    east.wait_recv()
    west.wait_recv()
    for tile in range(6):
        cols = slice(128 * tile, 128 * tile + 128)
        lo_v[tile, pl.ds(0, 48, stride=8), :] = ew_r[0, :, cols].astype(F32)
        hi_v[tile, pl.ds(6, 48, stride=8), :] = ew_r[1, :, cols].astype(F32)
    for half in range(2):
        lo = [lo_v[3 * half + tile] for tile in range(3)]
        hi = [hi_v[3 * half + tile] for tile in range(3)]
        for tile, value in enumerate((lo[0], lo[1], lo[2] + hi[0], hi[1], hi[2])):
            both = value.reshape(2, ROWS, 8, 128)
            for smp in range(2):
                s_v[half, smp, 1 : 1 + ROWS, :, 128 * tile : 128 * tile + 128] = both[smp]
    ns_s[0] = s_v[1, :, ROWS].astype(BF16)
    ns_s[1] = s_v[0, :, 1].astype(BF16)
    south = remote(ns_s.at[0], ns_r.at[0], halo_ss.at[2], halo_rs.at[2], (lax.rem(a + 1, NLAT), b))
    north = remote(
        ns_s.at[1], ns_r.at[1], halo_ss.at[3], halo_rs.at[3], (lax.rem(a + NLAT - 1, NLAT), b)
    )
    south.start()
    north.start()

    c_pw.wait()
    for count, (off, half, first) in enumerate(((1, 0, 1), (2, 1, 1), (0, 1, 0), (3, 0, 2))):
        if count == 2:
            south.wait_recv()
            north.wait_recv()
            s_v[1, :, 0] = jnp.where(a > 0, ns_r[0].astype(F32), 0.0)
            s_v[0, :, ROWS + 1] = jnp.where(a < NLAT - 1, ns_r[1].astype(F32), 0.0)
        for smp in range(2):
            x = s_v[half, smp, first : first + ROWS]
            rows = slice(192 * smp, 192 * smp + 192)
            lhs_v[rows, :640] = x.reshape(192, 640).astype(BF16)
            shifted = jnp.concatenate([x[:, 1:], x[:, :1]], axis=1)
            lhs_v[rows, 640:] = shifted.reshape(192, 640).astype(BF16)
        for tile in range(3):
            cols = slice(256 * tile, 256 * tile + 256)
            value = dot(lhs_v[...], pw_v[1280 * off : 1280 * off + 1280, cols])
            if count == 0:
                acc_v[:, cols] = value
            else:
                acc_v[:, cols] += value

    def send_tokens(c, _):
        rows = pl.ds(pl.multiple_of(c * 96, 96), 96)
        tok = acc_v[rows, :].astype(BF16).astype(F32)
        normed = norm(tok, g1_ref[...]).astype(BF16).astype(F32)
        tn_v[rows, :] = tok + normed
        planes = normed.reshape(ROW12, 8, C)
        smp = c // 2
        part = c % 2
        for blk in range(NB):
            msg = jnp.concatenate(
                [planes[i][:, BS * blk : BS * blk + BS] for i in range(ROW12)], axis=1
            )
            dest = part * 16 + smp * 8 + blk
            p1_s[dest] = msg.astype(BF16)

            @pl.when(dest != b)
            def _():
                remote(p1_s.at[dest], p1_r.at[b], s1.at[dest], r1.at[b], (a, dest)).start()

            @pl.when(dest == b)
            def _():
                p1_r[b] = msg.astype(BF16)

        return 0

    lax.fori_loop(0, 4, send_tokens, 0)

    c_one.wait()
    c_two.wait()
    for src, dst in ((one_v, w1_v), (two_v, w2_v)):
        dst[...] = jnp.zeros_like(dst)
        dst[0:BS, 0:BS] = src[0].astype(BF16)
        dst[0:BS, 128 : 128 + BS] = src[1].astype(BF16)
        dst[128 : 128 + BS, 0:BS] = -src[1].astype(BF16)
        dst[128 : 128 + BS, 128 : 128 + BS] = src[0].astype(BF16)
    bias = jnp.zeros((1, 256), F32)
    for blk in range(NB):
        parts = []
        for ri in range(2):
            parts.append(bias_ref[ri : ri + 1, BS * blk : BS * blk + BS])
            parts.append(jnp.zeros((1, 32), F32))
        bias = bias + jnp.where(n == blk, jnp.concatenate(parts, axis=1), 0.0)

    def wait1(d, _):
        src = lax.rem(b + d, NLON)
        remote(p1_s.at[src], p1_r.at[src], s1.at[src], r1.at[src], (a, src)).wait_recv()
        return 0

    lax.fori_loop(1, NLON, wait1, 0)

    x = p1_r[...].astype(F32).reshape(256, MSG).astype(BF16)
    y = dot(fw_ref[...], x)
    p2_s[...] = y.reshape(8, 16, MSG).astype(BF16)

    def mate_of(d):
        other = lax.rem(g + d, 8)
        return other, (other // 2, (other % 2) * 16 + p)

    def send2(d, _):
        other, dev = mate_of(d)
        remote(p2_s.at[other], p2_r.at[g], s2.at[other], r2.at[g], dev).start()
        return 0

    lax.fori_loop(1, 8, send2, 0)

    def spread(src, value):
        for i in range(ROW12):
            piece = value[:, BS * i : BS * i + BS]
            piece = jnp.concatenate([piece, jnp.zeros((16, 128 - BS), F32)], axis=1)
            z_v[pl.ds(ROW12 * src + i, 8, stride=192), :] = piece[:8]
            z_v[pl.ds(H + ROW12 * src + i, 8, stride=192), :] = piece[8:]

    spread(g, p2_s[g].astype(F32))

    def take2(d, _):
        other, dev = mate_of(d)
        remote(p2_s.at[other], p2_r.at[other], s2.at[other], r2.at[other], dev).wait_recv()
        spread(other, p2_r[other].astype(F32))
        return 0

    lax.fori_loop(1, 8, take2, 0)

    for pair in range(4):
        k0, k1 = 384 * pair, 384 * pair + 192
        z = jnp.concatenate([z_v[k0 : k0 + 192, :], z_v[k1 : k1 + 192, :]], axis=1).astype(BF16)
        spec = dot(fh_ref[...], z)
        modes = jnp.concatenate(
            [
                jnp.concatenate([spec[:H, :128], spec[H:, :128]], axis=1),
                jnp.concatenate([spec[:H, 128:], spec[H:, 128:]], axis=1),
            ],
            axis=0,
        )
        mid = jnp.maximum(dot(modes.astype(BF16), w1_v[...]) + bias, 0.0)
        res = dot(mid.astype(BF16), w2_v[...])
        res = res - jnp.clip(res, -0.01, 0.01)
        back = jnp.concatenate(
            [
                jnp.concatenate([res[:H, :128], res[H:, :128]], axis=1),
                jnp.concatenate([res[:H, 128:], res[H:, 128:]], axis=1),
            ],
            axis=0,
        )
        rows = dot(bh_ref[...], back.astype(BF16))
        v_v[k0 : k0 + 192, :] = rows[:, :128]
        v_v[k1 : k1 + 192, :] = rows[:, 128:]

    def gather_rows(dest):
        pieces = []
        for i in range(ROW12):
            re = v_v[pl.ds(ROW12 * dest + i, 8, stride=192), :]
            im = v_v[pl.ds(H + ROW12 * dest + i, 8, stride=192), :]
            pieces.append(jnp.concatenate([re, im], axis=0)[:, :BS])
        return jnp.concatenate(pieces, axis=1).astype(BF16)

    def send3(d, _):
        other, dev = mate_of(d)
        p3_s[other] = gather_rows(other)
        remote(p3_s.at[other], p3_r.at[g], s3.at[other], r3.at[g], dev).start()
        return 0

    lax.fori_loop(1, 8, send3, 0)
    p3_r[g] = gather_rows(g)

    def wait3(d, _):
        other, dev = mate_of(d)
        remote(p3_s.at[other], p3_r.at[other], s3.at[other], r3.at[other], dev).wait_recv()
        return 0

    lax.fori_loop(1, 8, wait3, 0)

    field = dot(bw_ref[...], p3_r[...].reshape(128, MSG))
    p4_s[...] = field.reshape(NLON, 8, MSG).astype(BF16)

    def send4(d, _):
        dest = lax.rem(b + d, NLON)
        remote(p4_s.at[dest], p4_r.at[b], s4.at[dest], r4.at[b], (a, dest)).start()
        return 0

    lax.fori_loop(1, NLON, send4, 0)
    p4_r[b] = p4_s[b]

    def wait4(d, _):
        src = lax.rem(b + d, NLON)
        remote(p4_s.at[src], p4_r.at[src], s4.at[src], r4.at[src], (a, src)).wait_recv()
        return 0

    lax.fori_loop(1, NLON, wait4, 0)

    def join(c, _):
        rows = pl.ds(pl.multiple_of(c * 96, 96), 96)
        smp = c // 2
        part = c % 2
        msgs = [p4_r[part * 16 + smp * 8 + blk].astype(F32) for blk in range(NB)]
        planes = [
            jnp.concatenate([m[:, BS * i : BS * i + BS] for m in msgs], axis=1)
            for i in range(ROW12)
        ]
        middle = jnp.concatenate(planes, axis=0) + tn_v[rows, :]
        middle = middle.astype(BF16).astype(F32)
        mid_v[rows, :] = middle
        nrm_v[rows, :] = norm(middle, g2_ref[...]).astype(BF16)
        return 0

    lax.fori_loop(0, 4, join, 0)

    c_up.wait()
    c_down.wait()

    def mlp(step, _):
        cols = pl.ds(pl.multiple_of(step * 256, 256), 256)
        hidden = dot(nrm_v[...], up_v[:, cols])
        hidden = 0.5 * hidden * (1.0 + lax.erf(hidden * (1.0 / math.sqrt(2.0))))
        mid_v[...] += dot(hidden.astype(BF16), down_v[cols, :])
        return 0

    lax.fori_loop(0, HID // 256, mlp, 0)

    for smp in range(2):
        rows = slice(192 * smp, 192 * smp + 192)
        out_ref[smp] = mid_v[rows, :].reshape(ROWS, 8, C)[:, :COLS].astype(BF16)

    for copy in (east, west, south, north):
        copy.wait_send()

    def drain_lon(d, _):
        dest = lax.rem(b + d, NLON)
        remote(p1_s.at[dest], p1_r.at[b], s1.at[dest], r1.at[b], (a, dest)).wait_send()
        remote(p4_s.at[dest], p4_r.at[b], s4.at[dest], r4.at[b], (a, dest)).wait_send()
        return 0

    lax.fori_loop(1, NLON, drain_lon, 0)

    def drain_lat(d, _):
        other, dev = mate_of(d)
        remote(p2_s.at[other], p2_r.at[g], s2.at[other], r2.at[g], dev).wait_send()
        remote(p3_s.at[other], p3_r.at[g], s3.at[other], r3.at[g], dev).wait_send()
        return 0

    lax.fori_loop(1, 8, drain_lat, 0)


def local(
    grid, patch_weight, norm_gain_one, spectral_one, spectral_bias, spectral_two,
    norm_gain_two, fc_up, fc_down,
):
    fw, bw = lon_tables()
    fh, bh = lat_tables()
    const = lambda x: jnp.asarray(x, F32).astype(BF16)
    any_spec = pl.BlockSpec(memory_space=pl.ANY)
    vmem = pl.BlockSpec(memory_space=pltpu.VMEM)
    dma = pltpu.SemaphoreType.DMA
    return pl.pallas_call(
        kernel,
        out_shape=jax.ShapeDtypeStruct((2, ROWS, COLS, C), BF16),
        in_specs=[any_spec] * 8 + [vmem] * 8,
        out_specs=vmem,
        scratch_shapes=[
            pltpu.VMEM((2, NV, 192, 48), BF16),
            pltpu.VMEM((5120, C), BF16),
            pltpu.VMEM((2, BS, BS), F32),
            pltpu.VMEM((2, BS, BS), F32),
            pltpu.VMEM((C, HID), BF16),
            pltpu.VMEM((HID, C), BF16),
            pltpu.VMEM((4, 160, 768), BF16),
            pltpu.VMEM((4, 160, 768), BF16),
            pltpu.VMEM((8, 384, 160), BF16),
            pltpu.VMEM((6, 384, 128), F32),
            pltpu.VMEM((6, 384, 128), F32),
            pltpu.VMEM((2, 2, ROWS + 2, 8, 640), F32),
            pltpu.VMEM((384, 1280), BF16),
            pltpu.VMEM((384, C), F32),
            pltpu.VMEM((384, C), F32),
            pltpu.VMEM((384, C), F32),
            pltpu.VMEM((384, C), BF16),
            pltpu.VMEM((2, 48, 768), BF16),
            pltpu.VMEM((2, 48, 768), BF16),
            pltpu.VMEM((2, 2, 8, 640), BF16),
            pltpu.VMEM((2, 2, 8, 640), BF16),
            pltpu.VMEM((NLON, 8, MSG), BF16),
            pltpu.VMEM((NLON, 8, MSG), BF16),
            pltpu.VMEM((8, 16, MSG), BF16),
            pltpu.VMEM((8, 16, MSG), BF16),
            pltpu.VMEM((8, 16, MSG), BF16),
            pltpu.VMEM((8, 16, MSG), BF16),
            pltpu.VMEM((NLON, 8, MSG), BF16),
            pltpu.VMEM((NLON, 8, MSG), BF16),
            pltpu.VMEM((8 * 192, 128), F32),
            pltpu.VMEM((8 * 192, 128), F32),
            pltpu.VMEM((256, 256), BF16),
            pltpu.VMEM((256, 256), BF16),
            dma((8,)),
            dma((4,)),
            dma((4,)),
            dma((NLON,)),
            dma((NLON,)),
            dma((8,)),
            dma((8,)),
            dma((8,)),
            dma((8,)),
            dma((NLON,)),
            dma((NLON,)),
        ],
        compiler_params=pltpu.CompilerParams(
            collective_id=0, has_side_effects=True, vmem_limit_bytes=56 * 1024 * 1024
        ),
    )(
        grid, patch_weight, spectral_one, spectral_two, fc_up, fc_down,
        const(feature_table(0)), const(feature_table(64)),
        norm_gain_one.reshape(1, C), spectral_bias, norm_gain_two.reshape(1, C),
        const(pick_table()), const(fw), const(bw), const(fh), const(bh),
    )


def solution(mesh):
    in_specs = (P(None, None, "lat", "lon"), P(), P(), P(), P(), P(), P(), P(), P())
    out_specs = P(None, "lat", "lon", None)
    return jax.shard_map(local, mesh=mesh, in_specs=in_specs, out_specs=out_specs, check_vma=False)
```

time: 407 us -> 80.8 us (0.20); the launches traced: 399 us -> 79.7 us
  local copies, waits for them, and re-layouts: 158 us -> 7.14 us
  matrix products: 76.2 us -> 0 us
  Pallas kernels: 0 us -> 72.6 us
  waiting for transfers between devices: 70.4 us -> 0 us
  blocking collectives: 35.5 us -> 0 us
  starting transfers between devices: 26.3 us -> 0 us
  other arithmetic: 18.2 us -> 0 us
  between operations: 14.6 us -> 0.01 us
    dot_general x25 -> x0, matrix products: 76.2 us -> none  [the longest x4 36.5 us: embed(): jnp.einsum('svirjq,vrqkc->sijkc', view, chosen, preferred_element_type=jn...]
    pallas_call x0 -> x1, Pallas kernels: none -> 72.6 us  [local(): pl.pallas_call(kernel, out_shape=jax.ShapeDtypeStruct((2, ROWS, COLS, C),...]
    unnamed x4 -> x0, waiting for transfers between devices: 58.5 us -> none
    reshape x14 -> x2, local copies, waits for them, and re-layouts: 45 us -> 2.54 us  [the longest x1 1.27 us: local(): norm_gain_two.reshape(1, C)]
    unnamed x74 -> x1, local copies, waits for them, and re-layouts: 40.5 us -> 2.71 us
    all_to_all x2 -> x0, blocking collectives: 35.5 us -> none  [the longest x1 18.2 us: local(): lax.all_to_all(surface.astype(jnp.bfloat16), 'lon', split_axis=0, concat_...]
    another operation x13 -> x0, local copies, waits for them, and re-layouts: 16.9 us -> none  [the longest x8 10.8 us: embed(): jnp.stack([table[2 * row_pair + row_par, 2 * col_pair + col_par] for row_...]
    all_to_all x2 -> x0, starting transfers between devices: 15.4 us -> none  [the longest x1 7.98 us: local(): lax.all_to_all(arranged, 'lon', split_axis=0, concat_axis=1, tiled=True)]
  transfers between devices with their start and end apart: 8 -> 0, of which waited for: 4 -> 0; matrix products, arithmetic and copies ran while one was open for 13% -> 0% of each run, Pallas kernels for 0% -> 0%
where the time goes in v1:
time: 80.8 us; the launch traced here: 79.7 us
  Pallas kernels  72.6 us (90%)
  local copies, waits for them, and re-layouts  7.14 us (9%)
    pallas_call x1, Pallas kernels, local(): pl.pallas_call(kernel, out_shape=jax.ShapeDtypeStruct((2, ROWS, COLS, C),...  72.6 us
    unnamed x1, local copies, waits for them, and re-layouts  2.71 us
    pallas_call x1, local copies, waits for them, and re-layouts, local(): pl.pallas_call(kernel, out_shape=jax.ShapeDtypeStruct((2, ROWS, COLS, C),...  1.9 us

profile of v1, /device:TPU:0, one launch (start us, length us, event | category | flops | bytes accessed | tf_op | source)
XLA Modules:
  0.0 79.7 jit_solution(5830450566489592763)
XLA Ops:
  0.0 1.3 %reshape.6.g1_ref = f32[1,768]{1,0:T(1,128)} reshape(f32[768]{0:T(1024)} %param.18) | data formatting | bytes 6144 | tf_op jit(solution)/shard_map/reshape | solution.py:489
  1.3 1.3 %reshape.7.g2_ref = f32[1,768]{1,0:T(1,128)} reshape(f32[768]{0:T(1024)} %param.22) | data formatting | bytes 6144 | tf_op jit(solution)/shard_map/reshape | solution.py:489
  2.5 2.7 %copy.17.grid_h = bf16[2,20,192,48]{3,2,1,0:T(8,128)(2,1)} copy(bf16[2,20,192,48]{2,3,1,0:T(8,128)(2,1)} %param.16) | data formatting | bytes 1474560 | tf_op args[0]
  5.2 72.6 %shard_map.154 = bf16[2,24,6,768]{3,2,1,0:T(8,128)(2,1)} custom-call(bf16[2,20,192,48]{3,2,1,0:T(8,128)(2,1)} %copy.17.grid_h, bf16[5120,768]{1,0:T(8,128)(2,1)} %pw_h.1, f32[2,8,96,96]{3,2,1,0:T(8,128)} %one_h.1, f32[2,8,96,96]{3,2,1,0:T(8,128)} %two_h.1, bf16[768,3072]{1,0:T(8,128)(2,1)} %up_h.1, bf16[3072,768]{1,0:T(8,128)(2,1)} %down_h.1, ...), custom_call_target="tpu_custom_call" | custom-call | tf_op jit(solution)/shard_map/pallas_call | solution.py:432
  77.8 1.9 %copy.18 = bf16[2,24,6,768]{3,1,2,0:T(8,128)(2,1)} copy(bf16[2,24,6,768]{3,2,1,0:T(8,128)(2,1)} %shard_map.154) | data formatting | bytes 884736 | tf_op jit(solution)/shard_map/pallas_call | solution.py:432

commit v2 on v1

--- a/solution.py
+++ b/solution.py
@@ -21,21 +21,19 @@
 
 
 def pick_table():
-    sel = np.zeros((64, 48), np.float32)
-    for q8 in range(8):
-        for jj in range(7):
-            lon = 8 * jj + q8 - 4
-            if 0 <= lon < 48:
-                sel[q8 * 8 + jj, lon] = 1.0
+    sel = np.zeros((192, 192), np.float32)
+    for r8 in range(8):
+        for row in range(ROWS):
+            sel[r8 * ROWS + row, 8 * row + r8] = 1.0
     return sel
 
 
-def feature_table(shift):
+def feature_table():
     table = np.zeros((4, 160, 768), np.float32)
-    for q in range(4):
+    for r in range(4):
         for v in range(NV):
-            for r8 in range(8):
-                table[q, v * 8 + r8, (r8 // 4) * 384 + shift + v * 16 + (r8 % 4) * 4 + q] = 1.0
+            for c8 in range(8):
+                table[r, v * 8 + c8, (64, 384)[c8 // 4] + v * 16 + 4 * r + c8 % 4] = 1.0
     return table
 
 
@@ -75,11 +73,11 @@
 
 
 def kernel(
-    grid_h, pw_h, one_h, two_h, up_h, down_h, elo_h, ehi_h,
+    grid_h, pw_h, one_h, two_h, up_h, down_h, tab_h,
     g1_ref, bias_ref, g2_ref, sel_ref, fw_ref, bw_ref, fh_ref, bh_ref,
     out_ref,
-    grid_v, pw_v, one_v, two_v, up_v, down_v, elo_v, ehi_v,
-    t_v, lo_v, hi_v, s_v, lhs_v, acc_v, tn_v, mid_v, nrm_v,
+    grid_v, pw_v, one_v, two_v, up_v, down_v, tab_v,
+    t_v, m_v, l_v, lhs_v, acc_v, nf_v, tn_v, nrm_v,
     ew_s, ew_r, ns_s, ns_r,
     p1_s, p1_r, p2_s, p2_r, p3_s, p3_r, p4_s, p4_r,
     z_v, v_v, w1_v, w2_v,
@@ -98,8 +96,7 @@
         return copy
 
     c_grid = load(0, grid_h, grid_v)
-    c_elo = load(1, elo_h, elo_v)
-    c_ehi = load(2, ehi_h, ehi_v)
+    c_tab = load(1, tab_h, tab_v)
     c_pw = load(3, pw_h, pw_v)
     c_one = load(4, one_h.at[:, n], one_v)
     c_two = load(5, two_h.at[:, n], two_v)
@@ -125,36 +122,35 @@
 
     lax.fori_loop(0, 6, greet_lat, 0)
 
+    nf_v[:, :, 144:] = jnp.zeros((6, 2, 48, 128), F32)
+    ns_s[...] = jnp.zeros_like(ns_s)
     c_grid.wait()
-
-    def turn(it, _):
-        smp = it // 12
-        rp = it % 12
-        block = grid_v[smp, :, pl.ds(pl.multiple_of(16 * rp, 16), 16), :]
-        block = block.astype(F32).reshape(NV, 2, 8, 48)
-        turned = []
-        for half in range(2):
-            x = block[:, half].reshape(NV * 8, 48).astype(BF16)
-            turned.append(
-                lax.dot_general(
+    for smp in range(2):
+        for lp in range(3):
+            block = grid_v[smp, :, 16 * lp : 16 * lp + 16, :]
+            block = block.astype(F32).reshape(NV, 2, 8, 192)
+            for half in range(2):
+                x = block[:, half].reshape(NV * 8, 192).astype(BF16)
+                turned = lax.dot_general(
                     sel_ref[...], x, (((1,), (1,)), ((), ())), preferred_element_type=F32
                 )
-            )
-        for q8 in range(8):
-            pair = jnp.concatenate([t[8 * q8 : 8 * q8 + 8] for t in turned], axis=0)
-            t_v[q8, pl.ds(pl.multiple_of(16 * it, 16), 16), :] = pair.astype(BF16)
-        return 0
-
-    lax.fori_loop(0, 24, turn, 0)
-
-    c_elo.wait()
-    c_ehi.wait()
-    for part, (table, total) in enumerate(((elo_v, lo_v), (ehi_v, hi_v))):
-        value = dot(t_v[4 * part], table[0])
-        for i in range(1, 4):
-            value = value + dot(t_v[4 * part + i], table[i])
+                first = (6 * smp + 2 * lp + half) * ROWS
+                for r8 in range(8):
+                    t_v[r8, first : first + ROWS, :] = turned[ROWS * r8 : ROWS * r8 + ROWS]
+
+    c_tab.wait()
+    for half in range(2):
+        value = dot(t_v[4 * half].astype(BF16), tab_v[0])
+        for r in range(1, 4):
+            value = value + dot(t_v[4 * half + r].astype(BF16), tab_v[r])
         for tile in range(6):
-            total[tile] = value[:, 128 * tile : 128 * tile + 128]
+            part = value[:, 128 * tile : 128 * tile + 128].reshape(2, COLS, ROWS, 128)
+            for smp in range(2):
+                m_v[half, tile, smp, 1 : 1 + COLS] = part[smp]
+                if tile >= 3:
+                    ew_s[0, half, tile - 3, smp] = part[smp, COLS - 1].astype(BF16)
+                else:
+                    ew_s[1, half, tile, smp] = part[smp, 0].astype(BF16)
 
     pl.semaphore_wait(barrier, NLON - 1 + 6)
 
@@ -164,10 +160,6 @@
             device_id=dev, device_id_type=MESH,
         )
 
-    for tile in range(6):
-        cols = slice(128 * tile, 128 * tile + 128)
-        ew_s[0, :, cols] = lo_v[tile, pl.ds(6, 48, stride=8), :].astype(BF16)
-        ew_s[1, :, cols] = hi_v[tile, pl.ds(0, 48, stride=8), :].astype(BF16)
     east = remote(ew_s.at[0], ew_r.at[0], halo_ss.at[0], halo_rs.at[0], (a, lax.rem(b + 1, NLON)))
     west = remote(
         ew_s.at[1], ew_r.at[1], halo_ss.at[1], halo_rs.at[1], (a, lax.rem(b + NLON - 1, NLON))
@@ -176,19 +168,34 @@
     west.start()
     east.wait_recv()
     west.wait_recv()
-    for tile in range(6):
-        cols = slice(128 * tile, 128 * tile + 128)
-        lo_v[tile, pl.ds(0, 48, stride=8), :] = ew_r[0, :, cols].astype(F32)
-        hi_v[tile, pl.ds(6, 48, stride=8), :] = ew_r[1, :, cols].astype(F32)
     for half in range(2):
-        lo = [lo_v[3 * half + tile] for tile in range(3)]
-        hi = [hi_v[3 * half + tile] for tile in range(3)]
-        for tile, value in enumerate((lo[0], lo[1], lo[2] + hi[0], hi[1], hi[2])):
-            both = value.reshape(2, ROWS, 8, 128)
+        for tile in range(3):
             for smp in range(2):
-                s_v[half, smp, 1 : 1 + ROWS, :, 128 * tile : 128 * tile + 128] = both[smp]
-    ns_s[0] = s_v[1, :, ROWS].astype(BF16)
-    ns_s[1] = s_v[0, :, 1].astype(BF16)
+                m_v[half, 3 + tile, smp, 0] = ew_r[0, half, tile, smp].astype(F32)
+                m_v[half, tile, smp, COLS + 1] = ew_r[1, half, tile, smp].astype(F32)
+
+    def patch_tile(half, tile, smp):
+        lane, slot = ((3, 0), (4, 0), (5, 0), (1, 1), (2, 1), (3, 1), (4, 1), (5, 1), (1, 2), (2, 2))[tile]
+        value = m_v[half, lane, smp, slot : slot + COLS]
+        if tile in (2, 7):
+            value = value + m_v[half, 0, smp, slot + 1 : slot + 1 + COLS]
+        return value
+
+    for half in (1, 0):
+        for tile in range(10):
+            for smp in range(2):
+                value = patch_tile(half, tile, smp)
+                for j in range(COLS):
+                    first = 40 * (COLS * smp + j) + 8
+                    l_v[half, tile, first : first + ROWS, :] = value[j]
+                lhs_v[half, 144 * smp : 144 * smp + 144, 128 * tile : 128 * tile + 128] = (
+                    value.reshape(144, 128).astype(BF16)
+                )
+            cols = slice(128 * tile, 128 * tile + 128)
+            if half == 1:
+                ns_s[0, :12, cols] = l_v[1, tile, pl.ds(31, 12, stride=40), :].astype(BF16)
+            else:
+                ns_s[1, :12, cols] = l_v[0, tile, pl.ds(8, 12, stride=40), :].astype(BF16)
     south = remote(ns_s.at[0], ns_r.at[0], halo_ss.at[2], halo_rs.at[2], (lax.rem(a + 1, NLAT), b))
     north = remote(
         ns_s.at[1], ns_r.at[1], halo_ss.at[3], halo_rs.at[3], (lax.rem(a + NLAT - 1, NLAT), b)
@@ -197,52 +204,67 @@
     north.start()
 
     c_pw.wait()
-    for count, (off, half, first) in enumerate(((1, 0, 1), (2, 1, 1), (0, 1, 0), (3, 0, 2))):
+    for count, (off, half) in enumerate(((1, 0), (2, 1), (0, 1), (3, 0))):
         if count == 2:
             south.wait_recv()
             north.wait_recv()
-            s_v[1, :, 0] = jnp.where(a > 0, ns_r[0].astype(F32), 0.0)
-            s_v[0, :, ROWS + 1] = jnp.where(a < NLAT - 1, ns_r[1].astype(F32), 0.0)
-        for smp in range(2):
-            x = s_v[half, smp, first : first + ROWS]
-            rows = slice(192 * smp, 192 * smp + 192)
-            lhs_v[rows, :640] = x.reshape(192, 640).astype(BF16)
-            shifted = jnp.concatenate([x[:, 1:], x[:, :1]], axis=1)
-            lhs_v[rows, 640:] = shifted.reshape(192, 640).astype(BF16)
+            for tile in range(10):
+                cols = slice(128 * tile, 128 * tile + 128)
+                l_v[1, tile, pl.ds(7, 12, stride=40), :] = jnp.where(
+                    a > 0, ns_r[0, :12, cols].astype(F32), 0.0
+                )
+                l_v[0, tile, pl.ds(32, 12, stride=40), :] = jnp.where(
+                    a < NLAT - 1, ns_r[1, :12, cols].astype(F32), 0.0
+                )
+        if count >= 2:
+            lead = 7 if half == 1 else 9
+            for tile in range(10):
+                rows = [l_v[half, tile, 40 * m + lead : 40 * m + lead + ROWS, :] for m in range(12)]
+                lhs_v[half, :, 128 * tile : 128 * tile + 128] = jnp.concatenate(
+                    rows, axis=0
+                ).astype(BF16)
         for tile in range(3):
             cols = slice(256 * tile, 256 * tile + 256)
-            value = dot(lhs_v[...], pw_v[1280 * off : 1280 * off + 1280, cols])
+            value = dot(lhs_v[half], pw_v[1280 * off : 1280 * off + 1280, cols])
             if count == 0:
                 acc_v[:, cols] = value
             else:
                 acc_v[:, cols] += value
 
-    def send_tokens(c, _):
-        rows = pl.ds(pl.multiple_of(c * 96, 96), 96)
+    for smp in range(2):
+        rows = slice(144 * smp, 144 * smp + 144)
         tok = acc_v[rows, :].astype(BF16).astype(F32)
-        normed = norm(tok, g1_ref[...]).astype(BF16).astype(F32)
+        normed = norm(tok, g1_ref[...].reshape(1, C)).astype(BF16).astype(F32)
         tn_v[rows, :] = tok + normed
-        planes = normed.reshape(ROW12, 8, C)
-        smp = c // 2
-        part = c % 2
-        for blk in range(NB):
-            msg = jnp.concatenate(
-                [planes[i][:, BS * blk : BS * blk + BS] for i in range(ROW12)], axis=1
-            )
-            dest = part * 16 + smp * 8 + blk
-            p1_s[dest] = msg.astype(BF16)
-
-            @pl.when(dest != b)
-            def _():
-                remote(p1_s.at[dest], p1_r.at[b], s1.at[dest], r1.at[b], (a, dest)).start()
-
-            @pl.when(dest == b)
-            def _():
-                p1_r[b] = msg.astype(BF16)
-
-        return 0
-
-    lax.fori_loop(0, 4, send_tokens, 0)
+        for tile in range(6):
+            nf_v[tile, smp, :144] = normed[:, 128 * tile : 128 * tile + 128]
+
+        def send_tokens(part, _):
+            planes = [
+                jnp.concatenate(
+                    [nf_v[t, smp, pl.ds(part * ROW12 + i, 8, stride=ROWS), :] for t in range(6)],
+                    axis=1,
+                )
+                for i in range(ROW12)
+            ]
+            for blk in range(NB):
+                msg = jnp.concatenate(
+                    [plane[:, BS * blk : BS * blk + BS] for plane in planes], axis=1
+                )
+                dest = part * 16 + smp * 8 + blk
+                p1_s[dest] = msg.astype(BF16)
+
+                @pl.when(dest != b)
+                def _():
+                    remote(p1_s.at[dest], p1_r.at[b], s1.at[dest], r1.at[b], (a, dest)).start()
+
+                @pl.when(dest == b)
+                def _():
+                    p1_r[b] = msg.astype(BF16)
+
+            return 0
+
+        lax.fori_loop(0, 2, send_tokens, 0)
 
     c_one.wait()
     c_two.wait()
@@ -366,22 +388,24 @@
 
     lax.fori_loop(1, NLON, wait4, 0)
 
-    def join(c, _):
-        rows = pl.ds(pl.multiple_of(c * 96, 96), 96)
-        smp = c // 2
-        part = c % 2
-        msgs = [p4_r[part * 16 + smp * 8 + blk].astype(F32) for blk in range(NB)]
-        planes = [
-            jnp.concatenate([m[:, BS * i : BS * i + BS] for m in msgs], axis=1)
-            for i in range(ROW12)
-        ]
-        middle = jnp.concatenate(planes, axis=0) + tn_v[rows, :]
-        middle = middle.astype(BF16).astype(F32)
-        mid_v[rows, :] = middle
-        nrm_v[rows, :] = norm(middle, g2_ref[...]).astype(BF16)
-        return 0
-
-    lax.fori_loop(0, 4, join, 0)
+    for smp in range(2):
+
+        def join(part, _):
+            msgs = [p4_r[part * 16 + smp * 8 + blk].astype(F32) for blk in range(NB)]
+            for i in range(ROW12):
+                plane = jnp.concatenate([m[:, BS * i : BS * i + BS] for m in msgs], axis=1)
+                for tile in range(6):
+                    nf_v[tile, smp, pl.ds(part * ROW12 + i, 8, stride=ROWS), :] = plane[
+                        :, 128 * tile : 128 * tile + 128
+                    ]
+            return 0
+
+        lax.fori_loop(0, 2, join, 0)
+        rows = slice(144 * smp, 144 * smp + 144)
+        field = jnp.concatenate([nf_v[tile, smp, :144] for tile in range(6)], axis=1)
+        middle = (field + tn_v[rows, :]).astype(BF16).astype(F32)
+        acc_v[rows, :] = middle
+        nrm_v[rows, :] = norm(middle, g2_ref[...].reshape(1, C)).astype(BF16)
 
     c_up.wait()
     c_down.wait()
@@ -390,14 +414,11 @@
         cols = pl.ds(pl.multiple_of(step * 256, 256), 256)
         hidden = dot(nrm_v[...], up_v[:, cols])
         hidden = 0.5 * hidden * (1.0 + lax.erf(hidden * (1.0 / math.sqrt(2.0))))
-        mid_v[...] += dot(hidden.astype(BF16), down_v[cols, :])
+        acc_v[...] += dot(hidden.astype(BF16), down_v[cols, :])
         return 0
 
     lax.fori_loop(0, HID // 256, mlp, 0)
-
-    for smp in range(2):
-        rows = slice(192 * smp, 192 * smp + 192)
-        out_ref[smp] = mid_v[rows, :].reshape(ROWS, 8, C)[:, :COLS].astype(BF16)
+    out_ref[...] = acc_v[...].reshape(2, COLS, ROWS, C).astype(BF16)
 
     for copy in (east, west, south, north):
         copy.wait_send()
@@ -429,33 +450,31 @@
     any_spec = pl.BlockSpec(memory_space=pl.ANY)
     vmem = pl.BlockSpec(memory_space=pltpu.VMEM)
     dma = pltpu.SemaphoreType.DMA
-    return pl.pallas_call(
+    out = pl.pallas_call(
         kernel,
-        out_shape=jax.ShapeDtypeStruct((2, ROWS, COLS, C), BF16),
-        in_specs=[any_spec] * 8 + [vmem] * 8,
+        out_shape=jax.ShapeDtypeStruct((2, COLS, ROWS, C), BF16),
+        in_specs=[any_spec] * 7 + [vmem] * 8,
         out_specs=vmem,
         scratch_shapes=[
-            pltpu.VMEM((2, NV, 192, 48), BF16),
+            pltpu.VMEM((2, NV, 48, 192), BF16),
             pltpu.VMEM((5120, C), BF16),
             pltpu.VMEM((2, BS, BS), F32),
             pltpu.VMEM((2, BS, BS), F32),
             pltpu.VMEM((C, HID), BF16),
             pltpu.VMEM((HID, C), BF16),
             pltpu.VMEM((4, 160, 768), BF16),
-            pltpu.VMEM((4, 160, 768), BF16),
-            pltpu.VMEM((8, 384, 160), BF16),
-            pltpu.VMEM((6, 384, 128), F32),
-            pltpu.VMEM((6, 384, 128), F32),
-            pltpu.VMEM((2, 2, ROWS + 2, 8, 640), F32),
-            pltpu.VMEM((384, 1280), BF16),
-            pltpu.VMEM((384, C), F32),
-            pltpu.VMEM((384, C), F32),
-            pltpu.VMEM((384, C), F32),
-            pltpu.VMEM((384, C), BF16),
-            pltpu.VMEM((2, 48, 768), BF16),
-            pltpu.VMEM((2, 48, 768), BF16),
-            pltpu.VMEM((2, 2, 8, 640), BF16),
-            pltpu.VMEM((2, 2, 8, 640), BF16),
+            pltpu.VMEM((8, 288, 160), F32),
+            pltpu.VMEM((2, 6, 2, COLS + 2, ROWS, 128), F32),
+            pltpu.VMEM((2, 10, 480, 128), F32),
+            pltpu.VMEM((2, 288, 1280), BF16),
+            pltpu.VMEM((288, C), F32),
+            pltpu.VMEM((6, 2, 192, 128), F32),
+            pltpu.VMEM((288, C), F32),
+            pltpu.VMEM((288, C), BF16),
+            pltpu.VMEM((2, 2, 3, 2, ROWS, 128), BF16),
+            pltpu.VMEM((2, 2, 3, 2, ROWS, 128), BF16),
+            pltpu.VMEM((2, 16, 1280), BF16),
+            pltpu.VMEM((2, 16, 1280), BF16),
             pltpu.VMEM((NLON, 8, MSG), BF16),
             pltpu.VMEM((NLON, 8, MSG), BF16),
             pltpu.VMEM((8, 16, MSG), BF16),
@@ -484,11 +503,12 @@
             collective_id=0, has_side_effects=True, vmem_limit_bytes=56 * 1024 * 1024
         ),
     )(
-        grid, patch_weight, spectral_one, spectral_two, fc_up, fc_down,
-        const(feature_table(0)), const(feature_table(64)),
-        norm_gain_one.reshape(1, C), spectral_bias, norm_gain_two.reshape(1, C),
+        grid.transpose(0, 1, 3, 2), patch_weight, spectral_one, spectral_two, fc_up, fc_down,
+        const(feature_table()),
+        norm_gain_one, spectral_bias, norm_gain_two,
         const(pick_table()), const(fw), const(bw), const(fh), const(bh),
     )
+    return out.transpose(0, 2, 1, 3)
 
 
 def solution(mesh):

time: 80.8 us -> 68.8 us (0.85)
  Pallas kernels: 72.6 us -> 66 us
  local copies, waits for them, and re-layouts: 7.14 us -> 1.8 us
    pallas_call x1, Pallas kernels: 72.6 us -> 66 us  [local(): pl.pallas_call(kernel, out_shape=jax.ShapeDtypeStruct((2, COLS, ROWS, C),...]
    reshape x2 -> x0, local copies, waits for them, and re-layouts: 2.54 us -> none  [the longest x1 1.27 us: local(): norm_gain_two.reshape(1, C)]
    pallas_call x1 -> x0, local copies, waits for them, and re-layouts: 1.9 us -> none  [local(): pl.pallas_call(kernel, out_shape=jax.ShapeDtypeStruct((2, ROWS, COLS, C),...]
    unnamed x1, local copies, waits for them, and re-layouts: 2.71 us -> 1.8 us
where the time goes in v2:
time: 68.8 us; the launch traced here: 67.8 us
  Pallas kernels  66 us (96%)
  local copies, waits for them, and re-layouts  1.8 us (3%)
    pallas_call x1, Pallas kernels, local(): pl.pallas_call(kernel, out_shape=jax.ShapeDtypeStruct((2, COLS, ROWS, C),...  66 us
    unnamed x1, local copies, waits for them, and re-layouts  1.8 us

profile of v2, /device:TPU:0, one launch (start us, length us, event | category | flops | bytes accessed | tf_op | source)
XLA Modules:
  0.0 67.8 jit_solution(8587662471328073354)
XLA Ops:
  0.0 66.0 %shard_map.145 = bf16[2,6,24,768]{3,2,1,0:T(8,128)(2,1)} custom-call(bf16[2,20,48,192]{3,2,1,0:T(8,128)(2,1)} %bitcast.3, bf16[5120,768]{1,0:T(8,128)(2,1)} %pw_h.1, f32[2,8,96,96]{3,2,1,0:T(8,128)} %one_h.1, f32[2,8,96,96]{3,2,1,0:T(8,128)} %two_h.1, bf16[768,3072]{1,0:T(8,128)(2,1)} %up_h.1, bf16[3072,768]{1,0:T(8,128)(2,1)} %down_h.1, ...), custom_call_target="tpu_custom_call" | custom-call | tf_op jit(solution)/shard_map/pallas_call | solution.py:453
  66.0 1.8 %copy.17 = bf16[2,24,6,768]{3,1,2,0:T(8,128)(2,1)} copy(bf16[2,24,6,768]{3,1,2,0:T(8,128)(2,1)} %bitcast.2) | data formatting | bytes 884736

commit v3 on v2

--- a/solution.py
+++ b/solution.py
@@ -77,7 +77,7 @@
     g1_ref, bias_ref, g2_ref, sel_ref, fw_ref, bw_ref, fh_ref, bh_ref,
     out_ref,
     grid_v, pw_v, one_v, two_v, up_v, down_v, tab_v,
-    t_v, m_v, l_v, lhs_v, acc_v, nf_v, tn_v, nrm_v,
+    t_v, m_v, lhs_v, q0_v, q3_v, tot_v, acc_v, nf_v, tn_v, nrm_v,
     ew_s, ew_r, ns_s, ns_r,
     p1_s, p1_r, p2_s, p2_r, p3_s, p3_r, p4_s, p4_r,
     z_v, v_v, w1_v, w2_v,
@@ -87,8 +87,12 @@
     b = lax.axis_index("lon")
     q = b // 16
     p = b % 16
-    n = b % 8
+    row_y = p // 4
+    row_z = p % 4
+    mine = (row_y + row_z) % 2
+    n = 2 * row_y + row_z // 2
     g = 2 * a + q
+    ways = [(da, db) for da in (1, 3) for db in (1, NLON - 1)]
 
     def load(index, src, dst):
         copy = pltpu.make_async_copy(src, dst, lsem.at[index])
@@ -121,9 +125,16 @@
         return 0
 
     lax.fori_loop(0, 6, greet_lat, 0)
+    for da, db in ways:
+        corner = (lax.rem(a + da, NLAT), lax.rem(b + db, NLON))
+        pl.semaphore_signal(barrier, inc=1, device_id=corner, device_id_type=MESH)
 
     nf_v[:, :, 144:] = jnp.zeros((6, 2, 48, 128), F32)
-    ns_s[...] = jnp.zeros_like(ns_s)
+    for slots in (slice(0, 2), slice(8, 10)):
+        m_v[:, :, :, slots] = jnp.zeros((2, 6, 2, 2, ROWS, 128), F32)
+    for tile in range(6):
+        q0_v[tile, pl.ds(0, 16, stride=32), :] = jnp.zeros((16, 128), F32)
+        q3_v[tile, pl.ds(31, 16, stride=32), :] = jnp.zeros((16, 128), F32)
     c_grid.wait()
     for smp in range(2):
         for lp in range(3):
@@ -146,13 +157,53 @@
         for tile in range(6):
             part = value[:, 128 * tile : 128 * tile + 128].reshape(2, COLS, ROWS, 128)
             for smp in range(2):
-                m_v[half, tile, smp, 1 : 1 + COLS] = part[smp]
-                if tile >= 3:
-                    ew_s[0, half, tile - 3, smp] = part[smp, COLS - 1].astype(BF16)
-                else:
-                    ew_s[1, half, tile, smp] = part[smp, 0].astype(BF16)
-
-    pl.semaphore_wait(barrier, NLON - 1 + 6)
+                m_v[half, tile, smp, 2 : 2 + COLS] = part[smp]
+
+    for half in range(2):
+        for tile in range(10):
+            lane, slot = (
+                (3, 0), (4, 0), (5, 0), (1, 1), (2, 1), (3, 1), (4, 1), (5, 1), (1, 2), (2, 2)
+            )[tile]
+            for smp in range(2):
+                value = m_v[half, lane, smp, slot : slot + 8]
+                if tile in (2, 7):
+                    value = value + m_v[half, 0, smp, slot + 1 : slot + 9]
+                lhs_v[half, 192 * smp : 192 * smp + 192, 128 * tile : 128 * tile + 128] = (
+                    value.reshape(192, 128).astype(BF16)
+                )
+
+    c_pw.wait()
+    for pair in range(3):
+        cols = slice(256 * pair, 256 * pair + 256)
+        weight = lambda off: pw_v[1280 * off : 1280 * off + 1280, cols]
+        above = dot(lhs_v[1], weight(0))
+        below = dot(lhs_v[0], weight(3))
+        for lane in range(2):
+            tile = 2 * pair + lane
+            lanes = slice(128 * lane, 128 * lane + 128)
+            for m in range(16):
+                rows = slice(ROWS * m, ROWS * m + ROWS)
+                q0_v[tile, 32 * m + 1 : 32 * m + 1 + ROWS, :] = above[rows, lanes]
+                q3_v[tile, 32 * m + 7 : 32 * m + 7 + ROWS, :] = below[rows, lanes]
+        value = dot(lhs_v[0], weight(1)) + dot(lhs_v[1], weight(2))
+        for lane in range(2):
+            tile = 2 * pair + lane
+            lanes = slice(128 * lane, 128 * lane + 128)
+            shifted = (
+                q0_v[tile].reshape(16, 32, 128)[:, :ROWS] + q3_v[tile].reshape(16, 32, 128)[:, 8:]
+            )
+            tot_v[tile] = value[:, lanes] + shifted.reshape(384, 128)
+
+    for tile in range(6):
+        cols = slice(128 * tile, 128 * tile + 128)
+        for smp in range(2):
+            for way, slot in ((0, 7), (1, 0)):
+                first = ROWS * (8 * smp + slot)
+                ew_s[way, smp, :, cols] = tot_v[tile, first : first + ROWS, :].astype(BF16)
+        ns_s[0, :, cols] = q0_v[tile, pl.ds(ROWS, 16, stride=32), :].astype(BF16)
+        ns_s[1, :, cols] = q3_v[tile, pl.ds(7, 16, stride=32), :].astype(BF16)
+
+    pl.semaphore_wait(barrier, NLON - 1 + 6 + 4)
 
     def remote(src, dst, ssem, rsem, dev):
         return pltpu.make_async_remote_copy(
@@ -160,86 +211,59 @@
             device_id=dev, device_id_type=MESH,
         )
 
-    east = remote(ew_s.at[0], ew_r.at[0], halo_ss.at[0], halo_rs.at[0], (a, lax.rem(b + 1, NLON)))
-    west = remote(
-        ew_s.at[1], ew_r.at[1], halo_ss.at[1], halo_rs.at[1], (a, lax.rem(b + NLON - 1, NLON))
-    )
-    east.start()
-    west.start()
-    east.wait_recv()
-    west.wait_recv()
-    for half in range(2):
-        for tile in range(3):
-            for smp in range(2):
-                m_v[half, 3 + tile, smp, 0] = ew_r[0, half, tile, smp].astype(F32)
-                m_v[half, tile, smp, COLS + 1] = ew_r[1, half, tile, smp].astype(F32)
-
-    def patch_tile(half, tile, smp):
-        lane, slot = ((3, 0), (4, 0), (5, 0), (1, 1), (2, 1), (3, 1), (4, 1), (5, 1), (1, 2), (2, 2))[tile]
-        value = m_v[half, lane, smp, slot : slot + COLS]
-        if tile in (2, 7):
-            value = value + m_v[half, 0, smp, slot + 1 : slot + 1 + COLS]
-        return value
-
-    for half in (1, 0):
-        for tile in range(10):
-            for smp in range(2):
-                value = patch_tile(half, tile, smp)
-                for j in range(COLS):
-                    first = 40 * (COLS * smp + j) + 8
-                    l_v[half, tile, first : first + ROWS, :] = value[j]
-                lhs_v[half, 144 * smp : 144 * smp + 144, 128 * tile : 128 * tile + 128] = (
-                    value.reshape(144, 128).astype(BF16)
-                )
-            cols = slice(128 * tile, 128 * tile + 128)
-            if half == 1:
-                ns_s[0, :12, cols] = l_v[1, tile, pl.ds(31, 12, stride=40), :].astype(BF16)
-            else:
-                ns_s[1, :12, cols] = l_v[0, tile, pl.ds(8, 12, stride=40), :].astype(BF16)
-    south = remote(ns_s.at[0], ns_r.at[0], halo_ss.at[2], halo_rs.at[2], (lax.rem(a + 1, NLAT), b))
-    north = remote(
-        ns_s.at[1], ns_r.at[1], halo_ss.at[3], halo_rs.at[3], (lax.rem(a + NLAT - 1, NLAT), b)
-    )
-    south.start()
-    north.start()
-
-    c_pw.wait()
-    for count, (off, half) in enumerate(((1, 0), (2, 1), (0, 1), (3, 0))):
-        if count == 2:
-            south.wait_recv()
-            north.wait_recv()
-            for tile in range(10):
-                cols = slice(128 * tile, 128 * tile + 128)
-                l_v[1, tile, pl.ds(7, 12, stride=40), :] = jnp.where(
-                    a > 0, ns_r[0, :12, cols].astype(F32), 0.0
-                )
-                l_v[0, tile, pl.ds(32, 12, stride=40), :] = jnp.where(
-                    a < NLAT - 1, ns_r[1, :12, cols].astype(F32), 0.0
-                )
-        if count >= 2:
-            lead = 7 if half == 1 else 9
-            for tile in range(10):
-                rows = [l_v[half, tile, 40 * m + lead : 40 * m + lead + ROWS, :] for m in range(12)]
-                lhs_v[half, :, 128 * tile : 128 * tile + 128] = jnp.concatenate(
-                    rows, axis=0
-                ).astype(BF16)
-        for tile in range(3):
-            cols = slice(256 * tile, 256 * tile + 256)
-            value = dot(lhs_v[half], pw_v[1280 * off : 1280 * off + 1280, cols])
-            if count == 0:
-                acc_v[:, cols] = value
-            else:
-                acc_v[:, cols] += value
+    halos = []
+    for src, da in ((0, 1), (1, 3)):
+        for side, db in enumerate((0, 1, NLON - 1)):
+            slot = 3 * src + side
+            halos.append((ns_s.at[src], ns_r.at[slot], 2 + slot, da, db))
+    for src, db in ((0, 1), (1, NLON - 1)):
+        halos.append((ew_s.at[src], ew_r.at[src], src, 0, db))
+    halos = [
+        remote(
+            src, dst, halo_ss.at[sem], halo_rs.at[sem],
+            (lax.rem(a + da, NLAT), lax.rem(b + db, NLON)),
+        )
+        for src, dst, sem, da, db in halos
+    ]
+    for copy in halos:
+        copy.start()
+    for copy in halos:
+        copy.wait_recv()
+
+    slot_ids = lax.broadcasted_iota(jnp.int32, (2, 8, 128), 1)
+
+    def edge_row(first, cols):
+        straight, west, east = [
+            ns_r[first + k, :, cols].astype(F32).reshape(2, 8, 128) for k in range(3)
+        ]
+        west = jnp.concatenate([west[:, 6:], west[:, :6]], axis=1)
+        east = jnp.concatenate([east[:, 2:], east[:, :2]], axis=1)
+        straight = straight + jnp.where(slot_ids == 1, west, 0.0)
+        return (straight + jnp.where(slot_ids == 6, east, 0.0)).reshape(16, 128)
+
+    for tile in range(6):
+        cols = slice(128 * tile, 128 * tile + 128)
+        for smp in range(2):
+            for way, slot in ((0, 1), (1, 6)):
+                first = ROWS * (8 * smp + slot)
+                tot_v[tile, first : first + ROWS, :] += ew_r[way, smp, :, cols].astype(F32)
+        top, bottom = pl.ds(0, 16, stride=ROWS), pl.ds(ROWS - 1, 16, stride=ROWS)
+        tot_v[tile, top, :] += jnp.where(a > 0, edge_row(0, cols), 0.0)
+        tot_v[tile, bottom, :] += jnp.where(a < NLAT - 1, edge_row(3, cols), 0.0)
+
+    def owner(part, smp, blk):
+        return part * 16 + (blk // 2) * 4 + (blk % 2) * 2 + (smp + blk // 2) % 2
 
     for smp in range(2):
         rows = slice(144 * smp, 144 * smp + 144)
-        tok = acc_v[rows, :].astype(BF16).astype(F32)
+        first = ROWS * (8 * smp + 1)
+        tok = jnp.concatenate([tot_v[t, first : first + 144, :] for t in range(6)], axis=1)
+        tok = tok.astype(BF16).astype(F32)
         normed = norm(tok, g1_ref[...].reshape(1, C)).astype(BF16).astype(F32)
         tn_v[rows, :] = tok + normed
         for tile in range(6):
             nf_v[tile, smp, :144] = normed[:, 128 * tile : 128 * tile + 128]
-
-        def send_tokens(part, _):
+        for part in range(2):
             planes = [
                 jnp.concatenate(
                     [nf_v[t, smp, pl.ds(part * ROW12 + i, 8, stride=ROWS), :] for t in range(6)],
@@ -251,20 +275,25 @@
                 msg = jnp.concatenate(
                     [plane[:, BS * blk : BS * blk + BS] for plane in planes], axis=1
                 )
-                dest = part * 16 + smp * 8 + blk
-                p1_s[dest] = msg.astype(BF16)
-
-                @pl.when(dest != b)
-                def _():
-                    remote(p1_s.at[dest], p1_r.at[b], s1.at[dest], r1.at[b], (a, dest)).start()
-
-                @pl.when(dest == b)
-                def _():
-                    p1_r[b] = msg.astype(BF16)
-
-            return 0
-
-        lax.fori_loop(0, 2, send_tokens, 0)
+                p1_s[owner(part, smp, blk)] = msg.astype(BF16)
+        odd = (smp + mine) % 2
+        for dx in (1, 0):
+            for dy in (2, 1, 3, 0):
+                for dz in (2, 0):
+                    dest = (
+                        ((q + dx) % 2) * 16 + ((row_y + dy) % 4) * 4 + (row_z + dz + (odd + dy) % 2) % 4
+                    )
+
+                    def send(dest=dest):
+                        remote(
+                            p1_s.at[dest], p1_r.at[b], s1.at[dest], r1.at[b], (a, dest)
+                        ).start()
+
+                    if (dx, dy, dz) == (0, 0, 0):
+                        pl.when(odd == 1)(send)
+                    else:
+                        send()
+    p1_r[b] = p1_s[b]
 
     c_one.wait()
     c_two.wait()
@@ -373,12 +402,11 @@
     field = dot(bw_ref[...], p3_r[...].reshape(128, MSG))
     p4_s[...] = field.reshape(NLON, 8, MSG).astype(BF16)
 
-    def send4(d, _):
-        dest = lax.rem(b + d, NLON)
+    steps = [(dx, dy, dz) for dx in range(2) for dy in range(4) for dz in range(4)]
+    steps.sort(key=lambda t: -(t[0] + min(t[1], 4 - t[1]) + min(t[2], 4 - t[2])))
+    for dx, dy, dz in steps[:-1]:
+        dest = ((q + dx) % 2) * 16 + ((row_y + dy) % 4) * 4 + (row_z + dz) % 4
         remote(p4_s.at[dest], p4_r.at[b], s4.at[dest], r4.at[b], (a, dest)).start()
-        return 0
-
-    lax.fori_loop(1, NLON, send4, 0)
     p4_r[b] = p4_s[b]
 
     def wait4(d, _):
@@ -391,7 +419,7 @@
     for smp in range(2):
 
         def join(part, _):
-            msgs = [p4_r[part * 16 + smp * 8 + blk].astype(F32) for blk in range(NB)]
+            msgs = [p4_r[owner(part, smp, blk)].astype(F32) for blk in range(NB)]
             for i in range(ROW12):
                 plane = jnp.concatenate([m[:, BS * i : BS * i + BS] for m in msgs], axis=1)
                 for tile in range(6):
@@ -420,7 +448,7 @@
     lax.fori_loop(0, HID // 256, mlp, 0)
     out_ref[...] = acc_v[...].reshape(2, COLS, ROWS, C).astype(BF16)
 
-    for copy in (east, west, south, north):
+    for copy in halos:
         copy.wait_send()
 
     def drain_lon(d, _):
@@ -464,17 +492,19 @@
             pltpu.VMEM((HID, C), BF16),
             pltpu.VMEM((4, 160, 768), BF16),
             pltpu.VMEM((8, 288, 160), F32),
-            pltpu.VMEM((2, 6, 2, COLS + 2, ROWS, 128), F32),
-            pltpu.VMEM((2, 10, 480, 128), F32),
-            pltpu.VMEM((2, 288, 1280), BF16),
+            pltpu.VMEM((2, 6, 2, 10, ROWS, 128), F32),
+            pltpu.VMEM((2, 384, 1280), BF16),
+            pltpu.VMEM((6, 512, 128), F32),
+            pltpu.VMEM((6, 512, 128), F32),
+            pltpu.VMEM((6, 384, 128), F32),
             pltpu.VMEM((288, C), F32),
             pltpu.VMEM((6, 2, 192, 128), F32),
             pltpu.VMEM((288, C), F32),
             pltpu.VMEM((288, C), BF16),
-            pltpu.VMEM((2, 2, 3, 2, ROWS, 128), BF16),
-            pltpu.VMEM((2, 2, 3, 2, ROWS, 128), BF16),
-            pltpu.VMEM((2, 16, 1280), BF16),
-            pltpu.VMEM((2, 16, 1280), BF16),
+            pltpu.VMEM((2, 2, ROWS, C), BF16),
+            pltpu.VMEM((2, 2, ROWS, C), BF16),
+            pltpu.VMEM((2, 16, C), BF16),
+            pltpu.VMEM((6, 16, C), BF16),
             pltpu.VMEM((NLON, 8, MSG), BF16),
             pltpu.VMEM((NLON, 8, MSG), BF16),
             pltpu.VMEM((8, 16, MSG), BF16),
@@ -488,8 +518,8 @@
             pltpu.VMEM((256, 256), BF16),
             pltpu.VMEM((256, 256), BF16),
             dma((8,)),
-            dma((4,)),
-            dma((4,)),
+            dma((8,)),
+            dma((8,)),
             dma((NLON,)),
             dma((NLON,)),
             dma((8,)),

time: 68.8 us -> 67.5 us (0.981)
  Pallas kernels: 66 us -> 64.6 us
    pallas_call x1, Pallas kernels: 66 us -> 64.6 us  [local(): pl.pallas_call(kernel, out_shape=jax.ShapeDtypeStruct((2, COLS, ROWS, C),...]
where the time goes in v3:
time: 67.5 us; the launch traced here: 66.5 us
  Pallas kernels  64.6 us (96%)
  local copies, waits for them, and re-layouts  1.8 us (3%)
    pallas_call x1, Pallas kernels, local(): pl.pallas_call(kernel, out_shape=jax.ShapeDtypeStruct((2, COLS, ROWS, C),...  64.6 us
    unnamed x1, local copies, waits for them, and re-layouts  1.8 us

profile of v3, /device:TPU:0, one launch (start us, length us, event | category | flops | bytes accessed | tf_op | source)
XLA Modules:
  0.0 66.5 jit_solution(8415191880085873683)
XLA Ops:
  0.0 64.6 %shard_map.145 = bf16[2,6,24,768]{3,2,1,0:T(8,128)(2,1)} custom-call(bf16[2,20,48,192]{3,2,1,0:T(8,128)(2,1)} %bitcast.3, bf16[5120,768]{1,0:T(8,128)(2,1)} %pw_h.1, f32[2,8,96,96]{3,2,1,0:T(8,128)} %one_h.1, f32[2,8,96,96]{3,2,1,0:T(8,128)} %two_h.1, bf16[768,3072]{1,0:T(8,128)(2,1)} %up_h.1, bf16[3072,768]{1,0:T(8,128)(2,1)} %down_h.1, ...), custom_call_target="tpu_custom_call" | custom-call | tf_op jit(solution)/shard_map/pallas_call | solution.py:481
  64.6 1.8 %copy.17 = bf16[2,24,6,768]{3,1,2,0:T(8,128)(2,1)} copy(bf16[2,24,6,768]{3,1,2,0:T(8,128)(2,1)} %bitcast.2) | data formatting | bytes 884736

commit v4 on v3

--- a/solution.py
+++ b/solution.py
@@ -43,11 +43,11 @@
     angle = 2.0 * math.pi * ((k[:, None] * w[None, :]) % W) / W
     scale = 1.0 / math.sqrt(W)
     both = np.stack([np.cos(angle), -np.sin(angle)]) * scale
-    fwd = both.reshape(2, 8, 8, NLON, COLS).transpose(1, 0, 2, 3, 4).reshape(128, NLON, COLS)
+    fwd = both.reshape(2, 8, 2, 4, W).transpose(2, 1, 3, 0, 4).reshape(128, NLON, COLS)
     fwd = np.pad(fwd, ((0, 0), (0, 0), (0, 2))).reshape(128, 256)
     weight = np.where(k == 0, 1.0, 2.0)
     back = both * weight[None, :, None]
-    back = back.reshape(2, 8, 8, NLON, COLS).transpose(3, 4, 1, 0, 2).reshape(NLON, COLS, 128)
+    back = back.reshape(2, 8, 2, 4, W).transpose(4, 2, 1, 3, 0).reshape(NLON, COLS, 128)
     back = np.pad(back, ((0, 0), (0, 2), (0, 0))).reshape(256, 128)
     return fwd, back
 
@@ -80,7 +80,7 @@
     t_v, m_v, lhs_v, q0_v, q3_v, tot_v, acc_v, nf_v, tn_v, nrm_v,
     ew_s, ew_r, ns_s, ns_r,
     p1_s, p1_r, p2_s, p2_r, p3_s, p3_r, p4_s, p4_r,
-    z_v, v_v, w1_v, w2_v,
+    z_v, v_v, w1_v, w2_v, h0_v, h1_v,
     lsem, halo_ss, halo_rs, s1, r1, s2, r2, s3, r3, s4, r4,
 ):
     a = lax.axis_index("lat")
@@ -101,11 +101,12 @@
 
     c_grid = load(0, grid_h, grid_v)
     c_tab = load(1, tab_h, tab_v)
-    c_pw = load(3, pw_h, pw_v)
-    c_one = load(4, one_h.at[:, n], one_v)
-    c_two = load(5, two_h.at[:, n], two_v)
-    c_up = load(6, up_h, up_v)
-    c_down = load(7, down_h, down_v)
+    c_pw = {}
+    for i, off in enumerate((1, 2, 0, 3)):
+        part = pl.ds(1280 * off, 1280)
+        c_pw[off] = load(2 + i, pw_h.at[part], pw_v.at[part])
+    c_one = load(6, one_h.at[:, n], one_v)
+    c_two = load(7, two_h.at[:, n], two_v)
 
     barrier = pltpu.get_barrier_semaphore()
 
@@ -172,27 +173,30 @@
                     value.reshape(192, 128).astype(BF16)
                 )
 
-    c_pw.wait()
+    def weight(off, pair):
+        return pw_v[1280 * off : 1280 * off + 1280, 256 * pair : 256 * pair + 256]
+
+    c_pw[1].wait()
+    c_pw[2].wait()
     for pair in range(3):
-        cols = slice(256 * pair, 256 * pair + 256)
-        weight = lambda off: pw_v[1280 * off : 1280 * off + 1280, cols]
-        above = dot(lhs_v[1], weight(0))
-        below = dot(lhs_v[0], weight(3))
-        for lane in range(2):
-            tile = 2 * pair + lane
-            lanes = slice(128 * lane, 128 * lane + 128)
-            for m in range(16):
-                rows = slice(ROWS * m, ROWS * m + ROWS)
-                q0_v[tile, 32 * m + 1 : 32 * m + 1 + ROWS, :] = above[rows, lanes]
-                q3_v[tile, 32 * m + 7 : 32 * m + 7 + ROWS, :] = below[rows, lanes]
-        value = dot(lhs_v[0], weight(1)) + dot(lhs_v[1], weight(2))
-        for lane in range(2):
-            tile = 2 * pair + lane
-            lanes = slice(128 * lane, 128 * lane + 128)
-            shifted = (
-                q0_v[tile].reshape(16, 32, 128)[:, :ROWS] + q3_v[tile].reshape(16, 32, 128)[:, 8:]
-            )
-            tot_v[tile] = value[:, lanes] + shifted.reshape(384, 128)
+        value = dot(lhs_v[0], weight(1, pair)) + dot(lhs_v[1], weight(2, pair))
+        tot_v[2 * pair] = value[:, :128]
+        tot_v[2 * pair + 1] = value[:, 128:]
+    for off, half, out_v, lead in ((0, 1, q0_v, 1), (3, 0, q3_v, 7)):
+        c_pw[off].wait()
+        for pair in range(3):
+            value = dot(lhs_v[half], weight(off, pair))
+            for lane in range(2):
+                lanes = slice(128 * lane, 128 * lane + 128)
+                for m in range(16):
+                    out_v[2 * pair + lane, 32 * m + lead : 32 * m + lead + ROWS, :] = value[
+                        ROWS * m : ROWS * m + ROWS, lanes
+                    ]
+    c_up = load(8, up_h, up_v)
+    c_down = load(9, down_h, down_v)
+    for tile in range(6):
+        shifted = q0_v[tile].reshape(16, 32, 128)[:, :ROWS] + q3_v[tile].reshape(16, 32, 128)[:, 8:]
+        tot_v[tile] += shifted.reshape(384, 128)
 
     for tile in range(6):
         cols = slice(128 * tile, 128 * tile + 128)
@@ -318,90 +322,93 @@
 
     lax.fori_loop(1, NLON, wait1, 0)
 
-    x = p1_r[...].astype(F32).reshape(256, MSG).astype(BF16)
-    y = dot(fw_ref[...], x)
-    p2_s[...] = y.reshape(8, 16, MSG).astype(BF16)
-
     def mate_of(d):
         other = lax.rem(g + d, 8)
         return other, (other // 2, (other % 2) * 16 + p)
 
-    def send2(d, _):
-        other, dev = mate_of(d)
-        remote(p2_s.at[other], p2_r.at[g], s2.at[other], r2.at[g], dev).start()
-        return 0
-
-    lax.fori_loop(1, 8, send2, 0)
-
-    def spread(src, value):
+    x = p1_r[...].astype(F32).reshape(256, MSG).astype(BF16)
+    for kh in range(2):
+        part = dot(fw_ref[64 * kh : 64 * kh + 64, :], x)
+        p2_s[kh] = part.reshape(8, 8, MSG).astype(BF16)
+        for d in range(1, 8):
+            other, dev = mate_of(d)
+            remote(
+                p2_s.at[kh, other], p2_r.at[kh, g], s2.at[kh, other], r2.at[kh, g], dev
+            ).start()
+
+    def spread(kh, src, value):
         for i in range(ROW12):
             piece = value[:, BS * i : BS * i + BS]
-            piece = jnp.concatenate([piece, jnp.zeros((16, 128 - BS), F32)], axis=1)
-            z_v[pl.ds(ROW12 * src + i, 8, stride=192), :] = piece[:8]
-            z_v[pl.ds(H + ROW12 * src + i, 8, stride=192), :] = piece[8:]
-
-    spread(g, p2_s[g].astype(F32))
-
-    def take2(d, _):
-        other, dev = mate_of(d)
-        remote(p2_s.at[other], p2_r.at[other], s2.at[other], r2.at[other], dev).wait_recv()
-        spread(other, p2_r[other].astype(F32))
-        return 0
-
-    lax.fori_loop(1, 8, take2, 0)
-
-    for pair in range(4):
-        k0, k1 = 384 * pair, 384 * pair + 192
-        z = jnp.concatenate([z_v[k0 : k0 + 192, :], z_v[k1 : k1 + 192, :]], axis=1).astype(BF16)
-        spec = dot(fh_ref[...], z)
-        modes = jnp.concatenate(
-            [
-                jnp.concatenate([spec[:H, :128], spec[H:, :128]], axis=1),
-                jnp.concatenate([spec[:H, 128:], spec[H:, 128:]], axis=1),
-            ],
-            axis=0,
-        )
-        mid = jnp.maximum(dot(modes.astype(BF16), w1_v[...]) + bias, 0.0)
-        res = dot(mid.astype(BF16), w2_v[...])
-        res = res - jnp.clip(res, -0.01, 0.01)
-        back = jnp.concatenate(
-            [
-                jnp.concatenate([res[:H, :128], res[H:, :128]], axis=1),
-                jnp.concatenate([res[:H, 128:], res[H:, 128:]], axis=1),
-            ],
-            axis=0,
-        )
-        rows = dot(bh_ref[...], back.astype(BF16))
-        v_v[k0 : k0 + 192, :] = rows[:, :128]
-        v_v[k1 : k1 + 192, :] = rows[:, 128:]
-
-    def gather_rows(dest):
-        pieces = []
-        for i in range(ROW12):
-            re = v_v[pl.ds(ROW12 * dest + i, 8, stride=192), :]
-            im = v_v[pl.ds(H + ROW12 * dest + i, 8, stride=192), :]
-            pieces.append(jnp.concatenate([re, im], axis=0)[:, :BS])
+            piece = jnp.concatenate([piece, jnp.zeros((8, 128 - BS), F32)], axis=1)
+            z_v[pl.ds(768 * kh + ROW12 * src + i, 8, stride=H), :] = piece
+
+    def gather(kh, dest):
+        pieces = [
+            v_v[pl.ds(768 * kh + ROW12 * dest + i, 8, stride=H), :][:, :BS] for i in range(ROW12)
+        ]
         return jnp.concatenate(pieces, axis=1).astype(BF16)
 
-    def send3(d, _):
-        other, dev = mate_of(d)
-        p3_s[other] = gather_rows(other)
-        remote(p3_s.at[other], p3_r.at[g], s3.at[other], r3.at[g], dev).start()
-        return 0
-
-    lax.fori_loop(1, 8, send3, 0)
-    p3_r[g] = gather_rows(g)
+    for kh in range(2):
+        spread(kh, g, p2_s[kh, g].astype(F32))
+
+        def take2(d, _):
+            other, dev = mate_of(d)
+            remote(
+                p2_s.at[kh, other], p2_r.at[kh, other], s2.at[kh, other], r2.at[kh, other], dev
+            ).wait_recv()
+            spread(kh, other, p2_r[kh, other].astype(F32))
+            return 0
+
+        lax.fori_loop(1, 8, take2, 0)
+
+        for pair in (2 * kh, 2 * kh + 1):
+            k0, k1 = 384 * pair, 384 * pair + 192
+            z = jnp.concatenate([z_v[k0 : k0 + 192, :], z_v[k1 : k1 + 192, :]], axis=1)
+            spec = dot(fh_ref[...], z.astype(BF16))
+            modes = jnp.concatenate(
+                [
+                    jnp.concatenate([spec[:H, :128], spec[H:, :128]], axis=1),
+                    jnp.concatenate([spec[:H, 128:], spec[H:, 128:]], axis=1),
+                ],
+                axis=0,
+            )
+            mid = jnp.maximum(dot(modes.astype(BF16), w1_v[...]) + bias, 0.0)
+            res = dot(mid.astype(BF16), w2_v[...])
+            res = res - jnp.clip(res, -0.01, 0.01)
+            back = jnp.concatenate(
+                [
+                    jnp.concatenate([res[:H, :128], res[H:, :128]], axis=1),
+                    jnp.concatenate([res[:H, 128:], res[H:, 128:]], axis=1),
+                ],
+                axis=0,
+            )
+            rows = dot(bh_ref[...], back.astype(BF16))
+            v_v[k0 : k0 + 192, :] = rows[:, :128]
+            v_v[k1 : k1 + 192, :] = rows[:, 128:]
+
+        def send3(d, _):
+            other, dev = mate_of(d)
+            p3_s[kh, other] = gather(kh, other)
+            remote(
+                p3_s.at[kh, other], p3_r.at[kh, g], s3.at[kh, other], r3.at[kh, g], dev
+            ).start()
+            return 0
+
+        lax.fori_loop(1, 8, send3, 0)
+        p3_r[kh, g] = gather(kh, g)
 
     def wait3(d, _):
         other, dev = mate_of(d)
-        remote(p3_s.at[other], p3_r.at[other], s3.at[other], r3.at[other], dev).wait_recv()
+        for kh in range(2):
+            remote(
+                p3_s.at[kh, other], p3_r.at[kh, other], s3.at[kh, other], r3.at[kh, other], dev
+            ).wait_recv()
         return 0
 
     lax.fori_loop(1, 8, wait3, 0)
 
-    field = dot(bw_ref[...], p3_r[...].reshape(128, MSG))
+    field = dot(bw_ref[...], p3_r[...].astype(F32).reshape(128, MSG).astype(BF16))
     p4_s[...] = field.reshape(NLON, 8, MSG).astype(BF16)
-
     steps = [(dx, dy, dz) for dx in range(2) for dy in range(4) for dz in range(4)]
     steps.sort(key=lambda t: -(t[0] + min(t[1], 4 - t[1]) + min(t[2], 4 - t[2])))
     for dx, dy, dz in steps[:-1]:
@@ -438,14 +445,25 @@
     c_up.wait()
     c_down.wait()
 
-    def mlp(step, _):
-        cols = pl.ds(pl.multiple_of(step * 256, 256), 256)
-        hidden = dot(nrm_v[...], up_v[:, cols])
+    def up(step):
+        return dot(nrm_v[...], up_v[:, pl.ds(pl.multiple_of(step * 256, 256), 256)])
+
+    def down(hidden, step):
         hidden = 0.5 * hidden * (1.0 + lax.erf(hidden * (1.0 / math.sqrt(2.0))))
-        acc_v[...] += dot(hidden.astype(BF16), down_v[cols, :])
-        return 0
-
-    lax.fori_loop(0, HID // 256, mlp, 0)
+        rows = pl.ds(pl.multiple_of(step * 256, 256), 256)
+        return dot(hidden.astype(BF16), down_v[rows, :])
+
+    h0_v[...] = up(0)
+
+    def mlp(it, _):
+        step = 2 * it
+        h1_v[...] = up(step + 1)
+        acc_v[...] += down(h0_v[...], step)
+        h0_v[...] = up(jnp.minimum(step + 2, HID // 256 - 1))
+        acc_v[...] += down(h1_v[...], step + 1)
+        return 0
+
+    lax.fori_loop(0, HID // 512, mlp, 0)
     out_ref[...] = acc_v[...].reshape(2, COLS, ROWS, C).astype(BF16)
 
     for copy in halos:
@@ -461,8 +479,13 @@
 
     def drain_lat(d, _):
         other, dev = mate_of(d)
-        remote(p2_s.at[other], p2_r.at[g], s2.at[other], r2.at[g], dev).wait_send()
-        remote(p3_s.at[other], p3_r.at[g], s3.at[other], r3.at[g], dev).wait_send()
+        for kh in range(2):
+            remote(
+                p2_s.at[kh, other], p2_r.at[kh, g], s2.at[kh, other], r2.at[kh, g], dev
+            ).wait_send()
+            remote(
+                p3_s.at[kh, other], p3_r.at[kh, g], s3.at[kh, other], r3.at[kh, g], dev
+            ).wait_send()
         return 0
 
     lax.fori_loop(1, 8, drain_lat, 0)
@@ -507,25 +530,27 @@
             pltpu.VMEM((6, 16, C), BF16),
             pltpu.VMEM((NLON, 8, MSG), BF16),
             pltpu.VMEM((NLON, 8, MSG), BF16),
-            pltpu.VMEM((8, 16, MSG), BF16),
-            pltpu.VMEM((8, 16, MSG), BF16),
-            pltpu.VMEM((8, 16, MSG), BF16),
-            pltpu.VMEM((8, 16, MSG), BF16),
+            pltpu.VMEM((2, 8, 8, MSG), BF16),
+            pltpu.VMEM((2, 8, 8, MSG), BF16),
+            pltpu.VMEM((2, 8, 8, MSG), BF16),
+            pltpu.VMEM((2, 8, 8, MSG), BF16),
             pltpu.VMEM((NLON, 8, MSG), BF16),
             pltpu.VMEM((NLON, 8, MSG), BF16),
             pltpu.VMEM((8 * 192, 128), F32),
             pltpu.VMEM((8 * 192, 128), F32),
             pltpu.VMEM((256, 256), BF16),
             pltpu.VMEM((256, 256), BF16),
-            dma((8,)),
+            pltpu.VMEM((288, 256), F32),
+            pltpu.VMEM((288, 256), F32),
+            dma((10,)),
             dma((8,)),
             dma((8,)),
             dma((NLON,)),
             dma((NLON,)),
-            dma((8,)),
-            dma((8,)),
-            dma((8,)),
-            dma((8,)),
+            dma((2, 8)),
+            dma((2, 8)),
+            dma((2, 8)),
+            dma((2, 8)),
             dma((NLON,)),
             dma((NLON,)),
         ],

time: 67.5 us -> 63.5 us (0.941)
  Pallas kernels: 64.6 us -> 60.9 us
    pallas_call x1, Pallas kernels: 64.6 us -> 60.9 us  [local(): pl.pallas_call(kernel, out_shape=jax.ShapeDtypeStruct((2, COLS, ROWS, C),...]
where the time goes in v4:
time: 63.5 us; the launch traced here: 62.7 us
  Pallas kernels  60.9 us (96%)
  local copies, waits for them, and re-layouts  1.8 us (3%)
    pallas_call x1, Pallas kernels, local(): pl.pallas_call(kernel, out_shape=jax.ShapeDtypeStruct((2, COLS, ROWS, C),...  60.9 us
    unnamed x1, local copies, waits for them, and re-layouts  1.8 us

profile of v4, /device:TPU:0, one launch (start us, length us, event | category | flops | bytes accessed | tf_op | source)
XLA Modules:
  0.0 62.7 jit_solution(304782945008276414)
XLA Ops:
  0.0 60.9 %shard_map.145 = bf16[2,6,24,768]{3,2,1,0:T(8,128)(2,1)} custom-call(bf16[2,20,48,192]{3,2,1,0:T(8,128)(2,1)} %bitcast.3, bf16[5120,768]{1,0:T(8,128)(2,1)} %pw_h.1, f32[2,8,96,96]{3,2,1,0:T(8,128)} %one_h.1, f32[2,8,96,96]{3,2,1,0:T(8,128)} %two_h.1, bf16[768,3072]{1,0:T(8,128)(2,1)} %up_h.1, bf16[3072,768]{1,0:T(8,128)(2,1)} %down_h.1, ...), custom_call_target="tpu_custom_call" | custom-call | tf_op jit(solution)/shard_map/pallas_call | solution.py:504
  60.9 1.8 %copy.17 = bf16[2,24,6,768]{3,1,2,0:T(8,128)(2,1)} copy(bf16[2,24,6,768]{3,1,2,0:T(8,128)(2,1)} %bitcast.2) | data formatting | bytes 884736

commit v5 on v4

--- a/solution.py
+++ b/solution.py
@@ -68,14 +68,36 @@
     return off * lax.rsqrt(spread + 1e-05) * gain
 
 
+def fold(msg):
+    row = lax.broadcasted_iota(jnp.int32, msg.shape[:-1] + (128,), msg.ndim - 2)
+    tiles = []
+    for u in range(7):
+        tile = msg[..., 128 * u : 128 * u + 128]
+        if u < COLS:
+            tile = jnp.where(row == 6, msg[..., u : u + 1, 896:1024], tile)
+            tile = jnp.where(row == 7, msg[..., u : u + 1, 1024:], tile)
+        tiles.append(tile)
+    return jnp.concatenate(tiles, axis=-1)
+
+
+def unfold(msg):
+    row = lax.broadcasted_iota(jnp.int32, msg.shape[:-1] + (128,), msg.ndim - 2)
+    last = [jnp.zeros(row.shape, F32)] * 2
+    for u in range(COLS):
+        for i in range(2):
+            piece = msg[..., 6 + i : 7 + i, 128 * u : 128 * u + 128]
+            last[i] = jnp.where(row == u, piece, last[i])
+    return jnp.concatenate([msg] + last, axis=-1)
+
+
 def dot(left, right):
     return jnp.dot(left, right, preferred_element_type=F32)
 
 
 def kernel(
-    grid_h, pw_h, one_h, two_h, up_h, down_h, tab_h,
-    g1_ref, bias_ref, g2_ref, sel_ref, fw_ref, bw_ref, fh_ref, bh_ref,
+    grid_h, pw_h, one_h, two_h, up_h, down_h, tab_h, sq_h, fw_h, bw_h, g1_h, bias_h, g2_h,
     out_ref,
+    sq_v, fw_ref, bw_ref, g1_ref, bias_ref, g2_ref,
     grid_v, pw_v, one_v, two_v, up_v, down_v, tab_v,
     t_v, m_v, lhs_v, q0_v, q3_v, tot_v, acc_v, nf_v, tn_v, nrm_v,
     ew_s, ew_r, ns_s, ns_r,
@@ -92,21 +114,6 @@
     mine = (row_y + row_z) % 2
     n = 2 * row_y + row_z // 2
     g = 2 * a + q
-    ways = [(da, db) for da in (1, 3) for db in (1, NLON - 1)]
-
-    def load(index, src, dst):
-        copy = pltpu.make_async_copy(src, dst, lsem.at[index])
-        copy.start()
-        return copy
-
-    c_grid = load(0, grid_h, grid_v)
-    c_tab = load(1, tab_h, tab_v)
-    c_pw = {}
-    for i, off in enumerate((1, 2, 0, 3)):
-        part = pl.ds(1280 * off, 1280)
-        c_pw[off] = load(2 + i, pw_h.at[part], pw_v.at[part])
-    c_one = load(6, one_h.at[:, n], one_v)
-    c_two = load(7, two_h.at[:, n], two_v)
 
     barrier = pltpu.get_barrier_semaphore()
 
@@ -126,9 +133,26 @@
         return 0
 
     lax.fori_loop(0, 6, greet_lat, 0)
-    for da, db in ways:
-        corner = (lax.rem(a + da, NLAT), lax.rem(b + db, NLON))
-        pl.semaphore_signal(barrier, inc=1, device_id=corner, device_id_type=MESH)
+    def load(index, src, dst):
+        copy = pltpu.make_async_copy(src, dst, lsem.at[index])
+        copy.start()
+        return copy
+
+    c_grid = load(0, grid_h, grid_v)
+    c_sq = load(10, sq_h, sq_v)
+    c_tab = load(1, tab_h, tab_v)
+    c_pw = {}
+    for i, off in enumerate((0, 3, 1, 2)):
+        part = pl.ds(1280 * off, 1280)
+        c_pw[off] = load(2 + i, pw_h.at[part], pw_v.at[part])
+    c_one = load(6, one_h.at[:, n], one_v)
+    c_two = load(7, two_h.at[:, n], two_v)
+    small = [
+        load(11 + i, src, dst)
+        for i, (src, dst) in enumerate(
+            ((g1_h, g1_ref), (bias_h, bias_ref), (g2_h, g2_ref), (fw_h, fw_ref), (bw_h, bw_ref))
+        )
+    ]
 
     nf_v[:, :, 144:] = jnp.zeros((6, 2, 48, 128), F32)
     for slots in (slice(0, 2), slice(8, 10)):
@@ -137,6 +161,7 @@
         q0_v[tile, pl.ds(0, 16, stride=32), :] = jnp.zeros((16, 128), F32)
         q3_v[tile, pl.ds(31, 16, stride=32), :] = jnp.zeros((16, 128), F32)
     c_grid.wait()
+    c_sq.wait()
     for smp in range(2):
         for lp in range(3):
             block = grid_v[smp, :, 16 * lp : 16 * lp + 16, :]
@@ -144,7 +169,7 @@
             for half in range(2):
                 x = block[:, half].reshape(NV * 8, 192).astype(BF16)
                 turned = lax.dot_general(
-                    sel_ref[...], x, (((1,), (1,)), ((), ())), preferred_element_type=F32
+                    sq_v[0], x, (((1,), (1,)), ((), ())), preferred_element_type=F32
                 )
                 first = (6 * smp + 2 * lp + half) * ROWS
                 for r8 in range(8):
@@ -176,12 +201,6 @@
     def weight(off, pair):
         return pw_v[1280 * off : 1280 * off + 1280, 256 * pair : 256 * pair + 256]
 
-    c_pw[1].wait()
-    c_pw[2].wait()
-    for pair in range(3):
-        value = dot(lhs_v[0], weight(1, pair)) + dot(lhs_v[1], weight(2, pair))
-        tot_v[2 * pair] = value[:, :128]
-        tot_v[2 * pair + 1] = value[:, 128:]
     for off, half, out_v, lead in ((0, 1, q0_v, 1), (3, 0, q3_v, 7)):
         c_pw[off].wait()
         for pair in range(3):
@@ -192,22 +211,12 @@
                     out_v[2 * pair + lane, 32 * m + lead : 32 * m + lead + ROWS, :] = value[
                         ROWS * m : ROWS * m + ROWS, lanes
                     ]
-    c_up = load(8, up_h, up_v)
-    c_down = load(9, down_h, down_v)
-    for tile in range(6):
-        shifted = q0_v[tile].reshape(16, 32, 128)[:, :ROWS] + q3_v[tile].reshape(16, 32, 128)[:, 8:]
-        tot_v[tile] += shifted.reshape(384, 128)
-
     for tile in range(6):
         cols = slice(128 * tile, 128 * tile + 128)
-        for smp in range(2):
-            for way, slot in ((0, 7), (1, 0)):
-                first = ROWS * (8 * smp + slot)
-                ew_s[way, smp, :, cols] = tot_v[tile, first : first + ROWS, :].astype(BF16)
         ns_s[0, :, cols] = q0_v[tile, pl.ds(ROWS, 16, stride=32), :].astype(BF16)
         ns_s[1, :, cols] = q3_v[tile, pl.ds(7, 16, stride=32), :].astype(BF16)
 
-    pl.semaphore_wait(barrier, NLON - 1 + 6 + 4)
+    pl.semaphore_wait(barrier, NLON - 1 + 6)
 
     def remote(src, dst, ssem, rsem, dev):
         return pltpu.make_async_remote_copy(
@@ -215,45 +224,56 @@
             device_id=dev, device_id_type=MESH,
         )
 
-    halos = []
-    for src, da in ((0, 1), (1, 3)):
-        for side, db in enumerate((0, 1, NLON - 1)):
-            slot = 3 * src + side
-            halos.append((ns_s.at[src], ns_r.at[slot], 2 + slot, da, db))
-    for src, db in ((0, 1), (1, NLON - 1)):
-        halos.append((ew_s.at[src], ew_r.at[src], src, 0, db))
     halos = [
         remote(
-            src, dst, halo_ss.at[sem], halo_rs.at[sem],
+            src.at[i], dst.at[i], halo_ss.at[sem + i], halo_rs.at[sem + i],
             (lax.rem(a + da, NLAT), lax.rem(b + db, NLON)),
         )
-        for src, dst, sem, da, db in halos
+        for src, dst, sem, ways in (
+            (ns_s, ns_r, 0, ((1, 0), (NLAT - 1, 0))),
+            (ew_s, ew_r, 2, ((0, 1), (0, NLON - 1))),
+        )
+        for i, (da, db) in enumerate(ways)
     ]
-    for copy in halos:
-        copy.start()
-    for copy in halos:
-        copy.wait_recv()
-
-    slot_ids = lax.broadcasted_iota(jnp.int32, (2, 8, 128), 1)
-
-    def edge_row(first, cols):
-        straight, west, east = [
-            ns_r[first + k, :, cols].astype(F32).reshape(2, 8, 128) for k in range(3)
-        ]
-        west = jnp.concatenate([west[:, 6:], west[:, :6]], axis=1)
-        east = jnp.concatenate([east[:, 2:], east[:, :2]], axis=1)
-        straight = straight + jnp.where(slot_ids == 1, west, 0.0)
-        return (straight + jnp.where(slot_ids == 6, east, 0.0)).reshape(16, 128)
-
+    halos[0].start()
+    halos[1].start()
+
+    c_pw[1].wait()
+    c_pw[2].wait()
+    for pair in range(3):
+        value = dot(lhs_v[0], weight(1, pair)) + dot(lhs_v[1], weight(2, pair))
+        for lane in range(2):
+            tile = 2 * pair + lane
+            shifted = (
+                q0_v[tile].reshape(16, 32, 128)[:, :ROWS] + q3_v[tile].reshape(16, 32, 128)[:, 8:]
+            )
+            tot_v[tile] = value[:, 128 * lane : 128 * lane + 128] + shifted.reshape(384, 128)
+    c_up = load(8, up_h, up_v)
+    c_down = load(9, down_h, down_v)
+
+    halos[0].wait_recv()
+    halos[1].wait_recv()
+    for tile in range(6):
+        cols = slice(128 * tile, 128 * tile + 128)
+        top, bottom = pl.ds(0, 16, stride=ROWS), pl.ds(ROWS - 1, 16, stride=ROWS)
+        tot_v[tile, top, :] += jnp.where(a > 0, ns_r[0, :, cols].astype(F32), 0.0)
+        tot_v[tile, bottom, :] += jnp.where(a < NLAT - 1, ns_r[1, :, cols].astype(F32), 0.0)
+        for smp in range(2):
+            for way, slot in ((0, 7), (1, 0)):
+                first = ROWS * (8 * smp + slot)
+                ew_s[way, smp, :, cols] = tot_v[tile, first : first + ROWS, :].astype(BF16)
+    halos[2].start()
+    halos[3].start()
+    halos[2].wait_recv()
+    halos[3].wait_recv()
     for tile in range(6):
         cols = slice(128 * tile, 128 * tile + 128)
         for smp in range(2):
             for way, slot in ((0, 1), (1, 6)):
                 first = ROWS * (8 * smp + slot)
                 tot_v[tile, first : first + ROWS, :] += ew_r[way, smp, :, cols].astype(F32)
-        top, bottom = pl.ds(0, 16, stride=ROWS), pl.ds(ROWS - 1, 16, stride=ROWS)
-        tot_v[tile, top, :] += jnp.where(a > 0, edge_row(0, cols), 0.0)
-        tot_v[tile, bottom, :] += jnp.where(a < NLAT - 1, edge_row(3, cols), 0.0)
+    for copy in small:
+        copy.wait()
 
     def owner(part, smp, blk):
         return part * 16 + (blk // 2) * 4 + (blk % 2) * 2 + (smp + blk // 2) % 2
@@ -279,7 +299,7 @@
                 msg = jnp.concatenate(
                     [plane[:, BS * blk : BS * blk + BS] for plane in planes], axis=1
                 )
-                p1_s[owner(part, smp, blk)] = msg.astype(BF16)
+                p1_s[owner(part, smp, blk)] = fold(msg).astype(BF16)
         odd = (smp + mine) % 2
         for dx in (1, 0):
             for dy in (2, 1, 3, 0):
@@ -326,7 +346,7 @@
         other = lax.rem(g + d, 8)
         return other, (other // 2, (other % 2) * 16 + p)
 
-    x = p1_r[...].astype(F32).reshape(256, MSG).astype(BF16)
+    x = unfold(p1_r[...].astype(F32)).reshape(256, MSG).astype(BF16)
     for kh in range(2):
         part = dot(fw_ref[64 * kh : 64 * kh + 64, :], x)
         p2_s[kh] = part.reshape(8, 8, MSG).astype(BF16)
@@ -364,7 +384,7 @@
         for pair in (2 * kh, 2 * kh + 1):
             k0, k1 = 384 * pair, 384 * pair + 192
             z = jnp.concatenate([z_v[k0 : k0 + 192, :], z_v[k1 : k1 + 192, :]], axis=1)
-            spec = dot(fh_ref[...], z.astype(BF16))
+            spec = dot(sq_v[1], z.astype(BF16))
             modes = jnp.concatenate(
                 [
                     jnp.concatenate([spec[:H, :128], spec[H:, :128]], axis=1),
@@ -382,7 +402,7 @@
                 ],
                 axis=0,
             )
-            rows = dot(bh_ref[...], back.astype(BF16))
+            rows = dot(sq_v[2], back.astype(BF16))
             v_v[k0 : k0 + 192, :] = rows[:, :128]
             v_v[k1 : k1 + 192, :] = rows[:, 128:]
 
@@ -408,7 +428,7 @@
     lax.fori_loop(1, 8, wait3, 0)
 
     field = dot(bw_ref[...], p3_r[...].astype(F32).reshape(128, MSG).astype(BF16))
-    p4_s[...] = field.reshape(NLON, 8, MSG).astype(BF16)
+    p4_s[...] = fold(field.reshape(NLON, 8, MSG)).astype(BF16)
     steps = [(dx, dy, dz) for dx in range(2) for dy in range(4) for dz in range(4)]
     steps.sort(key=lambda t: -(t[0] + min(t[1], 4 - t[1]) + min(t[2], 4 - t[2])))
     for dx, dy, dz in steps[:-1]:
@@ -426,7 +446,7 @@
     for smp in range(2):
 
         def join(part, _):
-            msgs = [p4_r[owner(part, smp, blk)].astype(F32) for blk in range(NB)]
+            msgs = [unfold(p4_r[owner(part, smp, blk)].astype(F32)) for blk in range(NB)]
             for i in range(ROW12):
                 plane = jnp.concatenate([m[:, BS * i : BS * i + BS] for m in msgs], axis=1)
                 for tile in range(6):
@@ -504,9 +524,15 @@
     out = pl.pallas_call(
         kernel,
         out_shape=jax.ShapeDtypeStruct((2, COLS, ROWS, C), BF16),
-        in_specs=[any_spec] * 7 + [vmem] * 8,
+        in_specs=[any_spec] * 13,
         out_specs=vmem,
         scratch_shapes=[
+            pltpu.VMEM((3, 192, 192), BF16),
+            pltpu.VMEM((128, 256), BF16),
+            pltpu.VMEM((256, 128), BF16),
+            pltpu.VMEM((C,), F32),
+            pltpu.VMEM((2, C), F32),
+            pltpu.VMEM((C,), F32),
             pltpu.VMEM((2, NV, 48, 192), BF16),
             pltpu.VMEM((5120, C), BF16),
             pltpu.VMEM((2, BS, BS), F32),
@@ -527,24 +553,24 @@
             pltpu.VMEM((2, 2, ROWS, C), BF16),
             pltpu.VMEM((2, 2, ROWS, C), BF16),
             pltpu.VMEM((2, 16, C), BF16),
-            pltpu.VMEM((6, 16, C), BF16),
-            pltpu.VMEM((NLON, 8, MSG), BF16),
-            pltpu.VMEM((NLON, 8, MSG), BF16),
+            pltpu.VMEM((2, 16, C), BF16),
+            pltpu.VMEM((NLON, 8, 896), BF16),
+            pltpu.VMEM((NLON, 8, 896), BF16),
             pltpu.VMEM((2, 8, 8, MSG), BF16),
             pltpu.VMEM((2, 8, 8, MSG), BF16),
             pltpu.VMEM((2, 8, 8, MSG), BF16),
             pltpu.VMEM((2, 8, 8, MSG), BF16),
-            pltpu.VMEM((NLON, 8, MSG), BF16),
-            pltpu.VMEM((NLON, 8, MSG), BF16),
+            pltpu.VMEM((NLON, 8, 896), BF16),
+            pltpu.VMEM((NLON, 8, 896), BF16),
             pltpu.VMEM((8 * 192, 128), F32),
             pltpu.VMEM((8 * 192, 128), F32),
             pltpu.VMEM((256, 256), BF16),
             pltpu.VMEM((256, 256), BF16),
             pltpu.VMEM((288, 256), F32),
             pltpu.VMEM((288, 256), F32),
-            dma((10,)),
-            dma((8,)),
-            dma((8,)),
+            dma((16,)),
+            dma((4,)),
+            dma((4,)),
             dma((NLON,)),
             dma((NLON,)),
             dma((2, 8)),
@@ -560,8 +586,8 @@
     )(
         grid.transpose(0, 1, 3, 2), patch_weight, spectral_one, spectral_two, fc_up, fc_down,
         const(feature_table()),
+        const(np.stack([pick_table(), fh, bh])), const(fw), const(bw),
         norm_gain_one, spectral_bias, norm_gain_two,
-        const(pick_table()), const(fw), const(bw), const(fh), const(bh),
     )
     return out.transpose(0, 2, 1, 3)
 

time: 63.5 us -> 60.4 us (0.951)
  Pallas kernels: 60.9 us -> 58.2 us
    pallas_call x1, Pallas kernels: 60.9 us -> 58.2 us  [local(): pl.pallas_call(kernel, out_shape=jax.ShapeDtypeStruct((2, COLS, ROWS, C),...]
where the time goes in v5:
time: 60.4 us; the launch traced here: 60 us
  Pallas kernels  58.2 us (96%)
  local copies, waits for them, and re-layouts  1.8 us (3%)
    pallas_call x1, Pallas kernels, local(): pl.pallas_call(kernel, out_shape=jax.ShapeDtypeStruct((2, COLS, ROWS, C),...  58.2 us
    unnamed x1, local copies, waits for them, and re-layouts  1.8 us

profile of v5, /device:TPU:0, one launch (start us, length us, event | category | flops | bytes accessed | tf_op | source)
XLA Modules:
  0.0 60.0 jit_solution(13586256298857508356)
XLA Ops:
  0.0 58.2 %shard_map.127 = bf16[2,6,24,768]{3,2,1,0:T(8,128)(2,1)} custom-call(bf16[2,20,48,192]{3,2,1,0:T(8,128)(2,1)} %bitcast.3, bf16[5120,768]{1,0:T(8,128)(2,1)} %pw_h.1, f32[2,8,96,96]{3,2,1,0:T(8,128)} %one_h.1, f32[2,8,96,96]{3,2,1,0:T(8,128)} %two_h.1, bf16[768,3072]{1,0:T(8,128)(2,1)} %up_h.1, bf16[3072,768]{1,0:T(8,128)(2,1)} %down_h.1, ...), custom_call_target="tpu_custom_call" | custom-call | tf_op jit(solution)/shard_map/pallas_call | solution.py:524
  58.2 1.8 %copy.15 = bf16[2,24,6,768]{3,1,2,0:T(8,128)(2,1)} copy(bf16[2,24,6,768]{3,1,2,0:T(8,128)(2,1)} %bitcast.2) | data formatting | bytes 884736

commit v6 on v5

--- a/solution.py
+++ b/solution.py
@@ -99,7 +99,7 @@
     out_ref,
     sq_v, fw_ref, bw_ref, g1_ref, bias_ref, g2_ref,
     grid_v, pw_v, one_v, two_v, up_v, down_v, tab_v,
-    t_v, m_v, lhs_v, q0_v, q3_v, tot_v, acc_v, nf_v, tn_v, nrm_v,
+    t_v, m_v, lhs_v, side_v, rim_v, te_v, q0_v, q3_v, tot_v, acc_v, nf_v, tn_v, nrm_v,
     ew_s, ew_r, ns_s, ns_r,
     p1_s, p1_r, p2_s, p2_r, p3_s, p3_r, p4_s, p4_r,
     z_v, v_v, w1_v, w2_v, h0_v, h1_v,
@@ -155,11 +155,12 @@
     ]
 
     nf_v[:, :, 144:] = jnp.zeros((6, 2, 48, 128), F32)
-    for slots in (slice(0, 2), slice(8, 10)):
-        m_v[:, :, :, slots] = jnp.zeros((2, 6, 2, 2, ROWS, 128), F32)
+    for smp in range(2):
+        for first in (240 * smp, 240 * smp + 192):
+            m_v[:, :, first : first + 48] = jnp.zeros((2, 6, 48, 128), F32)
     for tile in range(6):
-        q0_v[tile, pl.ds(0, 16, stride=32), :] = jnp.zeros((16, 128), F32)
-        q3_v[tile, pl.ds(31, 16, stride=32), :] = jnp.zeros((16, 128), F32)
+        q0_v[tile, pl.ds(0, 12, stride=32), :] = jnp.zeros((12, 128), F32)
+        q3_v[tile, pl.ds(31, 12, stride=32), :] = jnp.zeros((12, 128), F32)
     c_grid.wait()
     c_sq.wait()
     for smp in range(2):
@@ -181,40 +182,39 @@
         for r in range(1, 4):
             value = value + dot(t_v[4 * half + r].astype(BF16), tab_v[r])
         for tile in range(6):
-            part = value[:, 128 * tile : 128 * tile + 128].reshape(2, COLS, ROWS, 128)
+            lanes = slice(128 * tile, 128 * tile + 128)
             for smp in range(2):
-                m_v[half, tile, smp, 2 : 2 + COLS] = part[smp]
-
+                m_v[half, tile, 240 * smp + 48 : 240 * smp + 192] = value[
+                    144 * smp : 144 * smp + 144, lanes
+                ]
+
+    places = ((3, 0), (4, 0), (5, 0), (1, 1), (2, 1), (3, 1), (4, 1), (5, 1), (1, 2), (2, 2))
     for half in range(2):
-        for tile in range(10):
-            lane, slot = (
-                (3, 0), (4, 0), (5, 0), (1, 1), (2, 1), (3, 1), (4, 1), (5, 1), (1, 2), (2, 2)
-            )[tile]
+        for tile, (lane, slot) in enumerate(places):
+            cols = slice(128 * tile, 128 * tile + 128)
+            outer = []
             for smp in range(2):
-                value = m_v[half, lane, smp, slot : slot + 8]
+                first = (10 * smp + slot) * ROWS
+                rim = first + (0, ROWS - 1)[half]
+                value = m_v[half, lane, first : first + 192, :]
+                row = m_v[half, lane, pl.ds(rim, 8, stride=ROWS), :]
                 if tile in (2, 7):
-                    value = value + m_v[half, 0, smp, slot + 1 : slot + 9]
-                lhs_v[half, 192 * smp : 192 * smp + 192, 128 * tile : 128 * tile + 128] = (
-                    value.reshape(192, 128).astype(BF16)
-                )
+                    value = value + m_v[half, 0, first + ROWS : first + ROWS + 192, :]
+                    row = row + m_v[half, 0, pl.ds(rim + ROWS, 8, stride=ROWS), :]
+                outer.append(row)
+                lhs_v[half, 144 * smp : 144 * smp + 144, cols] = value[ROWS:168].astype(BF16)
+                side = jnp.concatenate([value[:ROWS], value[168:]], axis=0)
+                side_v[half, 48 * smp : 48 * smp + 48, cols] = side.astype(BF16)
+            rim_v[half, :, cols] = jnp.concatenate(outer, axis=0).astype(BF16)
 
     def weight(off, pair):
         return pw_v[1280 * off : 1280 * off + 1280, 256 * pair : 256 * pair + 256]
 
-    for off, half, out_v, lead in ((0, 1, q0_v, 1), (3, 0, q3_v, 7)):
+    for way, (off, half) in enumerate(((0, 1), (3, 0))):
         c_pw[off].wait()
         for pair in range(3):
-            value = dot(lhs_v[half], weight(off, pair))
-            for lane in range(2):
-                lanes = slice(128 * lane, 128 * lane + 128)
-                for m in range(16):
-                    out_v[2 * pair + lane, 32 * m + lead : 32 * m + lead + ROWS, :] = value[
-                        ROWS * m : ROWS * m + ROWS, lanes
-                    ]
-    for tile in range(6):
-        cols = slice(128 * tile, 128 * tile + 128)
-        ns_s[0, :, cols] = q0_v[tile, pl.ds(ROWS, 16, stride=32), :].astype(BF16)
-        ns_s[1, :, cols] = q3_v[tile, pl.ds(7, 16, stride=32), :].astype(BF16)
+            value = dot(rim_v[half], weight(off, pair))
+            ns_s[way, :, 256 * pair : 256 * pair + 256] = value.astype(BF16)
 
     pl.semaphore_wait(barrier, NLON - 1 + 6)
 
@@ -240,37 +240,66 @@
 
     c_pw[1].wait()
     c_pw[2].wait()
+    none = jnp.zeros((4, 1, 256), F32)
     for pair in range(3):
+        value = dot(side_v[0], weight(1, pair)) + dot(side_v[1], weight(2, pair))
+        above = dot(side_v[1], weight(0, pair)).reshape(4, ROWS, 256)
+        below = dot(side_v[0], weight(3, pair)).reshape(4, ROWS, 256)
+        above = jnp.concatenate([none, above[:, :-1]], axis=1)
+        below = jnp.concatenate([below[:, 1:], none], axis=1)
+        value = value + (above + below).reshape(96, 256)
+        te_v[2 * pair] = value[:, :128]
+        te_v[2 * pair + 1] = value[:, 128:]
+
+    def rim_rows(way, cols, picks):
+        rows = ns_r[way, :, cols].astype(F32)
+        rows = jnp.concatenate([rows[lo:hi] for lo, hi in picks], axis=0)
+        return jnp.where((a > 0, a < NLAT - 1)[way], rows, 0.0)
+
+    halos[0].wait_recv()
+    halos[1].wait_recv()
+    for tile in range(6):
+        cols = slice(128 * tile, 128 * tile + 128)
+        for way in range(2):
+            at = pl.ds((0, ROWS - 1)[way], 4, stride=ROWS)
+            te_v[tile, at, :] += rim_rows(way, cols, ((0, 1), (7, 8), (8, 9), (15, 16)))
+        for smp in range(2):
+            for way in range(2):
+                first = ROWS * (2 * smp + 1 - way)
+                ew_s[way, smp, :, cols] = te_v[tile, first : first + ROWS, :].astype(BF16)
+    halos[2].start()
+    halos[3].start()
+
+    for pair in range(3):
+        for off, half, out_v, lead in ((0, 1, q0_v, 1), (3, 0, q3_v, 7)):
+            value = dot(lhs_v[half], weight(off, pair))
+            for lane in range(2):
+                lanes = slice(128 * lane, 128 * lane + 128)
+                for m in range(12):
+                    out_v[2 * pair + lane, 32 * m + lead : 32 * m + lead + ROWS, :] = value[
+                        ROWS * m : ROWS * m + ROWS, lanes
+                    ]
         value = dot(lhs_v[0], weight(1, pair)) + dot(lhs_v[1], weight(2, pair))
         for lane in range(2):
             tile = 2 * pair + lane
             shifted = (
-                q0_v[tile].reshape(16, 32, 128)[:, :ROWS] + q3_v[tile].reshape(16, 32, 128)[:, 8:]
+                q0_v[tile].reshape(12, 32, 128)[:, :ROWS] + q3_v[tile].reshape(12, 32, 128)[:, 8:]
             )
-            tot_v[tile] = value[:, 128 * lane : 128 * lane + 128] + shifted.reshape(384, 128)
+            tot_v[tile] = value[:, 128 * lane : 128 * lane + 128] + shifted.reshape(288, 128)
     c_up = load(8, up_h, up_v)
     c_down = load(9, down_h, down_v)
-
-    halos[0].wait_recv()
-    halos[1].wait_recv()
     for tile in range(6):
         cols = slice(128 * tile, 128 * tile + 128)
-        top, bottom = pl.ds(0, 16, stride=ROWS), pl.ds(ROWS - 1, 16, stride=ROWS)
-        tot_v[tile, top, :] += jnp.where(a > 0, ns_r[0, :, cols].astype(F32), 0.0)
-        tot_v[tile, bottom, :] += jnp.where(a < NLAT - 1, ns_r[1, :, cols].astype(F32), 0.0)
-        for smp in range(2):
-            for way, slot in ((0, 7), (1, 0)):
-                first = ROWS * (8 * smp + slot)
-                ew_s[way, smp, :, cols] = tot_v[tile, first : first + ROWS, :].astype(BF16)
-    halos[2].start()
-    halos[3].start()
+        for way in range(2):
+            at = pl.ds((0, ROWS - 1)[way], 12, stride=ROWS)
+            tot_v[tile, at, :] += rim_rows(way, cols, ((1, 7), (9, 15)))
     halos[2].wait_recv()
     halos[3].wait_recv()
     for tile in range(6):
         cols = slice(128 * tile, 128 * tile + 128)
         for smp in range(2):
-            for way, slot in ((0, 1), (1, 6)):
-                first = ROWS * (8 * smp + slot)
+            for way, j in ((0, 0), (1, COLS - 1)):
+                first = ROWS * (COLS * smp + j)
                 tot_v[tile, first : first + ROWS, :] += ew_r[way, smp, :, cols].astype(F32)
     for copy in small:
         copy.wait()
@@ -280,8 +309,7 @@
 
     for smp in range(2):
         rows = slice(144 * smp, 144 * smp + 144)
-        first = ROWS * (8 * smp + 1)
-        tok = jnp.concatenate([tot_v[t, first : first + 144, :] for t in range(6)], axis=1)
+        tok = jnp.concatenate([tot_v[t, rows, :] for t in range(6)], axis=1)
         tok = tok.astype(BF16).astype(F32)
         normed = norm(tok, g1_ref[...].reshape(1, C)).astype(BF16).astype(F32)
         tn_v[rows, :] = tok + normed
@@ -381,30 +409,35 @@
 
         lax.fori_loop(1, 8, take2, 0)
 
-        for pair in (2 * kh, 2 * kh + 1):
-            k0, k1 = 384 * pair, 384 * pair + 192
-            z = jnp.concatenate([z_v[k0 : k0 + 192, :], z_v[k1 : k1 + 192, :]], axis=1)
-            spec = dot(sq_v[1], z.astype(BF16))
-            modes = jnp.concatenate(
-                [
-                    jnp.concatenate([spec[:H, :128], spec[H:, :128]], axis=1),
-                    jnp.concatenate([spec[:H, 128:], spec[H:, 128:]], axis=1),
-                ],
-                axis=0,
-            )
-            mid = jnp.maximum(dot(modes.astype(BF16), w1_v[...]) + bias, 0.0)
-            res = dot(mid.astype(BF16), w2_v[...])
-            res = res - jnp.clip(res, -0.01, 0.01)
-            back = jnp.concatenate(
-                [
-                    jnp.concatenate([res[:H, :128], res[H:, :128]], axis=1),
-                    jnp.concatenate([res[:H, 128:], res[H:, 128:]], axis=1),
-                ],
-                axis=0,
-            )
-            rows = dot(sq_v[2], back.astype(BF16))
-            v_v[k0 : k0 + 192, :] = rows[:, :128]
-            v_v[k1 : k1 + 192, :] = rows[:, 128:]
+        base = 768 * kh
+        z = jnp.concatenate(
+            [z_v[base + 192 * k : base + 192 * k + 192, :] for k in range(4)], axis=1
+        )
+        spec = dot(sq_v[1], z.astype(BF16))
+        modes = jnp.concatenate(
+            [
+                jnp.concatenate(
+                    [spec[:H, 128 * k : 128 * k + 128], spec[H:, 128 * k : 128 * k + 128]], axis=1
+                )
+                for k in range(4)
+            ],
+            axis=0,
+        )
+        mid = jnp.maximum(dot(modes.astype(BF16), w1_v[...]) + bias, 0.0)
+        res = dot(mid.astype(BF16), w2_v[...])
+        res = res - jnp.clip(res, -0.01, 0.01)
+        back = jnp.concatenate(
+            [
+                jnp.concatenate(
+                    [res[H * k : H * k + H, :128], res[H * k : H * k + H, 128:]], axis=0
+                )
+                for k in range(4)
+            ],
+            axis=1,
+        )
+        rows = dot(sq_v[2], back.astype(BF16))
+        for k in range(4):
+            v_v[base + 192 * k : base + 192 * k + 192, :] = rows[:, 128 * k : 128 * k + 128]
 
         def send3(d, _):
             other, dev = mate_of(d)
@@ -427,13 +460,17 @@
 
     lax.fori_loop(1, 8, wait3, 0)
 
-    field = dot(bw_ref[...], p3_r[...].astype(F32).reshape(128, MSG).astype(BF16))
-    p4_s[...] = fold(field.reshape(NLON, 8, MSG)).astype(BF16)
-    steps = [(dx, dy, dz) for dx in range(2) for dy in range(4) for dz in range(4)]
-    steps.sort(key=lambda t: -(t[0] + min(t[1], 4 - t[1]) + min(t[2], 4 - t[2])))
-    for dx, dy, dz in steps[:-1]:
-        dest = ((q + dx) % 2) * 16 + ((row_y + dy) % 4) * 4 + (row_z + dz) % 4
-        remote(p4_s.at[dest], p4_r.at[b], s4.at[dest], r4.at[b], (a, dest)).start()
+    spectra = p3_r[...].astype(F32).reshape(128, MSG).astype(BF16)
+    for dx in (1, 0):
+        other = (q + dx) % 2
+        field = dot(bw_ref[pl.ds(pl.multiple_of(128 * other, 128), 128), :], spectra)
+        p4_s[pl.ds(16 * other, 16)] = fold(field.reshape(16, 8, MSG)).astype(BF16)
+        steps = [(dy, dz) for dy in range(4) for dz in range(4)]
+        steps.sort(key=lambda t: -(min(t[0], 4 - t[0]) + min(t[1], 4 - t[1])))
+        for dy, dz in steps:
+            if (dx, dy, dz) != (0, 0, 0):
+                dest = 16 * other + ((row_y + dy) % 4) * 4 + (row_z + dz) % 4
+                remote(p4_s.at[dest], p4_r.at[b], s4.at[dest], r4.at[b], (a, dest)).start()
     p4_r[b] = p4_s[b]
 
     def wait4(d, _):
@@ -541,11 +578,14 @@
             pltpu.VMEM((HID, C), BF16),
             pltpu.VMEM((4, 160, 768), BF16),
             pltpu.VMEM((8, 288, 160), F32),
-            pltpu.VMEM((2, 6, 2, 10, ROWS, 128), F32),
-            pltpu.VMEM((2, 384, 1280), BF16),
-            pltpu.VMEM((6, 512, 128), F32),
-            pltpu.VMEM((6, 512, 128), F32),
+            pltpu.VMEM((2, 6, 480, 128), F32),
+            pltpu.VMEM((2, 288, 1280), BF16),
+            pltpu.VMEM((2, 96, 1280), BF16),
+            pltpu.VMEM((2, 16, 1280), BF16),
+            pltpu.VMEM((6, 96, 128), F32),
             pltpu.VMEM((6, 384, 128), F32),
+            pltpu.VMEM((6, 384, 128), F32),
+            pltpu.VMEM((6, 288, 128), F32),
             pltpu.VMEM((288, C), F32),
             pltpu.VMEM((6, 2, 192, 128), F32),
             pltpu.VMEM((288, C), F32),

time: 60.4 us -> 58.6 us (0.970)
  Pallas kernels: 58.2 us -> 55.9 us
    pallas_call x1, Pallas kernels: 58.2 us -> 55.9 us  [local(): pl.pallas_call(kernel, out_shape=jax.ShapeDtypeStruct((2, COLS, ROWS, C),...]
where the time goes in v6:
time: 58.6 us; the launch traced here: 57.7 us
  Pallas kernels  55.9 us (95%)
  local copies, waits for them, and re-layouts  1.8 us (3%)
    pallas_call x1, Pallas kernels, local(): pl.pallas_call(kernel, out_shape=jax.ShapeDtypeStruct((2, COLS, ROWS, C),...  55.9 us
    unnamed x1, local copies, waits for them, and re-layouts  1.8 us

profile of v6, /device:TPU:0, one launch (start us, length us, event | category | flops | bytes accessed | tf_op | source)
XLA Modules:
  0.0 57.7 jit_solution(1107520505575787171)
XLA Ops:
  0.0 55.9 %shard_map.127 = bf16[2,6,24,768]{3,2,1,0:T(8,128)(2,1)} custom-call(bf16[2,20,48,192]{3,2,1,0:T(8,128)(2,1)} %bitcast.3, bf16[5120,768]{1,0:T(8,128)(2,1)} %pw_h.1, f32[2,8,96,96]{3,2,1,0:T(8,128)} %one_h.1, f32[2,8,96,96]{3,2,1,0:T(8,128)} %two_h.1, bf16[768,3072]{1,0:T(8,128)(2,1)} %up_h.1, bf16[3072,768]{1,0:T(8,128)(2,1)} %down_h.1, ...), custom_call_target="tpu_custom_call" | custom-call | tf_op jit(solution)/shard_map/pallas_call | solution.py:561
  55.9 1.8 %copy.15 = bf16[2,24,6,768]{3,1,2,0:T(8,128)(2,1)} copy(bf16[2,24,6,768]{3,1,2,0:T(8,128)(2,1)} %bitcast.2) | data formatting | bytes 884736

commit v7 on v6

--- a/solution.py
+++ b/solution.py
@@ -102,7 +102,7 @@
     t_v, m_v, lhs_v, side_v, rim_v, te_v, q0_v, q3_v, tot_v, acc_v, nf_v, tn_v, nrm_v,
     ew_s, ew_r, ns_s, ns_r,
     p1_s, p1_r, p2_s, p2_r, p3_s, p3_r, p4_s, p4_r,
-    z_v, v_v, w1_v, w2_v, h0_v, h1_v,
+    z_v, v_v, w1_v, w2_v, h0_v, h1_v, res_v,
     lsem, halo_ss, halo_rs, s1, r1, s2, r2, s3, r3, s4, r4,
 ):
     a = lax.axis_index("lat")
@@ -473,14 +473,19 @@
                 remote(p4_s.at[dest], p4_r.at[b], s4.at[dest], r4.at[b], (a, dest)).start()
     p4_r[b] = p4_s[b]
 
-    def wait4(d, _):
-        src = lax.rem(b + d, NLON)
-        remote(p4_s.at[src], p4_r.at[src], s4.at[src], r4.at[src], (a, src)).wait_recv()
-        return 0
-
-    lax.fori_loop(1, NLON, wait4, 0)
-
+    c_up.wait()
+    c_down.wait()
+    results = []
     for smp in range(2):
+        for part in range(2):
+            for blk in range(NB):
+                src = owner(part, smp, blk)
+
+                @pl.when(src != b)
+                def _(src=src):
+                    remote(
+                        p4_s.at[src], p4_r.at[src], s4.at[src], r4.at[src], (a, src)
+                    ).wait_recv()
 
         def join(part, _):
             msgs = [unfold(p4_r[owner(part, smp, blk)].astype(F32)) for blk in range(NB)]
@@ -499,29 +504,27 @@
         acc_v[rows, :] = middle
         nrm_v[rows, :] = norm(middle, g2_ref[...].reshape(1, C)).astype(BF16)
 
-    c_up.wait()
-    c_down.wait()
-
-    def up(step):
-        return dot(nrm_v[...], up_v[:, pl.ds(pl.multiple_of(step * 256, 256), 256)])
-
-    def down(hidden, step):
-        hidden = 0.5 * hidden * (1.0 + lax.erf(hidden * (1.0 / math.sqrt(2.0))))
-        rows = pl.ds(pl.multiple_of(step * 256, 256), 256)
-        return dot(hidden.astype(BF16), down_v[rows, :])
-
-    h0_v[...] = up(0)
-
-    def mlp(it, _):
-        step = 2 * it
-        h1_v[...] = up(step + 1)
-        acc_v[...] += down(h0_v[...], step)
-        h0_v[...] = up(jnp.minimum(step + 2, HID // 256 - 1))
-        acc_v[...] += down(h1_v[...], step + 1)
-        return 0
-
-    lax.fori_loop(0, HID // 512, mlp, 0)
-    out_ref[...] = acc_v[...].reshape(2, COLS, ROWS, C).astype(BF16)
+        def up(step):
+            return dot(nrm_v[rows, :], up_v[:, pl.ds(pl.multiple_of(step * 512, 512), 512)])
+
+        def down(hidden, step):
+            hidden = 0.5 * hidden * (1.0 + lax.erf(hidden * (1.0 / math.sqrt(2.0))))
+            part = pl.ds(pl.multiple_of(step * 512, 512), 512)
+            return dot(hidden.astype(BF16), down_v[part, :])
+
+        h0_v[...] = up(0)
+
+        def mlp(it, _):
+            step = 2 * it
+            h1_v[...] = up(step + 1)
+            acc_v[rows, :] += down(h0_v[...], step)
+            h0_v[...] = up(jnp.minimum(step + 2, HID // 512 - 1))
+            acc_v[rows, :] += down(h1_v[...], step + 1)
+            return 0
+
+        lax.fori_loop(0, HID // 1024, mlp, 0)
+        res_v[smp] = acc_v[rows, :].reshape(COLS, ROWS, C).astype(BF16)
+        results.append(load(16 + smp, res_v.at[smp], out_ref.at[smp]))
 
     for copy in halos:
         copy.wait_send()
@@ -546,6 +549,8 @@
         return 0
 
     lax.fori_loop(1, 8, drain_lat, 0)
+    for copy in results:
+        copy.wait()
 
 
 def local(
@@ -556,13 +561,12 @@
     fh, bh = lat_tables()
     const = lambda x: jnp.asarray(x, F32).astype(BF16)
     any_spec = pl.BlockSpec(memory_space=pl.ANY)
-    vmem = pl.BlockSpec(memory_space=pltpu.VMEM)
     dma = pltpu.SemaphoreType.DMA
     out = pl.pallas_call(
         kernel,
         out_shape=jax.ShapeDtypeStruct((2, COLS, ROWS, C), BF16),
         in_specs=[any_spec] * 13,
-        out_specs=vmem,
+        out_specs=any_spec,
         scratch_shapes=[
             pltpu.VMEM((3, 192, 192), BF16),
             pltpu.VMEM((128, 256), BF16),
@@ -606,9 +610,10 @@
             pltpu.VMEM((8 * 192, 128), F32),
             pltpu.VMEM((256, 256), BF16),
             pltpu.VMEM((256, 256), BF16),
-            pltpu.VMEM((288, 256), F32),
-            pltpu.VMEM((288, 256), F32),
-            dma((16,)),
+            pltpu.VMEM((144, 512), F32),
+            pltpu.VMEM((144, 512), F32),
+            pltpu.VMEM((2, COLS, ROWS, C), BF16),
+            dma((18,)),
             dma((4,)),
             dma((4,)),
             dma((NLON,)),

time: 58.6 us -> 56 us (0.956)
  Pallas kernels: 55.9 us -> 53.6 us
    pallas_call x1, Pallas kernels: 55.9 us -> 53.6 us  [local(): pl.pallas_call(kernel, out_shape=jax.ShapeDtypeStruct((2, COLS, ROWS, C),...]
where the time goes in v7:
time: 56 us; the launch traced here: 55.4 us
  Pallas kernels  53.6 us (96%)
  local copies, waits for them, and re-layouts  1.8 us (3%)
    pallas_call x1, Pallas kernels, local(): pl.pallas_call(kernel, out_shape=jax.ShapeDtypeStruct((2, COLS, ROWS, C),...  53.6 us
    unnamed x1, local copies, waits for them, and re-layouts  1.8 us

profile of v7, /device:TPU:0, one launch (start us, length us, event | category | flops | bytes accessed | tf_op | source)
XLA Modules:
  0.0 55.4 jit_solution(3644328312440043174)
XLA Ops:
  0.0 53.6 %shard_map.127 = bf16[2,6,24,768]{3,2,1,0:T(8,128)(2,1)} custom-call(bf16[2,20,48,192]{3,2,1,0:T(8,128)(2,1)} %bitcast.3, bf16[5120,768]{1,0:T(8,128)(2,1)} %pw_h.1, f32[2,8,96,96]{3,2,1,0:T(8,128)} %one_h.1, f32[2,8,96,96]{3,2,1,0:T(8,128)} %two_h.1, bf16[768,3072]{1,0:T(8,128)(2,1)} %up_h.1, bf16[3072,768]{1,0:T(8,128)(2,1)} %down_h.1, ...), custom_call_target="tpu_custom_call" | custom-call | tf_op jit(solution)/shard_map/pallas_call | solution.py:565
  53.6 1.8 %copy.15 = bf16[2,24,6,768]{3,1,2,0:T(8,128)(2,1)} copy(bf16[2,24,6,768]{3,1,2,0:T(8,128)(2,1)} %bitcast.2) | data formatting | bytes 884736

commit v8 on v7

--- a/solution.py
+++ b/solution.py
@@ -102,7 +102,7 @@
     t_v, m_v, lhs_v, side_v, rim_v, te_v, q0_v, q3_v, tot_v, acc_v, nf_v, tn_v, nrm_v,
     ew_s, ew_r, ns_s, ns_r,
     p1_s, p1_r, p2_s, p2_r, p3_s, p3_r, p4_s, p4_r,
-    z_v, v_v, w1_v, w2_v, h0_v, h1_v, res_v,
+    z_v, v_v, w1_v, w2_v, h0_v, h1_v, res_v, x_v,
     lsem, halo_ss, halo_rs, s1, r1, s2, r2, s3, r3, s4, r4,
 ):
     a = lax.axis_index("lat")
@@ -226,14 +226,17 @@
 
     halos = [
         remote(
-            src.at[i], dst.at[i], halo_ss.at[sem + i], halo_rs.at[sem + i],
+            src, dst, halo_ss.at[sem], halo_rs.at[sem],
             (lax.rem(a + da, NLAT), lax.rem(b + db, NLON)),
         )
-        for src, dst, sem, ways in (
-            (ns_s, ns_r, 0, ((1, 0), (NLAT - 1, 0))),
-            (ew_s, ew_r, 2, ((0, 1), (0, NLON - 1))),
-        )
-        for i, (da, db) in enumerate(ways)
+        for src, dst, sem, da, db in (
+            [(ns_s.at[i], ns_r.at[i], i, (1, NLAT - 1)[i], 0) for i in range(2)]
+            + [
+                (ew_s.at[i, smp], ew_r.at[i, smp], 2 + 2 * smp + i, 0, (1, NLON - 1)[i])
+                for smp in range(2)
+                for i in range(2)
+            ]
+        )
     ]
     halos[0].start()
     halos[1].start()
@@ -263,12 +266,13 @@
         for way in range(2):
             at = pl.ds((0, ROWS - 1)[way], 4, stride=ROWS)
             te_v[tile, at, :] += rim_rows(way, cols, ((0, 1), (7, 8), (8, 9), (15, 16)))
-        for smp in range(2):
-            for way in range(2):
-                first = ROWS * (2 * smp + 1 - way)
+    for smp in range(2):
+        for way in range(2):
+            first = ROWS * (2 * smp + 1 - way)
+            for tile in range(6):
+                cols = slice(128 * tile, 128 * tile + 128)
                 ew_s[way, smp, :, cols] = te_v[tile, first : first + ROWS, :].astype(BF16)
-    halos[2].start()
-    halos[3].start()
+            halos[2 + 2 * smp + way].start()
 
     for pair in range(3):
         for off, half, out_v, lead in ((0, 1, q0_v, 1), (3, 0, q3_v, 7)):
@@ -293,14 +297,6 @@
         for way in range(2):
             at = pl.ds((0, ROWS - 1)[way], 12, stride=ROWS)
             tot_v[tile, at, :] += rim_rows(way, cols, ((1, 7), (9, 15)))
-    halos[2].wait_recv()
-    halos[3].wait_recv()
-    for tile in range(6):
-        cols = slice(128 * tile, 128 * tile + 128)
-        for smp in range(2):
-            for way, j in ((0, 0), (1, COLS - 1)):
-                first = ROWS * (COLS * smp + j)
-                tot_v[tile, first : first + ROWS, :] += ew_r[way, smp, :, cols].astype(F32)
     for copy in small:
         copy.wait()
 
@@ -309,6 +305,12 @@
 
     for smp in range(2):
         rows = slice(144 * smp, 144 * smp + 144)
+        for way, j in ((0, 0), (1, COLS - 1)):
+            halos[2 + 2 * smp + way].wait_recv()
+            first = ROWS * (COLS * smp + j)
+            for tile in range(6):
+                cols = slice(128 * tile, 128 * tile + 128)
+                tot_v[tile, first : first + ROWS, :] += ew_r[way, smp, :, cols].astype(F32)
         tok = jnp.concatenate([tot_v[t, rows, :] for t in range(6)], axis=1)
         tok = tok.astype(BF16).astype(F32)
         normed = norm(tok, g1_ref[...].reshape(1, C)).astype(BF16).astype(F32)
@@ -363,18 +365,24 @@
             parts.append(jnp.zeros((1, 32), F32))
         bias = bias + jnp.where(n == blk, jnp.concatenate(parts, axis=1), 0.0)
 
-    def wait1(d, _):
+    def take1(d, _):
         src = lax.rem(b + d, NLON)
-        remote(p1_s.at[src], p1_r.at[src], s1.at[src], r1.at[src], (a, src)).wait_recv()
+
+        @pl.when(d > 0)
+        def _():
+            remote(p1_s.at[src], p1_r.at[src], s1.at[src], r1.at[src], (a, src)).wait_recv()
+
+        at = pl.ds(pl.multiple_of(8 * src, 8), 8)
+        x_v[at, :] = unfold(p1_r[src].astype(F32))
         return 0
 
-    lax.fori_loop(1, NLON, wait1, 0)
+    lax.fori_loop(0, NLON, take1, 0)
 
     def mate_of(d):
         other = lax.rem(g + d, 8)
         return other, (other // 2, (other % 2) * 16 + p)
 
-    x = unfold(p1_r[...].astype(F32)).reshape(256, MSG).astype(BF16)
+    x = x_v[...].astype(BF16)
     for kh in range(2):
         part = dot(fw_ref[64 * kh : 64 * kh + 64, :], x)
         p2_s[kh] = part.reshape(8, 8, MSG).astype(BF16)
@@ -473,69 +481,15 @@
                 remote(p4_s.at[dest], p4_r.at[b], s4.at[dest], r4.at[b], (a, dest)).start()
     p4_r[b] = p4_s[b]
 
-    c_up.wait()
-    c_down.wait()
-    results = []
-    for smp in range(2):
-        for part in range(2):
-            for blk in range(NB):
-                src = owner(part, smp, blk)
-
-                @pl.when(src != b)
-                def _(src=src):
-                    remote(
-                        p4_s.at[src], p4_r.at[src], s4.at[src], r4.at[src], (a, src)
-                    ).wait_recv()
-
-        def join(part, _):
-            msgs = [unfold(p4_r[owner(part, smp, blk)].astype(F32)) for blk in range(NB)]
-            for i in range(ROW12):
-                plane = jnp.concatenate([m[:, BS * i : BS * i + BS] for m in msgs], axis=1)
-                for tile in range(6):
-                    nf_v[tile, smp, pl.ds(part * ROW12 + i, 8, stride=ROWS), :] = plane[
-                        :, 128 * tile : 128 * tile + 128
-                    ]
-            return 0
-
-        lax.fori_loop(0, 2, join, 0)
-        rows = slice(144 * smp, 144 * smp + 144)
-        field = jnp.concatenate([nf_v[tile, smp, :144] for tile in range(6)], axis=1)
-        middle = (field + tn_v[rows, :]).astype(BF16).astype(F32)
-        acc_v[rows, :] = middle
-        nrm_v[rows, :] = norm(middle, g2_ref[...].reshape(1, C)).astype(BF16)
-
-        def up(step):
-            return dot(nrm_v[rows, :], up_v[:, pl.ds(pl.multiple_of(step * 512, 512), 512)])
-
-        def down(hidden, step):
-            hidden = 0.5 * hidden * (1.0 + lax.erf(hidden * (1.0 / math.sqrt(2.0))))
-            part = pl.ds(pl.multiple_of(step * 512, 512), 512)
-            return dot(hidden.astype(BF16), down_v[part, :])
-
-        h0_v[...] = up(0)
-
-        def mlp(it, _):
-            step = 2 * it
-            h1_v[...] = up(step + 1)
-            acc_v[rows, :] += down(h0_v[...], step)
-            h0_v[...] = up(jnp.minimum(step + 2, HID // 512 - 1))
-            acc_v[rows, :] += down(h1_v[...], step + 1)
-            return 0
-
-        lax.fori_loop(0, HID // 1024, mlp, 0)
-        res_v[smp] = acc_v[rows, :].reshape(COLS, ROWS, C).astype(BF16)
-        results.append(load(16 + smp, res_v.at[smp], out_ref.at[smp]))
-
     for copy in halos:
         copy.wait_send()
 
-    def drain_lon(d, _):
+    def drain1(d, _):
         dest = lax.rem(b + d, NLON)
         remote(p1_s.at[dest], p1_r.at[b], s1.at[dest], r1.at[b], (a, dest)).wait_send()
-        remote(p4_s.at[dest], p4_r.at[b], s4.at[dest], r4.at[b], (a, dest)).wait_send()
         return 0
 
-    lax.fori_loop(1, NLON, drain_lon, 0)
+    lax.fori_loop(1, NLON, drain1, 0)
 
     def drain_lat(d, _):
         other, dev = mate_of(d)
@@ -549,6 +503,64 @@
         return 0
 
     lax.fori_loop(1, 8, drain_lat, 0)
+    c_up.wait()
+    c_down.wait()
+    results = []
+    for smp in range(2):
+        def join(part, _):
+            for blk in range(NB):
+                src = owner(part, smp, blk)
+
+                @pl.when(src != b)
+                def _(src=src):
+                    remote(
+                        p4_s.at[src], p4_r.at[src], s4.at[src], r4.at[src], (a, src)
+                    ).wait_recv()
+
+            msgs = [unfold(p4_r[owner(part, smp, blk)].astype(F32)) for blk in range(NB)]
+            for i in range(ROW12):
+                plane = jnp.concatenate([m[:, BS * i : BS * i + BS] for m in msgs], axis=1)
+                for tile in range(6):
+                    nf_v[tile, smp, pl.ds(part * ROW12 + i, 8, stride=ROWS), :] = plane[
+                        :, 128 * tile : 128 * tile + 128
+                    ]
+            return 0
+
+        lax.fori_loop(0, 2, join, 0)
+        rows = slice(144 * smp, 144 * smp + 144)
+        field = jnp.concatenate([nf_v[tile, smp, :144] for tile in range(6)], axis=1)
+        middle = (field + tn_v[rows, :]).astype(BF16).astype(F32)
+        acc_v[rows, :] = middle
+        nrm_v[rows, :] = norm(middle, g2_ref[...].reshape(1, C)).astype(BF16)
+
+        def up(step):
+            return dot(nrm_v[rows, :], up_v[:, pl.ds(pl.multiple_of(step * 512, 512), 512)])
+
+        def down(hidden, step):
+            hidden = 0.5 * hidden * (1.0 + lax.erf(hidden * (1.0 / math.sqrt(2.0))))
+            part = pl.ds(pl.multiple_of(step * 512, 512), 512)
+            return dot(hidden.astype(BF16), down_v[part, :])
+
+        h0_v[...] = up(0)
+
+        def mlp(it, _):
+            step = 2 * it
+            h1_v[...] = up(step + 1)
+            acc_v[rows, :] += down(h0_v[...], step)
+            h0_v[...] = up(jnp.minimum(step + 2, HID // 512 - 1))
+            acc_v[rows, :] += down(h1_v[...], step + 1)
+            return 0
+
+        lax.fori_loop(0, HID // 1024, mlp, 0)
+        res_v[smp] = acc_v[rows, :].reshape(COLS, ROWS, C).astype(BF16)
+        results.append(load(16 + smp, res_v.at[smp], out_ref.at[smp]))
+
+    def drain4(d, _):
+        dest = lax.rem(b + d, NLON)
+        remote(p4_s.at[dest], p4_r.at[b], s4.at[dest], r4.at[b], (a, dest)).wait_send()
+        return 0
+
+    lax.fori_loop(1, NLON, drain4, 0)
     for copy in results:
         copy.wait()
 
@@ -613,9 +625,10 @@
             pltpu.VMEM((144, 512), F32),
             pltpu.VMEM((144, 512), F32),
             pltpu.VMEM((2, COLS, ROWS, C), BF16),
+            pltpu.VMEM((256, MSG), F32),
             dma((18,)),
-            dma((4,)),
-            dma((4,)),
+            dma((6,)),
+            dma((6,)),
             dma((NLON,)),
             dma((NLON,)),
             dma((2, 8)),

time: 56 us -> 55.4 us (0.989)
  Pallas kernels: 53.6 us -> 53 us
    pallas_call x1, Pallas kernels: 53.6 us -> 53 us  [local(): pl.pallas_call(kernel, out_shape=jax.ShapeDtypeStruct((2, COLS, ROWS, C),...]
where the time goes in v8:
time: 55.4 us; the launch traced here: 54.8 us
  Pallas kernels  53 us (96%)
  local copies, waits for them, and re-layouts  1.8 us (3%)
    pallas_call x1, Pallas kernels, local(): pl.pallas_call(kernel, out_shape=jax.ShapeDtypeStruct((2, COLS, ROWS, C),...  53 us
    unnamed x1, local copies, waits for them, and re-layouts  1.8 us

profile of v8, /device:TPU:0, one launch (start us, length us, event | category | flops | bytes accessed | tf_op | source)
XLA Modules:
  0.0 54.8 jit_solution(5206690523646582905)
XLA Ops:
  0.0 53.0 %shard_map.127 = bf16[2,6,24,768]{3,2,1,0:T(8,128)(2,1)} custom-call(bf16[2,20,48,192]{3,2,1,0:T(8,128)(2,1)} %bitcast.3, bf16[5120,768]{1,0:T(8,128)(2,1)} %pw_h.1, f32[2,8,96,96]{3,2,1,0:T(8,128)} %one_h.1, f32[2,8,96,96]{3,2,1,0:T(8,128)} %two_h.1, bf16[768,3072]{1,0:T(8,128)(2,1)} %up_h.1, bf16[3072,768]{1,0:T(8,128)(2,1)} %down_h.1, ...), custom_call_target="tpu_custom_call" | custom-call | tf_op jit(solution)/shard_map/pallas_call | solution.py:577
  53.0 1.8 %copy.15 = bf16[2,24,6,768]{3,1,2,0:T(8,128)(2,1)} copy(bf16[2,24,6,768]{3,1,2,0:T(8,128)(2,1)} %bitcast.2) | data formatting | bytes 884736

commit v9 on v8

--- a/solution.py
+++ b/solution.py
@@ -99,7 +99,7 @@
     out_ref,
     sq_v, fw_ref, bw_ref, g1_ref, bias_ref, g2_ref,
     grid_v, pw_v, one_v, two_v, up_v, down_v, tab_v,
-    t_v, m_v, lhs_v, side_v, rim_v, te_v, q0_v, q3_v, tot_v, acc_v, nf_v, tn_v, nrm_v,
+    t_v, m_v, lhs_v, side_v, rim_v, q0_v, q3_v, tot_v, acc_v, nf_v, tn_v, nrm_v,
     ew_s, ew_r, ns_s, ns_r,
     p1_s, p1_r, p2_s, p2_r, p3_s, p3_r, p4_s, p4_r,
     z_v, v_v, w1_v, w2_v, h0_v, h1_v, res_v, x_v,
@@ -133,6 +133,10 @@
         return 0
 
     lax.fori_loop(0, 6, greet_lat, 0)
+    for da in (1, NLAT - 1):
+        for db in (1, NLON - 1):
+            corner = (lax.rem(a + da, NLAT), lax.rem(b + db, NLON))
+            pl.semaphore_signal(barrier, inc=1, device_id=corner, device_id_type=MESH)
     def load(index, src, dst):
         copy = pltpu.make_async_copy(src, dst, lsem.at[index])
         copy.start()
@@ -203,8 +207,10 @@
                     row = row + m_v[half, 0, pl.ds(rim + ROWS, 8, stride=ROWS), :]
                 outer.append(row)
                 lhs_v[half, 144 * smp : 144 * smp + 144, cols] = value[ROWS:168].astype(BF16)
-                side = jnp.concatenate([value[:ROWS], value[168:]], axis=0)
-                side_v[half, 48 * smp : 48 * smp + 48, cols] = side.astype(BF16)
+                if tile < 3 or tile >= 7:
+                    side = jnp.concatenate([value[:ROWS], value[168:]], axis=0)
+                    at = 128 * (tile if tile < 3 else tile - 4)
+                    side_v[half, 48 * smp : 48 * smp + 48, at : at + 128] = side.astype(BF16)
             rim_v[half, :, cols] = jnp.concatenate(outer, axis=0).astype(BF16)
 
     def weight(off, pair):
@@ -216,7 +222,7 @@
             value = dot(rim_v[half], weight(off, pair))
             ns_s[way, :, 256 * pair : 256 * pair + 256] = value.astype(BF16)
 
-    pl.semaphore_wait(barrier, NLON - 1 + 6)
+    pl.semaphore_wait(barrier, NLON - 1 + 6 + 4)
 
     def remote(src, dst, ssem, rsem, dev):
         return pltpu.make_async_remote_copy(
@@ -230,49 +236,54 @@
             (lax.rem(a + da, NLAT), lax.rem(b + db, NLON)),
         )
         for src, dst, sem, da, db in (
-            [(ns_s.at[i], ns_r.at[i], i, (1, NLAT - 1)[i], 0) for i in range(2)]
+            [
+                (ns_s.at[i], ns_r.at[3 * i + side], 3 * i + side, (1, NLAT - 1)[i], db)
+                for i in range(2)
+                for side, db in enumerate((0, 1, NLON - 1))
+            ]
             + [
-                (ew_s.at[i, smp], ew_r.at[i, smp], 2 + 2 * smp + i, 0, (1, NLON - 1)[i])
+                (ew_s.at[i, smp], ew_r.at[i, smp], 6 + 2 * smp + i, 0, (1, NLON - 1)[i])
                 for smp in range(2)
                 for i in range(2)
             ]
         )
     ]
-    halos[0].start()
-    halos[1].start()
+    for copy in halos[:6]:
+        copy.start()
 
     c_pw[1].wait()
     c_pw[2].wait()
     none = jnp.zeros((4, 1, 256), F32)
+
+    def outer_weight(off, pair):
+        cols = slice(256 * pair, 256 * pair + 256)
+        first = 1280 * off
+        return jnp.concatenate(
+            [pw_v[first : first + 384, cols], pw_v[first + 896 : first + 1280, cols]], axis=0
+        )
+
     for pair in range(3):
-        value = dot(side_v[0], weight(1, pair)) + dot(side_v[1], weight(2, pair))
-        above = dot(side_v[1], weight(0, pair)).reshape(4, ROWS, 256)
-        below = dot(side_v[0], weight(3, pair)).reshape(4, ROWS, 256)
+        value = dot(side_v[0], outer_weight(1, pair)) + dot(side_v[1], outer_weight(2, pair))
+        above = dot(side_v[1], outer_weight(0, pair)).reshape(4, ROWS, 256)
+        below = dot(side_v[0], outer_weight(3, pair)).reshape(4, ROWS, 256)
         above = jnp.concatenate([none, above[:, :-1]], axis=1)
         below = jnp.concatenate([below[:, 1:], none], axis=1)
-        value = value + (above + below).reshape(96, 256)
-        te_v[2 * pair] = value[:, :128]
-        te_v[2 * pair + 1] = value[:, 128:]
-
-    def rim_rows(way, cols, picks):
-        rows = ns_r[way, :, cols].astype(F32)
-        rows = jnp.concatenate([rows[lo:hi] for lo, hi in picks], axis=0)
-        return jnp.where((a > 0, a < NLAT - 1)[way], rows, 0.0)
-
-    halos[0].wait_recv()
-    halos[1].wait_recv()
-    for tile in range(6):
-        cols = slice(128 * tile, 128 * tile + 128)
-        for way in range(2):
-            at = pl.ds((0, ROWS - 1)[way], 4, stride=ROWS)
-            te_v[tile, at, :] += rim_rows(way, cols, ((0, 1), (7, 8), (8, 9), (15, 16)))
-    for smp in range(2):
-        for way in range(2):
-            first = ROWS * (2 * smp + 1 - way)
-            for tile in range(6):
-                cols = slice(128 * tile, 128 * tile + 128)
-                ew_s[way, smp, :, cols] = te_v[tile, first : first + ROWS, :].astype(BF16)
-            halos[2 + 2 * smp + way].start()
+        value = (value + (above + below).reshape(96, 256)).astype(BF16)
+        for smp in range(2):
+            for way in range(2):
+                first = ROWS * (2 * smp + 1 - way)
+                ew_s[way, smp, :, 256 * pair : 256 * pair + 256] = value[first : first + ROWS]
+    for copy in halos[6:]:
+        copy.start()
+
+    def rim_rows(way, cols):
+        straight, west, east = [ns_r[3 * way + side, :, cols].astype(F32) for side in range(3)]
+        none = jnp.zeros((4, 128), F32)
+        value = jnp.concatenate([straight[1:7], straight[9:15]], axis=0)
+        value = value + jnp.concatenate(
+            [west[7:8], none, east[0:1], west[15:16], none, east[8:9]], axis=0
+        )
+        return jnp.where((a > 0, a < NLAT - 1)[way], value, 0.0)
 
     for pair in range(3):
         for off, half, out_v, lead in ((0, 1, q0_v, 1), (3, 0, q3_v, 7)):
@@ -292,11 +303,13 @@
             tot_v[tile] = value[:, 128 * lane : 128 * lane + 128] + shifted.reshape(288, 128)
     c_up = load(8, up_h, up_v)
     c_down = load(9, down_h, down_v)
+    for copy in halos[:6]:
+        copy.wait_recv()
     for tile in range(6):
         cols = slice(128 * tile, 128 * tile + 128)
         for way in range(2):
             at = pl.ds((0, ROWS - 1)[way], 12, stride=ROWS)
-            tot_v[tile, at, :] += rim_rows(way, cols, ((1, 7), (9, 15)))
+            tot_v[tile, at, :] += rim_rows(way, cols)
     for copy in small:
         copy.wait()
 
@@ -306,7 +319,7 @@
     for smp in range(2):
         rows = slice(144 * smp, 144 * smp + 144)
         for way, j in ((0, 0), (1, COLS - 1)):
-            halos[2 + 2 * smp + way].wait_recv()
+            halos[6 + 2 * smp + way].wait_recv()
             first = ROWS * (COLS * smp + j)
             for tile in range(6):
                 cols = slice(128 * tile, 128 * tile + 128)
@@ -596,9 +609,8 @@
             pltpu.VMEM((8, 288, 160), F32),
             pltpu.VMEM((2, 6, 480, 128), F32),
             pltpu.VMEM((2, 288, 1280), BF16),
-            pltpu.VMEM((2, 96, 1280), BF16),
+            pltpu.VMEM((2, 96, 768), BF16),
             pltpu.VMEM((2, 16, 1280), BF16),
-            pltpu.VMEM((6, 96, 128), F32),
             pltpu.VMEM((6, 384, 128), F32),
             pltpu.VMEM((6, 384, 128), F32),
             pltpu.VMEM((6, 288, 128), F32),
@@ -609,7 +621,7 @@
             pltpu.VMEM((2, 2, ROWS, C), BF16),
             pltpu.VMEM((2, 2, ROWS, C), BF16),
             pltpu.VMEM((2, 16, C), BF16),
-            pltpu.VMEM((2, 16, C), BF16),
+            pltpu.VMEM((6, 16, C), BF16),
             pltpu.VMEM((NLON, 8, 896), BF16),
             pltpu.VMEM((NLON, 8, 896), BF16),
             pltpu.VMEM((2, 8, 8, MSG), BF16),
@@ -627,8 +639,8 @@
             pltpu.VMEM((2, COLS, ROWS, C), BF16),
             pltpu.VMEM((256, MSG), F32),
             dma((18,)),
-            dma((6,)),
-            dma((6,)),
+            dma((10,)),
+            dma((10,)),
             dma((NLON,)),
             dma((NLON,)),
             dma((2, 8)),

time: 55.4 us -> 55.3 us (level)
  no operation moved by 1% of the time
where the time goes in v9:
time: 55.3 us; the launch traced here: 54.7 us
  Pallas kernels  52.9 us (96%)
  local copies, waits for them, and re-layouts  1.8 us (3%)
    pallas_call x1, Pallas kernels, local(): pl.pallas_call(kernel, out_shape=jax.ShapeDtypeStruct((2, COLS, ROWS, C),...  52.9 us
    unnamed x1, local copies, waits for them, and re-layouts  1.8 us

profile of v9, /device:TPU:0, one launch (start us, length us, event | category | flops | bytes accessed | tf_op | source)
XLA Modules:
  0.0 54.7 jit_solution(8044197035126345623)
XLA Ops:
  0.0 52.9 %shard_map.127 = bf16[2,6,24,768]{3,2,1,0:T(8,128)(2,1)} custom-call(bf16[2,20,48,192]{3,2,1,0:T(8,128)(2,1)} %bitcast.3, bf16[5120,768]{1,0:T(8,128)(2,1)} %pw_h.1, f32[2,8,96,96]{3,2,1,0:T(8,128)} %one_h.1, f32[2,8,96,96]{3,2,1,0:T(8,128)} %two_h.1, bf16[768,3072]{1,0:T(8,128)(2,1)} %up_h.1, bf16[3072,768]{1,0:T(8,128)(2,1)} %down_h.1, ...), custom_call_target="tpu_custom_call" | custom-call | tf_op jit(solution)/shard_map/pallas_call | solution.py:590
  52.9 1.8 %copy.15 = bf16[2,24,6,768]{3,1,2,0:T(8,128)(2,1)} copy(bf16[2,24,6,768]{3,1,2,0:T(8,128)(2,1)} %bitcast.2) | data formatting | bytes 884736

commit v10 on v9

--- a/solution.py
+++ b/solution.py
@@ -276,40 +276,16 @@
     for copy in halos[6:]:
         copy.start()
 
-    def rim_rows(way, cols):
-        straight, west, east = [ns_r[3 * way + side, :, cols].astype(F32) for side in range(3)]
+    def rim_rows(way, smp, cols):
+        straight, west, east = [
+            ns_r[3 * way + side, :, cols].astype(F32)[8 * smp : 8 * smp + 8] for side in range(3)
+        ]
         none = jnp.zeros((4, 128), F32)
-        value = jnp.concatenate([straight[1:7], straight[9:15]], axis=0)
-        value = value + jnp.concatenate(
-            [west[7:8], none, east[0:1], west[15:16], none, east[8:9]], axis=0
-        )
+        value = straight[1:7] + jnp.concatenate([west[7:8], none, east[0:1]], axis=0)
         return jnp.where((a > 0, a < NLAT - 1)[way], value, 0.0)
 
-    for pair in range(3):
-        for off, half, out_v, lead in ((0, 1, q0_v, 1), (3, 0, q3_v, 7)):
-            value = dot(lhs_v[half], weight(off, pair))
-            for lane in range(2):
-                lanes = slice(128 * lane, 128 * lane + 128)
-                for m in range(12):
-                    out_v[2 * pair + lane, 32 * m + lead : 32 * m + lead + ROWS, :] = value[
-                        ROWS * m : ROWS * m + ROWS, lanes
-                    ]
-        value = dot(lhs_v[0], weight(1, pair)) + dot(lhs_v[1], weight(2, pair))
-        for lane in range(2):
-            tile = 2 * pair + lane
-            shifted = (
-                q0_v[tile].reshape(12, 32, 128)[:, :ROWS] + q3_v[tile].reshape(12, 32, 128)[:, 8:]
-            )
-            tot_v[tile] = value[:, 128 * lane : 128 * lane + 128] + shifted.reshape(288, 128)
     c_up = load(8, up_h, up_v)
     c_down = load(9, down_h, down_v)
-    for copy in halos[:6]:
-        copy.wait_recv()
-    for tile in range(6):
-        cols = slice(128 * tile, 128 * tile + 128)
-        for way in range(2):
-            at = pl.ds((0, ROWS - 1)[way], 12, stride=ROWS)
-            tot_v[tile, at, :] += rim_rows(way, cols)
     for copy in small:
         copy.wait()
 
@@ -318,6 +294,35 @@
 
     for smp in range(2):
         rows = slice(144 * smp, 144 * smp + 144)
+        for pair in range(3):
+            for off, half, out_v, lead in ((0, 1, q0_v, 1), (3, 0, q3_v, 7)):
+                value = dot(lhs_v[half, rows], weight(off, pair))
+                for lane in range(2):
+                    lanes = slice(128 * lane, 128 * lane + 128)
+                    for m in range(COLS):
+                        first = 32 * (COLS * smp + m) + lead
+                        out_v[2 * pair + lane, first : first + ROWS, :] = value[
+                            ROWS * m : ROWS * m + ROWS, lanes
+                        ]
+            value = dot(lhs_v[0, rows], weight(1, pair)) + dot(lhs_v[1, rows], weight(2, pair))
+            for lane in range(2):
+                tile = 2 * pair + lane
+                groups = slice(192 * smp, 192 * smp + 192)
+                shifted = (
+                    q0_v[tile, groups].reshape(COLS, 32, 128)[:, :ROWS]
+                    + q3_v[tile, groups].reshape(COLS, 32, 128)[:, 8:]
+                )
+                tot_v[tile, rows] = (
+                    value[:, 128 * lane : 128 * lane + 128] + shifted.reshape(144, 128)
+                )
+        if smp == 0:
+            for copy in halos[:6]:
+                copy.wait_recv()
+        for tile in range(6):
+            cols = slice(128 * tile, 128 * tile + 128)
+            for way in range(2):
+                at = pl.ds(144 * smp + (0, ROWS - 1)[way], COLS, stride=ROWS)
+                tot_v[tile, at, :] += rim_rows(way, smp, cols)
         for way, j in ((0, 0), (1, COLS - 1)):
             halos[6 + 2 * smp + way].wait_recv()
             first = ROWS * (COLS * smp + j)
@@ -395,12 +400,20 @@
         other = lax.rem(g + d, 8)
         return other, (other // 2, (other % 2) * 16 + p)
 
+    mates = [(dh, dc, dl) for dh in range(2) for dc in range(2) for dl in range(2)][1:]
+    mates.sort(key=lambda t: (not (t[0] and not t[2]), not t[2]))
+
+    def mate_at(dh, dc, dl):
+        lat = ((a // 2 + dh) % 2) * 2 + (a % 2 + dc) % 2
+        half = (q + dl) % 2
+        return 2 * lat + half, (lat, half * 16 + p)
+
     x = x_v[...].astype(BF16)
     for kh in range(2):
         part = dot(fw_ref[64 * kh : 64 * kh + 64, :], x)
         p2_s[kh] = part.reshape(8, 8, MSG).astype(BF16)
-        for d in range(1, 8):
-            other, dev = mate_of(d)
+        for way in mates:
+            other, dev = mate_at(*way)
             remote(
                 p2_s.at[kh, other], p2_r.at[kh, g], s2.at[kh, other], r2.at[kh, g], dev
             ).start()
@@ -460,15 +473,12 @@
         for k in range(4):
             v_v[base + 192 * k : base + 192 * k + 192, :] = rows[:, 128 * k : 128 * k + 128]
 
-        def send3(d, _):
-            other, dev = mate_of(d)
+        for way in mates:
+            other, dev = mate_at(*way)
             p3_s[kh, other] = gather(kh, other)
             remote(
                 p3_s.at[kh, other], p3_r.at[kh, g], s3.at[kh, other], r3.at[kh, g], dev
             ).start()
-            return 0
-
-        lax.fori_loop(1, 8, send3, 0)
         p3_r[kh, g] = gather(kh, g)
 
     def wait3(d, _):

time: 55.3 us -> 54.8 us (level)
  no operation moved by 1% of the time
where the time goes in v10:
time: 54.8 us; the launch traced here: 54.2 us
  Pallas kernels  52.4 us (96%)
  local copies, waits for them, and re-layouts  1.8 us (3%)
    pallas_call x1, Pallas kernels, local(): pl.pallas_call(kernel, out_shape=jax.ShapeDtypeStruct((2, COLS, ROWS, C),...  52.4 us
    unnamed x1, local copies, waits for them, and re-layouts  1.8 us

profile of v10, /device:TPU:0, one launch (start us, length us, event | category | flops | bytes accessed | tf_op | source)
XLA Modules:
  0.0 54.2 jit_solution(11138554276081750363)
XLA Ops:
  0.0 52.4 %shard_map.127 = bf16[2,6,24,768]{3,2,1,0:T(8,128)(2,1)} custom-call(bf16[2,20,48,192]{3,2,1,0:T(8,128)(2,1)} %bitcast.3, bf16[5120,768]{1,0:T(8,128)(2,1)} %pw_h.1, f32[2,8,96,96]{3,2,1,0:T(8,128)} %one_h.1, f32[2,8,96,96]{3,2,1,0:T(8,128)} %two_h.1, bf16[768,3072]{1,0:T(8,128)(2,1)} %up_h.1, bf16[3072,768]{1,0:T(8,128)(2,1)} %down_h.1, ...), custom_call_target="tpu_custom_call" | custom-call | tf_op jit(solution)/shard_map/pallas_call | solution.py:600
  52.4 1.8 %copy.15 = bf16[2,24,6,768]{3,1,2,0:T(8,128)(2,1)} copy(bf16[2,24,6,768]{3,1,2,0:T(8,128)(2,1)} %bitcast.2) | data formatting | bytes 884736

commit v11 on v10

--- a/solution.py
+++ b/solution.py
@@ -574,7 +574,7 @@
             acc_v[rows, :] += down(h1_v[...], step + 1)
             return 0
 
-        lax.fori_loop(0, HID // 1024, mlp, 0)
+        lax.fori_loop(0, HID // 1024, mlp, 0, unroll=True)
         res_v[smp] = acc_v[rows, :].reshape(COLS, ROWS, C).astype(BF16)
         results.append(load(16 + smp, res_v.at[smp], out_ref.at[smp]))
 

time: 54.8 us -> 53.4 us (0.974)
  Pallas kernels: 52.4 us -> 51.1 us
    pallas_call x1, Pallas kernels: 52.4 us -> 51.1 us  [local(): pl.pallas_call(kernel, out_shape=jax.ShapeDtypeStruct((2, COLS, ROWS, C),...]
where the time goes in v11:
time: 53.4 us; the launch traced here: 52.9 us
  Pallas kernels  51.1 us (96%)
  local copies, waits for them, and re-layouts  1.8 us (3%)
    pallas_call x1, Pallas kernels, local(): pl.pallas_call(kernel, out_shape=jax.ShapeDtypeStruct((2, COLS, ROWS, C),...  51.1 us
    unnamed x1, local copies, waits for them, and re-layouts  1.8 us

profile of v11, /device:TPU:0, one launch (start us, length us, event | category | flops | bytes accessed | tf_op | source)
XLA Modules:
  0.0 52.9 jit_solution(10104863894932819295)
XLA Ops:
  0.0 51.1 %shard_map.127 = bf16[2,6,24,768]{3,2,1,0:T(8,128)(2,1)} custom-call(bf16[2,20,48,192]{3,2,1,0:T(8,128)(2,1)} %bitcast.3, bf16[5120,768]{1,0:T(8,128)(2,1)} %pw_h.1, f32[2,8,96,96]{3,2,1,0:T(8,128)} %one_h.1, f32[2,8,96,96]{3,2,1,0:T(8,128)} %two_h.1, bf16[768,3072]{1,0:T(8,128)(2,1)} %up_h.1, bf16[3072,768]{1,0:T(8,128)(2,1)} %down_h.1, ...), custom_call_target="tpu_custom_call" | custom-call | tf_op jit(solution)/shard_map/pallas_call | solution.py:600
  51.1 1.8 %copy.15 = bf16[2,24,6,768]{3,1,2,0:T(8,128)(2,1)} copy(bf16[2,24,6,768]{3,1,2,0:T(8,128)(2,1)} %bitcast.2) | data formatting | bytes 884736
